TPU v7x, 512 devices: a whole 4x4x16 slice. The times are simulated.
512 devices in a mesh: ctx: 16 (over y_hi, x, core), fsdp: 32 (over z, y_lo).
Axes of the slice: x: 4, y: 4 (y_hi: 2, y_lo: 2; y = y_hi * 2 + y_lo), z: 16, core: 2. Of those that a mesh axis runs over, the one named last changes fastest.
Arguments:
- tokens: bfloat16 [32, 4096, 2048], P('fsdp', 'ctx'), may hold values from -32 to 32
- query_weight: bfloat16 [2048, 512], P('fsdp'), may hold values from -0.125 to 0.125
- key_weight: bfloat16 [2048, 512], P('fsdp'), may hold values from -0.125 to 0.125
- value_weight: bfloat16 [2048, 512], P('fsdp'), may hold values from -0.125 to 0.125
- cotangent: bfloat16 [32, 4096, 512], P('fsdp', 'ctx'), may hold values from -0.29882812 to 0.29882812
- rand_owner: int32 [32, 64, 3], P('fsdp'), may hold values from 0 to 15, all different within a row; in each aligned block of 4 rows (0 to 3, 4 to 7, ..., all dimensions but the last counted through in order) at most 2 rows name the same one
- rand_offset: int32 [32, 64, 3], P('fsdp'), may hold values from 0 to 3
- global_ids: int32 [32, 2], P('fsdp'), may hold values from 0 to 63
Outputs:
- attn_out: bfloat16 [32, 4096, 512], P('fsdp', 'ctx')
- query_grad: float32 [2048, 512], P('fsdp')
Inputs may be any that keep to these rules, and one draw needn't show every extreme that they name: `rand_owner`: the 3 owners named for one query block differ. The query blocks of one context shard (aligned runs of 4 blocks) take at most 2 random blocks from one owner, and exactly 2 from some owner.
All inputs are finite; a program needn't handle non-finite values.
Results may differ from a plain program's by a relative error of at most 0.015.
The roundings to bfloat16 on the way count: a program that leaves them out, or rounds other values in their place, can miss the bound.
Values may be sent and summed in bfloat16 or wider, within the bound.
No kernel may reach another device: no remote copies, remote signals or barrier semaphores. Data moves between devices by JAX's collectives and lax.ppermute only.
A program may use at most 64 MiB of HBM per device.

v0:
```python
import jax
import jax.numpy as jnp
from jax import lax
from jax.sharding import PartitionSpec as P

HD = 128
BLK = 64
RND = 3
GLB = 2


masked_score = -1e30


def padded(cells, sides, width):
    for axis, dim in sides:
        count = lax.axis_size(axis)
        ends = count - 1
        head = lax.slice_in_dim(cells, 0, width, axis=dim)
        tail = lax.slice_in_dim(cells, cells.shape[dim] - width, cells.shape[dim], axis=dim)
        cells = jnp.concatenate(
            [
                lax.ppermute(tail, axis, [(i, (i + 1) % count) for i in range(ends)]),
                cells,
                lax.ppermute(head, axis, [((i + 1) % count, i) for i in range(ends)]),
            ],
            axis=dim,
        )
    return cells


def add_piece(source, shard_rows):
    return jnp.dot(source, shard_rows, preferred_element_type=jnp.float32)


def send_blocks(pair_blocks, owners, offsets, own_index, ctx_count, capacity):
    pair_owner = owners.reshape(ctx_count, -1)
    pair_offset = offsets.reshape(ctx_count, -1)
    is_mine = (pair_owner == own_index).astype(jnp.int32)
    earlier_hits = jnp.cumsum(is_mine, axis=1) - 1
    slot_ids = jnp.arange(capacity, dtype=jnp.int32)
    picked = is_mine[:, None, :] * (earlier_hits[:, None, :] == slot_ids[None, :, None]).astype(
        jnp.int32
    )
    local_pick = jnp.sum(picked * pair_offset[:, None, :], axis=2)
    return pair_blocks[local_pick]


def take_blocks(received, mine_owners, capacity):
    pair_owner = mine_owners.reshape(-1)
    pair_total = pair_owner.shape[0]
    same_owner = pair_owner[:, None] == pair_owner[None, :]
    position = jnp.arange(pair_total, dtype=jnp.int32)
    before_mask = position[None, :] < position[:, None]
    slot_index = jnp.sum((same_owner & before_mask).astype(jnp.int32), axis=1)
    flat_index = pair_owner * capacity + slot_index
    ctx_count = received.shape[0]
    flat_blocks = received.reshape(ctx_count * capacity, received.shape[2], received.shape[3])
    return flat_blocks[flat_index]


def per_device(
    tokens, query_weight, key_weight, value_weight, cotangent, rand_owner, rand_offset, global_ids
):
    inputs = tokens[0]
    grad_out = cotangent[0]
    owners = rand_owner[0]
    offsets = rand_offset[0]
    global_list = global_ids[0]
    ctx_count = lax.axis_size("ctx")
    own_index = lax.axis_index("ctx")
    row_count = inputs.shape[0]
    block_count = row_count // BLK
    feature_width = key_weight.shape[1]
    head_count = feature_width // HD
    capacity = max(2, (block_count * RND + ctx_count - 1) // ctx_count)
    key_count = (3 + RND) * BLK
    score_scale = HD ** (-0.5)
    shard_rows = (
        lax.all_gather(query_weight, "fsdp", axis=0, tiled=True),
        lax.all_gather(key_weight, "fsdp", axis=0, tiled=True),
        lax.all_gather(value_weight, "fsdp", axis=0, tiled=True),
    )
    query_sum, key_sum, value_sum = tuple(
        (add_piece(inputs, part_rows) for part_rows in shard_rows)
    )
    queries = query_sum.astype(jnp.bfloat16)
    stacked = jnp.concatenate(
        [key_sum.astype(jnp.bfloat16), value_sum.astype(jnp.bfloat16)], axis=1
    )
    pair_blocks = stacked.reshape(block_count, BLK, 2 * feature_width)
    outgoing = send_blocks(pair_blocks, owners, offsets, own_index, ctx_count, capacity)
    received = lax.all_to_all(outgoing, "ctx", split_axis=0, concat_axis=0, tiled=True)
    extended = padded(stacked, (("ctx", 0),), BLK)
    block_owner = global_list // block_count
    block_place = global_list % block_count
    candidate = pair_blocks[block_place]
    owned_part = jnp.where(
        (block_owner == own_index)[:, None, None], candidate, jnp.zeros_like(candidate)
    ).astype(jnp.float32)
    global_pairs = lax.psum(owned_part.astype(jnp.bfloat16), "ctx")
    mine_owners = lax.dynamic_slice_in_dim(owners, own_index * block_count, block_count, 0)
    random_pairs = take_blocks(received, mine_owners, capacity).reshape(
        block_count, RND, BLK, 2 * feature_width
    )
    ext_blocks = extended.reshape(block_count + 2, BLK, 2 * feature_width)
    window = jnp.stack([ext_blocks[:-2], ext_blocks[1:-1], ext_blocks[2:]], axis=1)
    local_pairs = jnp.concatenate([window, random_pairs], axis=1).reshape(
        block_count, key_count, 2 * feature_width
    )
    local_keys = local_pairs[..., :feature_width].reshape(block_count, key_count, head_count, HD)
    local_values = local_pairs[..., feature_width:].reshape(block_count, key_count, head_count, HD)
    global_keys = global_pairs[..., :feature_width].reshape(GLB * BLK, head_count, HD)
    global_values = global_pairs[..., feature_width:].reshape(GLB * BLK, head_count, HD)
    query_heads = queries.reshape(block_count, BLK, head_count, HD)
    scores = (
        jnp.concatenate(
            [
                jnp.einsum(
                    "nqhd,nkhd->nhqk", query_heads, local_keys, preferred_element_type=jnp.float32
                ),
                jnp.einsum(
                    "nqhd,khd->nhqk", query_heads, global_keys, preferred_element_type=jnp.float32
                ),
            ],
            axis=-1,
        )
        * score_scale
    )
    block_ids = own_index * block_count + jnp.arange(block_count, dtype=jnp.int32)
    left_ok = block_ids > 0
    right_ok = block_ids < block_count * ctx_count - 1
    key_valid = jnp.concatenate(
        [
            jnp.repeat(left_ok[:, None], BLK, axis=1),
            jnp.ones((block_count, BLK), bool),
            jnp.repeat(right_ok[:, None], BLK, axis=1),
            jnp.ones((block_count, (RND + GLB) * BLK), bool),
        ],
        axis=1,
    )
    scores = jnp.where(key_valid[:, None, None, :], scores, masked_score)
    row_max = jnp.max(scores, axis=-1, keepdims=True)
    exponent = jnp.exp(scores - row_max)
    probabilities = exponent / jnp.sum(exponent, axis=-1, keepdims=True)
    weights = probabilities.astype(jnp.bfloat16)
    summed = jnp.einsum(
        "nhqk,nkhd->nqhd",
        weights[..., :key_count],
        local_values,
        preferred_element_type=jnp.float32,
    )
    summed = summed + jnp.einsum(
        "nhqk,khd->nqhd",
        weights[..., key_count:],
        global_values,
        preferred_element_type=jnp.float32,
    )
    attended = summed.reshape(row_count, feature_width).astype(jnp.bfloat16)
    grad_heads = grad_out.reshape(block_count, BLK, head_count, HD)
    grad_probs = jnp.concatenate(
        [
            jnp.einsum(
                "nqhd,nkhd->nhqk", grad_heads, local_values, preferred_element_type=jnp.float32
            ),
            jnp.einsum(
                "nqhd,khd->nhqk", grad_heads, global_values, preferred_element_type=jnp.float32
            ),
        ],
        axis=-1,
    )
    row_delta = jnp.sum(probabilities * grad_probs, axis=-1, keepdims=True)
    grad_scores = (probabilities * (grad_probs - row_delta) * score_scale).astype(jnp.bfloat16)
    grad_query = jnp.einsum(
        "nhqk,nkhd->nqhd",
        grad_scores[..., :key_count],
        local_keys,
        preferred_element_type=jnp.float32,
    )
    grad_query = grad_query + jnp.einsum(
        "nhqk,khd->nqhd",
        grad_scores[..., key_count:],
        global_keys,
        preferred_element_type=jnp.float32,
    )
    grad_query = grad_query.reshape(row_count, feature_width).astype(jnp.bfloat16)
    fsdp_rows = lax.psum_scatter(
        lax.dot_general(
            inputs, grad_query, (((0,), (0,)), ((), ())), preferred_element_type=jnp.float32
        ),
        "fsdp",
        scatter_dimension=0,
        tiled=True,
    )
    query_grad = lax.psum(fsdp_rows, "ctx")
    return (attended[None], query_grad)


def solution(mesh):
    placed = (
        P("fsdp", "ctx", None),
        P("fsdp", None),
        P("fsdp", None),
        P("fsdp", None),
        P("fsdp", "ctx", None),
        P("fsdp", None, None),
        P("fsdp", None, None),
        P("fsdp", None),
    )
    return jax.shard_map(
        per_device,
        mesh=mesh,
        in_specs=placed,
        out_specs=(P("fsdp", "ctx", None), P("fsdp", None)),
        check_vma=False,
    )
```

profile of v0, /device:TPU:1, one launch (start us, length us, event | category | flops | bytes accessed | tf_op | source)
XLA Modules:
  0.0 946.1 jit_solution(4117602353361528883)
XLA Ops:
  11.6 117.1 %all-gather.4.cloned.1.call-done = bf16[2048,512]{1,0:T(8,128)(2,1)} async-done(((bf16[64,512]{1,0:T(8,128)(2,1)}), bf16[2048,512]{1,0:T(8,128)(2,1)}) %all-gather.4.cloned.1.call-update) | async-done | bytes 2097168 | tf_op jit(solution)/shard_map/all_gather | solution.py:81
  128.6 2.3 convolution_convert_fusion.2
  130.9 132.3 %all-gather.6.cloned.1.call-done = bf16[2048,512]{1,0:T(8,128)(2,1)} async-done(((bf16[64,512]{1,0:T(8,128)(2,1)}), bf16[2048,512]{1,0:T(8,128)(2,1)}) %all-gather.6.cloned.1.call-update) | async-done | bytes 2097168 | tf_op jit(solution)/shard_map/all_gather | solution.py:82
  263.2 2.3 convolution_convert_fusion.1
  265.5 24.3 %collective-permute-start = (bf16[64,1024]{1,0:T(8,128)(2,1)S(1)}, bf16[64,1024]{1,0:T(8,128)(2,1)S(1)}, u32[]{:S(2)}, u32[]{:S(2)}) collective-permute-start(bf16[64,1024]{1,0:T(8,128)(2,1)S(1)} %get-tuple-element.19), channel_id=1, source_target_pairs={{0,32},{32,64},{64,96},{96,128},{128,160},{160,192},{192,224},{224... | collective-permute-start | bytes 393224 | tf_op jit(solution)/shard_map/ppermute | solution.py:23
  289.8 1.9 collective-permute-start.1
  292.0 4.1 collective-permute-done.1
  297.3 2.8 gather_fusion
  300.1 9.3 all-to-all-start
  312.1 120.0 %all-gather.8.cloned.1.call-done = bf16[2048,512]{1,0:T(8,128)(2,1)} async-done(((bf16[64,512]{1,0:T(8,128)(2,1)}), bf16[2048,512]{1,0:T(8,128)(2,1)}) %all-gather.8.cloned.1.call-update) | async-done | bytes 2097168 | tf_op jit(solution)/shard_map/all_gather | solution.py:80
  432.1 2.3 convolution_convert_fusion
  434.5 171.0 %all-reduce.3.cloned.1.call-done = bf16[2,64,1024]{2,1,0:T(8,128)(2,1)} async-done(((bf16[2,64,1024]{2,1,0:T(8,128)(2,1)}), bf16[2,64,1024]{2,1,0:T(8,128)(2,1)}) %all-reduce.3.cloned.1.call-update) | async-done | bytes 262160 | tf_op jit(solution)/shard_map/psum | solution.py:101
  608.7 2.8 gather_fusion.1
  612.9 1.9 fusion.54
  614.8 1.9 copy.118
  618.5 1.9 copy.117
  622.9 5.6 multiply_convert_fusion
  629.8 2.7 convolution_bitcast_fusion
  632.5 5.4 copy.138
  638.0 1.8 fusion.53
  641.0 120.8 %reduce-scatter.4.cloned.1.call-done = f32[64,512]{1,0:T(8,128)} async-done(((f32[2048,512]{1,0:T(8,128)}), f32[64,512]{1,0:T(8,128)}) %reduce-scatter.4.cloned.1.call-update) | async-done | bytes 131088
  761.8 1.7 copy.139
  763.5 1.9 fusion.11
  766.5 171.1 %all-reduce.5.cloned.1.call-done = f32[64,512]{0,1:T(8,128)} async-done(((f32[64,512]{0,1:T(8,128)}), f32[64,512]{0,1:T(8,128)}) %all-reduce.5.cloned.1.call-update) | async-done | bytes 131088 | tf_op jit(solution)/shard_map/psum | solution.py:195
  (100 shorter events, 22.3 us)
Async XLA Ops:
  7.2 121.5 %copy-start = (bf16[1,256,2048]{2,1,0:T(8,128)(2,1)S(1)}, bf16[1,256,2048]{2,1,0:T(8,128)(2,1)}, u32[]{:S(2)}) copy-start(bf16[1,256,2048]{2,1,0:T(8,128)(2,1)} %param.8) | copy-start | bytes 3145732
  7.2 121.5 %all-gather.4.cloned.1.call-start = ((), (), s32[]{:S(2)}) async-start(), calls=%async_computation.2 | async-start | bytes 2162688 | tf_op jit(solution)/shard_map/all_gather | solution.py:81
  7.9 255.3 %all-gather.6.cloned.1.call-start = ((), (), s32[]{:S(2)}) async-start(), calls=%async_computation.3 | async-start | bytes 2162688 | tf_op jit(solution)/shard_map/all_gather | solution.py:82
  8.7 423.4 %all-gather.8.cloned.1.call-start = ((), (), s32[]{:S(2)}) async-start(), calls=%async_computation.4 | async-start | bytes 2162688 | tf_op jit(solution)/shard_map/all_gather | solution.py:80
  265.5 26.4 %collective-permute-start = (bf16[64,1024]{1,0:T(8,128)(2,1)S(1)}, bf16[64,1024]{1,0:T(8,128)(2,1)S(1)}, u32[]{:S(2)}, u32[]{:S(2)}) collective-permute-start(bf16[64,1024]{1,0:T(8,128)(2,1)S(1)} %get-tuple-element.19), channel_id=1, source_target_pairs={{0,32},{32,64},{64,96},{96,128},{128,160},{160,192},{192,224},{224... | collective-permute-start | bytes 393224 | tf_op jit(solution)/shard_map/ppermute | solution.py:23
  289.8 6.3 collective-permute-start.1
  300.1 9.4 copy-start.13
  300.1 10.0 %copy-start.12 = (bf16[1,256,512]{2,1,0:T(8,128)(2,1)S(1)}, bf16[1,256,512]{2,1,0:T(8,128)(2,1)}, u32[]{:S(2)}) copy-start(bf16[1,256,512]{2,1,0:T(8,128)(2,1)} %param.12) | copy-start | bytes 786436
  300.1 10.1 %copy-start.14 = (s32[1,2]{1,0:T(1,128)S(1)}, s32[1,2]{1,0:T(1,128)}, u32[]{:S(2)}) copy-start(s32[1,2]{1,0:T(1,128)} %param.15) | copy-start | bytes 28
  300.1 308.5 %all-to-all-start = ((bf16[16,2,64,1024]{3,2,1,0:T(8,128)(2,1)}), bf16[16,2,64,1024]{3,2,1,0:T(8,128)(2,1)}, u32[]{:S(2)}, u32[]{:S(2)}) async-start(bf16[16,2,64,1024]{3,2,1,0:T(8,128)(2,1)} %bitcast.101), calls=%async_computation | async-start | bytes 8388608 | tf_op jit(solution)/shard_map/all_to_all | solution.py:93
  309.4 296.0 %all-reduce.3.cloned.1.call-start = ((), (), s32[]{:S(2)}) async-start(), calls=%async_computation.5 | async-start | bytes 524288 | tf_op jit(solution)/shard_map/psum | solution.py:101
  312.0 449.8 %reduce-scatter.4.cloned.1.call-start = ((), (), s32[]{:S(2)}) async-start(), calls=%async_computation.7 | async-start | bytes 4325376
  434.4 174.2 %copy-start.4 = (bf16[4,64,4,128]{3,2,1,0:T(4,128)(2,1)}, bf16[4,64,4,128]{3,2,1,0:T(4,128)(2,1)S(1)}, u32[]{:S(2)}) copy-start(bf16[4,64,4,128]{3,2,1,0:T(4,128)(2,1)S(1)} %reshape.230) | copy-start | bytes 786436
  606.5 2.2 copy-start.8
  614.8 2.0 copy-start.5
  616.8 1.7 copy-start.1
  620.4 1.4 copy-start.7
  620.4 1.5 copy-start.11
  621.9 1.0 copy-start.10
  622.8 5.7 copy-start.6
  622.9 5.6 copy-start.9
  622.9 5.8 copy-start.2
  637.9 299.6 %all-reduce.5.cloned.1.call-start = ((), (), s32[]{:S(2)}) async-start(), calls=%async_computation.6 | async-start | bytes 524288 | tf_op jit(solution)/shard_map/psum | solution.py:195
  639.8 1.0 copy-start.3
Sparse Core Ops, SparseCore 0:
  10.1 118.4 all-gather.3
  130.7 132.4 all-gather.5
  265.3 166.7 all-gather.7
  435.4 169.9 all-reduce.2
  638.0 123.6 reduce-scatter.3
  764.8 172.7 all-reduce.4
where the time goes:
time: 947 us; the launch traced here: 946 us
  waiting for transfers between devices  838 us (88%)
  starting transfers between devices  35.8 us (4%)
  local copies, waits for them, and re-layouts  27.5 us (3%)
  matrix products  17 us (2%)
  between operations  14.5 us (2%)
  other arithmetic  13 us (1%)
    psum x1, waiting for transfers between devices, per_device(): query_grad = lax.psum(fsdp_rows, 'ctx')  171 us
    psum x1, waiting for transfers between devices, per_device(): global_pairs = lax.psum(owned_part.astype(jnp.bfloat16), 'ctx')  171 us
    all_gather x1, waiting for transfers between devices, per_device(): lax.all_gather(value_weight, 'fsdp', axis=0, tiled=True)  132 us
    unnamed x7, waiting for transfers between devices  123 us
    all_gather x1, waiting for transfers between devices, per_device(): lax.all_gather(query_weight, 'fsdp', axis=0, tiled=True)  120 us
    all_gather x1, waiting for transfers between devices, per_device(): lax.all_gather(key_weight, 'fsdp', axis=0, tiled=True)  117 us
    ppermute x1, starting transfers between devices, padded(): lax.ppermute(tail, axis, [(i, (i + 1) % count) for i in range(ends)])  24.3 us
  transfers between devices with their start and end apart: 9, of which 7 were waited for; matrix products, arithmetic and copies ran while one was open for 3% of the time, Pallas kernels for 0%

commit v1 on v0

v1 whole, which is shorter than its diff:
```python
import jax
import jax.numpy as jnp
from jax import lax
from jax.experimental import pallas as pl
from jax.experimental.pallas import tpu as pltpu
from jax.sharding import Mesh
from jax.sharding import PartitionSpec as P

HD = 128
BLK = 64
RND = 3
GLB = 2
NBL = 4
CHIP_BLOCKS = 8
CHIPS = 8
MASKED = -1e30

NT = (((1,), (1,)), ((), ()))
NN = (((1,), (0,)), ((), ()))
TN = (((0,), (0,)), ((), ()))


def dot32(a, b, dims):
    return lax.dot_general(a, b, dims, preferred_element_type=jnp.float32)


def spread(block, axes):
    count = lax.axis_size(axes)
    return lax.all_to_all(
        jnp.broadcast_to(block[None], (count, *block.shape)), axes, 0, 0, tiled=True
    )


def shifted(block, axis, step):
    count = lax.axis_size(axis)
    return lax.ppermute(block, axis, [(i, (i + step) % count) for i in range(count)])


def attention_kernel(
    where_ref, owner_ref, offset_ref, global_ref, q_ref, g_ref, *rest
):
    pieces, (out_ref, gq_ref, kv_ref, sems) = rest[:CHIPS], rest[CHIPS:]
    copies = [
        pltpu.make_async_copy(
            piece, kv_ref.at[pl.ds(slot * CHIP_BLOCKS, CHIP_BLOCKS)], sems.at[slot]
        )
        for slot, piece in enumerate(pieces)
    ]
    for copy in copies:
        copy.start()
    my_yh, my_x, my_core = where_ref[0], where_ref[1], where_ref[2]
    my_chip = my_yh * 4 + my_x

    def place(block):
        chip = block // CHIP_BLOCKS
        inside = lax.rem(block, CHIP_BLOCKS)
        inside = lax.rem(inside + NBL * my_core, CHIP_BLOCKS)
        hop = lax.rem(chip + 4 - my_x, 4)
        side = jnp.where(chip // 4 == my_yh, 0, 1)
        return (side * 4 + hop) * CHIP_BLOCKS + inside

    for copy in copies:
        copy.wait()

    lane = lax.broadcasted_iota(jnp.int32, (1, 2 * BLK), 1)
    total = CHIPS * CHIP_BLOCKS
    scale = HD**-0.5

    def one_block(local, carry):
        inside = lax.rem(local + NBL * my_core, CHIP_BLOCKS)
        block = my_chip * CHIP_BLOCKS + inside
        left = jnp.maximum(block - 1, 0)
        right = jnp.minimum(block + 1, total - 1)
        named = [left, right, block]
        for r in range(RND):
            named.append(owner_ref[block, r] * NBL + offset_ref[block, r])
        for r in range(GLB):
            named.append(global_ref[0, r])
        spots = [place(b) for b in named]
        kv = jnp.concatenate([kv_ref[s] for s in spots], axis=0)
        allowed = ((lane < BLK) & (block > 0)) | ((lane >= BLK) & (block < total - 1))
        rows = pl.ds(pl.multiple_of(local * BLK, BLK), BLK)
        for h in range(2):
            cols = slice(h * HD, (h + 1) * HD)
            q = q_ref[rows, cols]
            g = g_ref[rows, cols]
            k = kv[:, h * HD : (h + 1) * HD]
            v = kv[:, (2 + h) * HD : (3 + h) * HD]
            s = dot32(q, k, NT) * scale
            s = jnp.concatenate(
                [jnp.where(allowed, s[:, : 2 * BLK], MASKED), s[:, 2 * BLK :]], axis=1
            )
            e = jnp.exp(s - jnp.max(s, axis=1, keepdims=True))
            p = e / jnp.sum(e, axis=1, keepdims=True)
            out_ref[rows, cols] = dot32(p.astype(jnp.bfloat16), v, NN).astype(
                jnp.bfloat16
            )
            gp = dot32(g, v, NT)
            delta = jnp.sum(p * gp, axis=1, keepdims=True)
            ds = (p * (gp - delta) * scale).astype(jnp.bfloat16)
            gq_ref[rows, cols] = dot32(ds, k, NN).astype(jnp.bfloat16)
        return carry

    lax.fori_loop(0, CHIP_BLOCKS, one_block, 0)


def attention(where, owners, offsets, global_list, queries, grads, pieces):
    rows, width = queries.shape
    smem = pl.BlockSpec(memory_space=pltpu.SMEM)
    vmem = pl.BlockSpec(memory_space=pltpu.VMEM)
    return pl.pallas_call(
        attention_kernel,
        out_shape=(
            jax.ShapeDtypeStruct((rows, width), jnp.bfloat16),
            jax.ShapeDtypeStruct((rows, width), jnp.bfloat16),
        ),
        in_specs=[smem] * 4 + [vmem] * 2 + [pl.BlockSpec(memory_space=pl.ANY)] * CHIPS,
        out_specs=(vmem, vmem),
        scratch_shapes=[
            pltpu.VMEM((CHIPS * CHIP_BLOCKS, BLK, 2 * width), jnp.bfloat16),
            pltpu.SemaphoreType.DMA((CHIPS,)),
        ],
        compiler_params=pltpu.CompilerParams(vmem_limit_bytes=24 * 1024 * 1024),
        name="attention",
    )(where, owners, offsets, global_list, queries, grads, *pieces)


def per_device(
    tokens, query_weight, key_weight, value_weight, cotangent, rand_owner, rand_offset, global_ids
):
    own = tokens[0]
    grad_out = cotangent[0]
    yh, x, core = lax.axis_index("yh"), lax.axis_index("x"), lax.axis_index("core")
    part = yh * 4 + x
    half = query_weight.shape[1] // 2

    other = shifted(own, "core", 1)
    grads_mine = lax.dynamic_slice_in_dim(grad_out, core * half, half, 1)
    grads_send = lax.dynamic_slice_in_dim(grad_out, (1 - core) * half, half, 1)
    grads = jnp.concatenate([grads_mine, shifted(grads_send, "core", 1)], axis=0)

    rows = query_weight.shape[0] // 8
    weight_part = jnp.concatenate(
        [
            lax.dynamic_slice(w, (part * rows, core * half), (rows, half))
            for w in (key_weight, value_weight, query_weight)
        ],
        axis=1,
    )
    weight = spread(weight_part, "z").reshape(16, rows, 3 * half)
    weight = spread(weight, ("yh", "yl"))
    weight = spread(weight, "x")
    weight = weight.reshape(4, 2, 2, 16, rows, 3 * half)
    weight = weight.transpose(3, 2, 1, 0, 4, 5).reshape(-1, 3 * half)

    def project(inputs):
        return dot32(inputs, weight, NN).astype(jnp.bfloat16)

    mine, theirs = project(own), project(other)
    kv = jnp.concatenate([mine[:, : 2 * half], theirs[:, : 2 * half]], axis=0)
    queries = jnp.concatenate([mine[:, 2 * half :], theirs[:, 2 * half :]], axis=0)
    kv = kv.reshape(CHIP_BLOCKS, BLK, 2 * half)
    across = shifted(kv, "yh", 1)
    pieces = []
    for block in (kv, across):
        before, after = shifted(block, "x", 1), shifted(block, "x", -1)
        cut = CHIP_BLOCKS // 2
        far = jnp.concatenate(
            [shifted(before[:cut], "x", 1), shifted(after[cut:], "x", -1)], axis=0
        )
        pieces += [block, after, far, before]

    where = jnp.stack([yh, x, core]).astype(jnp.int32)
    attended, grad_query = attention(
        where, rand_owner[0], rand_offset[0], global_ids, queries, grads, pieces
    )
    count = own.shape[0]
    out_back = shifted(attended[count:], "core", 1)
    out_mine = attended[:count]
    attn = jnp.where(
        core == 0,
        jnp.concatenate([out_mine, out_back], axis=1),
        jnp.concatenate([out_back, out_mine], axis=1),
    )

    partial = dot32(own, grad_query[:count], TN) + dot32(other, grad_query[count:], TN)
    partial = partial.astype(jnp.bfloat16).reshape(16, 2, 2, 4, rows, half)
    partial = partial.transpose(1, 2, 3, 0, 4, 5).reshape(16, 16 * rows, half)
    partial = lax.all_to_all(partial, ("yl", "yh", "x"), 0, 0, tiled=True)
    partial = jnp.sum(partial.astype(jnp.float32), axis=0).astype(jnp.bfloat16)
    partial = lax.all_to_all(partial.reshape(16, rows, half), "z", 0, 0, tiled=True)
    partial = jnp.sum(partial.astype(jnp.float32), axis=0)
    final = spread(partial, ("yh", "x", "core")).reshape(8, 2, rows, half)
    query_grad = final.transpose(0, 2, 1, 3).reshape(8 * rows, 2 * half)
    return attn[None], query_grad


def solution(mesh):
    fine = Mesh(
        mesh.devices.reshape(2, 4, 2, 16, 2),
        ("yh", "x", "core", "z", "yl"),
        axis_types=(jax.sharding.AxisType.Auto,) * 5,
    )
    ctx, fsdp = ("yh", "x", "core"), ("z", "yl")
    placed = (
        P(fsdp, ctx, None),
        P(fsdp, None),
        P(fsdp, None),
        P(fsdp, None),
        P(fsdp, ctx, None),
        P(fsdp, None, None),
        P(fsdp, None, None),
        P(fsdp, None),
    )
    return jax.shard_map(
        per_device,
        mesh=fine,
        in_specs=placed,
        out_specs=(P(fsdp, ctx, None), P(fsdp, None)),
        check_vma=False,
    )
```

time: 947 us -> 215 us (0.23)
  waiting for transfers between devices: 838 us -> 44.4 us
  blocking collectives: 0 us -> 59.4 us
  starting transfers between devices: 35.8 us -> 75.5 us
  local copies, waits for them, and re-layouts: 27.5 us -> 10.7 us
  between operations: 14.5 us -> 1.06 us
  Pallas kernels: 0 us -> 13.1 us
  matrix products: 17 us -> 5.47 us
    all_gather x3 -> x0, waiting for transfers between devices: 369 us -> none  [the longest x1 132 us: per_device(): lax.all_gather(value_weight, 'fsdp', axis=0, tiled=True)]
    psum x2 -> x0, waiting for transfers between devices: 342 us -> none  [the longest x1 171 us: per_device(): query_grad = lax.psum(fsdp_rows, 'ctx')]
    unnamed x7 -> x0, waiting for transfers between devices: 123 us -> none
    all_to_all x0 -> x3, blocking collectives: none -> 59.4 us  [the longest x2 40.4 us: spread(): lax.all_to_all(jnp.broadcast_to(block[None], (count, *block.shape)), axes...]
    all_to_all x1 -> x3, waiting for transfers between devices: 0.01 us -> 36.5 us  [the longest x2 29.4 us: spread(): lax.all_to_all(jnp.broadcast_to(block[None], (count, *block.shape)), axes...]
    ppermute x2 -> x12, starting transfers between devices: 26.2 us -> 50.2 us  [shifted(): lax.ppermute(block, axis, [(i, (i + step) % count) for i in range(count)])]
    all_to_all x1 -> x3, starting transfers between devices: 9.34 us -> 25.2 us  [the longest x1 14 us: per_device(): lax.all_to_all(partial.reshape(16, rows, half), 'z', 0, 0, tiled=True)]
    pallas_call x0 -> x1, Pallas kernels: none -> 13.1 us  [attention(): pl.pallas_call(attention_kernel, out_shape=(jax.ShapeDtypeStruct((rows, w...]
  transfers between devices with their start and end apart: 9 -> 15, of which waited for: 7 -> 6; matrix products, arithmetic and copies ran while one was open for 3% -> 4% of each run, Pallas kernels for 0% -> 0%
where the time goes in v1:
time: 215 us; the launch traced here: 214 us
  starting transfers between devices  75.5 us (35%)
  blocking collectives  59.4 us (28%)
  waiting for transfers between devices  44.4 us (21%)
  Pallas kernels  13.1 us (6%)
  local copies, waits for them, and re-layouts  10.7 us (5%)
  matrix products  5.47 us (3%)
  other arithmetic  3.87 us (2%)
    ppermute x12, starting transfers between devices, shifted(): lax.ppermute(block, axis, [(i, (i + step) % count) for i in range(count)])  50.2 us
    all_to_all x2, blocking collectives, spread(): lax.all_to_all(jnp.broadcast_to(block[None], (count, *block.shape)), axes...  40.4 us
    all_to_all x2, waiting for transfers between devices, spread(): lax.all_to_all(jnp.broadcast_to(block[None], (count, *block.shape)), axes...  29.4 us
    all_to_all x1, blocking collectives, per_device(): partial = lax.all_to_all(partial, ('yl', 'yh', 'x'), 0, 0, tiled=True)  19 us
    all_to_all x1, starting transfers between devices, per_device(): lax.all_to_all(partial.reshape(16, rows, half), 'z', 0, 0, tiled=True)  14 us
    pallas_call x1, Pallas kernels, attention(): pl.pallas_call(attention_kernel, out_shape=(jax.ShapeDtypeStruct((rows, w...  13.1 us
    all_to_all x2, starting transfers between devices, spread(): lax.all_to_all(jnp.broadcast_to(block[None], (count, *block.shape)), axes...  11.3 us
    ppermute x12, waiting for transfers between devices, shifted(): lax.ppermute(block, axis, [(i, (i + step) % count) for i in range(count)])  7.92 us
  transfers between devices with their start and end apart: 15, of which 6 were waited for; matrix products, arithmetic and copies ran while one was open for 4% of the time, Pallas kernels for 0%

profile of v1, /device:TPU:1, one launch (start us, length us, event | category | flops | bytes accessed | tf_op | source)
XLA Modules:
  0.0 213.5 jit_solution(9800137847426013554)
XLA Ops:
  2.7 28.1 %all_to_all.30 = bf16[16,8,768]{2,1,0:T(8,128)(2,1)S(1)} all-to-all(bf16[16,8,768]{2,1,0:T(8,128)(2,1)S(1)} %broadcast_in_dim.8), channel_id=1, replica_groups=mesh['yh'=2,'x'=4,'core'=2,'z'=16,'yl'=2] {'z'}, dimensions={0} | all-to-all | bytes 393216 | tf_op jit(solution)/shard_map/all_to_all | solution.py:29
  30.9 12.3 %all_to_all.31 = bf16[4,16,8,768]{3,2,1,0:T(8,128)(2,1)S(1)} all-to-all(bf16[4,16,8,768]{3,2,1,0:T(8,128)(2,1)S(1)} %broadcast_in_dim.9), channel_id=1, replica_groups=mesh['yh'=2,'x'=4,'core'=2,'z'=16,'yl'=2] {'yh','yl'}, dimensions={0} | all-to-all | bytes 1572864 | tf_op jit(solution)/shard_map/all_to_all | solution.py:29
  45.2 4.0 %all-to-all-start.2 = ((bf16[4,4,16,8,768]{4,3,2,1,0:T(8,128)(2,1)}), bf16[4,4,16,8,768]{4,3,2,1,0:T(8,128)(2,1)S(1)}, u32[]{:S(2)}, u32[]{:S(2)}) async-start(bf16[4,4,16,8,768]{4,3,2,1,0:T(8,128)(2,1)} %broadcast_in_dim.10), calls=%async_computation.2 | async-start | bytes 6291456 | tf_op jit(solution)/shard_map/all_to_all | solution.py:29
  49.2 8.4 %collective-permute-start = (bf16[256,2048]{1,0:T(8,128)(2,1)}, bf16[256,2048]{1,0:T(8,128)(2,1)}, u32[]{:S(2)}, u32[]{:S(2)}) collective-permute-start(bf16[256,2048]{1,0:T(8,128)(2,1)} %bitcast.53), channel_id=1, source_target_pairs={{0,32},{32,0},{1,33},{33,1},{2,34},{34,2},{3,35},{35,3},{4,36},{36... | collective-permute-start | bytes 3145736 | tf_op jit(solution)/shard_map/ppermute | solution.py:36
  57.6 22.6 %all-to-all-done.2 = bf16[4,4,16,8,768]{4,3,2,1,0:T(8,128)(2,1)S(1)} async-done(((bf16[4,4,16,8,768]{4,3,2,1,0:T(8,128)(2,1)}), bf16[4,4,16,8,768]{4,3,2,1,0:T(8,128)(2,1)S(1)}, u32[]{:S(2)}, u32[]{:S(2)}) %all-to-all-start.2) | async-done | bytes 3145760 | tf_op jit(solution)/shard_map/all_to_all | solution.py:29
  82.4 2.3 %fusion.3 = bf16[256,768]{1,0:T(8,128)(2,1)S(1)} fusion(bf16[256,2048]{1,0:T(8,128)(2,1)} %collective-permute-done, bf16[2048,768]{1,0:T(8,128)(2,1)S(1)} %bitcast.52), kind=kOutput, calls=%fused_computation.6 | convolution fusion | flops 805502976 | bytes 4587520 | tf_op jit(solution)/shard_map/dot_general | solution.py:24
  85.0 2.6 %collective-permute-start.6 = (bf16[8,64,512]{2,1,0:T(8,128)(2,1)S(1)}, bf16[8,64,512]{2,1,0:T(8,128)(2,1)S(1)}, u32[]{:S(2)}, u32[]{:S(2)}) collective-permute-start(bf16[8,64,512]{2,1,0:T(8,128)(2,1)S(1)} %bitcast.42), channel_id=1, source_target_pairs={{0,256},{256,0},{1,257},{257,1},{2,258},{258,2},{3,259},{259,3},{4... | collective-permute-start | bytes 1572872 | tf_op jit(solution)/shard_map/ppermute | solution.py:36
  87.5 2.2 %collective-permute-start.3 = (bf16[8,64,512]{2,1,0:T(8,128)(2,1)S(1)}, bf16[8,64,512]{2,1,0:T(8,128)(2,1)S(1)}, u32[]{:S(2)}, u32[]{:S(2)}) collective-permute-start(bf16[8,64,512]{2,1,0:T(8,128)(2,1)S(1)} %bitcast.43), channel_id=1, source_target_pairs={{0,64},{64,128},{128,192},{192,0},{1,65},{65,129},{129,193},{193,1... | collective-permute-start | bytes 1572872 | tf_op jit(solution)/shard_map/ppermute | solution.py:36
  89.7 4.3 %collective-permute-start.2 = (bf16[8,64,512]{2,1,0:T(8,128)(2,1)S(1)}, bf16[8,64,512]{2,1,0:T(8,128)(2,1)S(1)}, u32[]{:S(2)}, u32[]{:S(2)}) collective-permute-start(bf16[8,64,512]{2,1,0:T(8,128)(2,1)S(1)} %bitcast.44), channel_id=1, source_target_pairs={{0,192},{64,0},{128,64},{192,128},{1,193},{65,1},{129,65},{193,129... | collective-permute-start | bytes 1572872 | tf_op jit(solution)/shard_map/ppermute | solution.py:36
  94.0 2.5 %collective-permute-done.6.rest_4_ = bf16[8,64,512]{2,1,0:T(8,128)(2,1)S(1)} collective-permute-done((bf16[8,64,512]{2,1,0:T(8,128)(2,1)S(1)}, bf16[8,64,512]{2,1,0:T(8,128)(2,1)S(1)}, u32[]{:S(2)}, u32[]{:S(2)}) %collective-permute-start.6) | collective-permute-done | bytes 524320 | tf_op jit(solution)/shard_map/ppermute | solution.py:36
  96.5 2.8 %collective-permute-start.7 = (bf16[8,64,512]{2,1,0:T(8,128)(2,1)S(1)}, bf16[8,64,512]{2,1,0:T(8,128)(2,1)S(1)}, u32[]{:S(2)}, u32[]{:S(2)}) collective-permute-start(bf16[8,64,512]{2,1,0:T(8,128)(2,1)S(1)} %collective-permute-done.6.rest_4_), channel_id=1, source_target_pairs={{0,192},{64,0},{128,64},{192,128},{1,193},{65,1},{129,65},{193,129... | collective-permute-start | bytes 1572872 | tf_op jit(solution)/shard_map/ppermute | solution.py:36
  99.3 2.6 %collective-permute-start.8 = (bf16[8,64,512]{2,1,0:T(8,128)(2,1)S(1)}, bf16[8,64,512]{2,1,0:T(8,128)(2,1)S(1)}, u32[]{:S(2)}, u32[]{:S(2)}) collective-permute-start(bf16[8,64,512]{2,1,0:T(8,128)(2,1)S(1)} %collective-permute-done.6.rest_4_), channel_id=1, source_target_pairs={{0,64},{64,128},{128,192},{192,0},{1,65},{65,129},{129,193},{193,1... | collective-permute-start | bytes 1572872 | tf_op jit(solution)/shard_map/ppermute | solution.py:36
  103.6 11.1 %collective-permute-start.1 = (bf16[256,256]{1,0:T(8,128)(2,1)}, bf16[256,256]{1,0:T(8,128)(2,1)}, u32[]{:S(2)}, u32[]{:S(2)}) collective-permute-start(bf16[256,256]{1,0:T(8,128)(2,1)} %get-tuple-element.9), channel_id=1, source_target_pairs={{0,32},{32,0},{1,33},{33,1},{2,34},{34,2},{3,35},{35,3},{4,36},{36... | collective-permute-start | bytes 393224 | tf_op jit(solution)/shard_map/ppermute | solution.py:36
  118.4 4.3 %collective-permute-start.5 = (bf16[4,64,512]{2,1,0:T(8,128)(2,1)}, bf16[4,64,512]{2,1,0:T(8,128)(2,1)}, u32[]{:S(2)}, u32[]{:S(2)}) collective-permute-start(bf16[4,64,512]{2,1,0:T(8,128)(2,1)} %slice.53), channel_id=1, source_target_pairs={{0,192},{64,0},{128,64},{192,128},{1,193},{65,1},{129,65},{193,129... | collective-permute-start | bytes 786440 | tf_op jit(solution)/shard_map/ppermute | solution.py:36
  123.0 2.8 %collective-permute-start.10 = (bf16[4,64,512]{2,1,0:T(8,128)(2,1)S(1)}, bf16[4,64,512]{2,1,0:T(8,128)(2,1)S(1)}, u32[]{:S(2)}, u32[]{:S(2)}) collective-permute-start(bf16[4,64,512]{2,1,0:T(8,128)(2,1)S(1)} %slice.55), channel_id=1, source_target_pairs={{0,192},{64,0},{128,64},{192,128},{1,193},{65,1},{129,65},{193,129... | collective-permute-start | bytes 786440 | tf_op jit(solution)/shard_map/ppermute | solution.py:36
  125.8 2.5 %collective-permute-start.9 = (bf16[4,64,512]{2,1,0:T(8,128)(2,1)S(1)}, bf16[4,64,512]{2,1,0:T(8,128)(2,1)S(1)}, u32[]{:S(2)}, u32[]{:S(2)}) collective-permute-start(bf16[4,64,512]{2,1,0:T(8,128)(2,1)S(1)} %slice.54), channel_id=1, source_target_pairs={{0,64},{64,128},{128,192},{192,0},{1,65},{65,129},{129,193},{193,1... | collective-permute-start | bytes 786440 | tf_op jit(solution)/shard_map/ppermute | solution.py:36
  130.5 3.4 %collective-permute-done.10 = bf16[4,64,512]{2,1,0:T(8,128)(2,1)S(1)} collective-permute-done((bf16[4,64,512]{2,1,0:T(8,128)(2,1)S(1)}, bf16[4,64,512]{2,1,0:T(8,128)(2,1)S(1)}, u32[]{:S(2)}, u32[]{:S(2)}) %collective-permute-start.10) | collective-permute-done | bytes 262176 | tf_op jit(solution)/shard_map/ppermute | solution.py:36
  136.0 13.1 %attention.1 = (bf16[512,256]{1,0:T(8,128)(2,1)S(1)}, bf16[512,256]{1,0:T(8,128)(2,1)S(1)}) custom-call(s32[3]{0:T(128)S(1)} %pad_add_fusion.where_ref, s32[64,3]{1,0:T(8,128)S(1)} %bitcast.46, s32[64,3]{1,0:T(8,128)S(1)} %bitcast.47, s32[1,2]{1,0:T(1,128)S(1)} %copy-done, bf16[512,256]{1,0:T(8,128)(2,1)S(1)} %pad_maximum_fusion.3.q_ref, ...), custom_call_target="tpu_custom_call" | custom-call | tf_op jit(solution)/shard_map/attention/pallas_call | solution.py:111
  151.9 19.0 %all_to_all.32 = bf16[16,128,256]{2,1,0:T(8,128)(2,1)S(1)} all-to-all(bf16[16,128,256]{2,1,0:T(8,128)(2,1)S(1)} %bitcast.50), channel_id=1, replica_groups=mesh['yh'=2,'x'=4,'core'=2,'z'=16,'yl'=2] {'yl','yh','x'}, dimensions={0} | all-to-all | bytes 2097152 | tf_op jit(solution)/shard_map/all_to_all | solution.py:189
  171.7 14.0 %all-to-all-start.4 = ((bf16[16,8,256]{2,1,0:T(8,128)(2,1)}), bf16[16,8,256]{2,1,0:T(8,128)(2,1)S(1)}, u32[]{:S(2)}, u32[]{:S(2)}) async-start(bf16[16,8,256]{2,1,0:T(8,128)(2,1)} %bitcast.20), calls=%async_computation.4 | async-start | bytes 131072 | tf_op jit(solution)/shard_map/all_to_all | solution.py:191
  185.7 4.5 %collective-permute-start.11 = (bf16[256,256]{1,0:T(8,128)(2,1)S(1)}, bf16[256,256]{1,0:T(8,128)(2,1)S(1)}, u32[]{:S(2)}, u32[]{:S(2)}) collective-permute-start(bf16[256,256]{1,0:T(8,128)(2,1)S(1)} %get-tuple-element.7), channel_id=1, source_target_pairs={{0,32},{32,0},{1,33},{33,1},{2,34},{34,2},{3,35},{35,3},{4,36},{36... | collective-permute-start | bytes 393224 | tf_op jit(solution)/shard_map/ppermute | solution.py:36
  190.2 7.0 %all-to-all-done.4 = bf16[16,8,256]{2,1,0:T(8,128)(2,1)S(1)} async-done(((bf16[16,8,256]{2,1,0:T(8,128)(2,1)}), bf16[16,8,256]{2,1,0:T(8,128)(2,1)S(1)}, u32[]{:S(2)}, u32[]{:S(2)}) %all-to-all-start.4) | async-done | bytes 65568 | tf_op jit(solution)/shard_map/all_to_all | solution.py:191
  197.9 7.3 %all-to-all-start.5 = ((f32[16,8,256]{2,1,0:T(8,128)}), f32[16,8,256]{2,1,0:T(8,128)S(1)}, u32[]{:S(2)}, u32[]{:S(2)}) async-start(f32[16,8,256]{2,1,0:T(8,128)} %broadcast_in_dim.11), calls=%async_computation.5 | async-start | bytes 262144 | tf_op jit(solution)/shard_map/all_to_all | solution.py:29
  206.0 6.8 %all-to-all-done.5 = f32[16,8,256]{2,1,0:T(8,128)S(1)} async-done(((f32[16,8,256]{2,1,0:T(8,128)}), f32[16,8,256]{2,1,0:T(8,128)S(1)}, u32[]{:S(2)}, u32[]{:S(2)}) %all-to-all-start.5) | async-done | bytes 131104 | tf_op jit(solution)/shard_map/all_to_all | solution.py:29
  (63 shorter events, 21.9 us)
Async XLA Ops:
  45.2 35.1 %all-to-all-start.2 = ((bf16[4,4,16,8,768]{4,3,2,1,0:T(8,128)(2,1)}), bf16[4,4,16,8,768]{4,3,2,1,0:T(8,128)(2,1)S(1)}, u32[]{:S(2)}, u32[]{:S(2)}) async-start(bf16[4,4,16,8,768]{4,3,2,1,0:T(8,128)(2,1)} %broadcast_in_dim.10), calls=%async_computation.2 | async-start | bytes 6291456 | tf_op jit(solution)/shard_map/all_to_all | solution.py:29
  49.2 33.3 %collective-permute-start = (bf16[256,2048]{1,0:T(8,128)(2,1)}, bf16[256,2048]{1,0:T(8,128)(2,1)}, u32[]{:S(2)}, u32[]{:S(2)}) collective-permute-start(bf16[256,2048]{1,0:T(8,128)(2,1)} %bitcast.53), channel_id=1, source_target_pairs={{0,32},{32,0},{1,33},{33,1},{2,34},{34,2},{3,35},{35,3},{4,36},{36... | collective-permute-start | bytes 3145736 | tf_op jit(solution)/shard_map/ppermute | solution.py:36
  80.2 1.2 copy-start.1
  82.4 2.5 %copy-start.4 = (bf16[256,768]{1,0:T(8,128)(2,1)}, bf16[256,768]{1,0:T(8,128)(2,1)S(1)}, u32[]{:S(2)}) copy-start(bf16[256,768]{1,0:T(8,128)(2,1)S(1)} %fusion.2) | copy-start | bytes 1179652
  84.8 11.7 %copy-start.3 = (bf16[256,768]{1,0:T(8,128)(2,1)}, bf16[256,768]{1,0:T(8,128)(2,1)S(1)}, u32[]{:S(2)}) copy-start(bf16[256,768]{1,0:T(8,128)(2,1)S(1)} %fusion.3) | copy-start | bytes 1179652
  84.8 38.0 %copy-start.5 = (s32[1,64,3]{1,0,2:T(1,128)S(1)}, s32[1,64,3]{1,0,2:T(1,128)}, u32[]{:S(2)}) copy-start(s32[1,64,3]{1,0,2:T(1,128)} %param.13) | copy-start | bytes 2308
  84.8 38.0 %copy-start.6 = (s32[1,64,3]{1,0,2:T(1,128)S(1)}, s32[1,64,3]{1,0,2:T(1,128)}, u32[]{:S(2)}) copy-start(s32[1,64,3]{1,0,2:T(1,128)} %param.14) | copy-start | bytes 2308
  84.9 44.4 %slice-start.1 = ((bf16[256,768]{1,0:T(8,128)(2,1)}), bf16[256,256]{1,0:T(8,128)(2,1)S(1)}, s32[]{:S(2)}) async-start(bf16[256,768]{1,0:T(8,128)(2,1)} %copy-done.4), calls=%async_computation.7 | async-start | bytes 262144 | tf_op jit(solution)/shard_map/slice | solution.py:161
  85.0 11.6 %collective-permute-start.6 = (bf16[8,64,512]{2,1,0:T(8,128)(2,1)S(1)}, bf16[8,64,512]{2,1,0:T(8,128)(2,1)S(1)}, u32[]{:S(2)}, u32[]{:S(2)}) collective-permute-start(bf16[8,64,512]{2,1,0:T(8,128)(2,1)S(1)} %bitcast.42), channel_id=1, source_target_pairs={{0,256},{256,0},{1,257},{257,1},{2,258},{258,2},{3,259},{259,3},{4... | collective-permute-start | bytes 1572872 | tf_op jit(solution)/shard_map/ppermute | solution.py:36
  87.5 27.2 %collective-permute-start.3 = (bf16[8,64,512]{2,1,0:T(8,128)(2,1)S(1)}, bf16[8,64,512]{2,1,0:T(8,128)(2,1)S(1)}, u32[]{:S(2)}, u32[]{:S(2)}) collective-permute-start(bf16[8,64,512]{2,1,0:T(8,128)(2,1)S(1)} %bitcast.43), channel_id=1, source_target_pairs={{0,64},{64,128},{128,192},{192,0},{1,65},{65,129},{129,193},{193,1... | collective-permute-start | bytes 1572872 | tf_op jit(solution)/shard_map/ppermute | solution.py:36
  89.7 27.9 %collective-permute-start.2 = (bf16[8,64,512]{2,1,0:T(8,128)(2,1)S(1)}, bf16[8,64,512]{2,1,0:T(8,128)(2,1)S(1)}, u32[]{:S(2)}, u32[]{:S(2)}) collective-permute-start(bf16[8,64,512]{2,1,0:T(8,128)(2,1)S(1)} %bitcast.44), channel_id=1, source_target_pairs={{0,192},{64,0},{128,64},{192,128},{1,193},{65,1},{129,65},{193,129... | collective-permute-start | bytes 1572872 | tf_op jit(solution)/shard_map/ppermute | solution.py:36
  96.5 26.4 %collective-permute-start.7 = (bf16[8,64,512]{2,1,0:T(8,128)(2,1)S(1)}, bf16[8,64,512]{2,1,0:T(8,128)(2,1)S(1)}, u32[]{:S(2)}, u32[]{:S(2)}) collective-permute-start(bf16[8,64,512]{2,1,0:T(8,128)(2,1)S(1)} %collective-permute-done.6.rest_4_), channel_id=1, source_target_pairs={{0,192},{64,0},{128,64},{192,128},{1,193},{65,1},{129,65},{193,129... | collective-permute-start | bytes 1572872 | tf_op jit(solution)/shard_map/ppermute | solution.py:36
  99.3 30.0 %slice-start = ((bf16[256,768]{1,0:T(8,128)(2,1)}), bf16[256,256]{1,0:T(8,128)(2,1)S(1)}, s32[]{:S(2)}) async-start(bf16[256,768]{1,0:T(8,128)(2,1)} %copy-done.3), calls=%async_computation.6 | async-start | bytes 262144 | tf_op jit(solution)/shard_map/slice | solution.py:161
  99.3 26.5 %collective-permute-start.8 = (bf16[8,64,512]{2,1,0:T(8,128)(2,1)S(1)}, bf16[8,64,512]{2,1,0:T(8,128)(2,1)S(1)}, u32[]{:S(2)}, u32[]{:S(2)}) collective-permute-start(bf16[8,64,512]{2,1,0:T(8,128)(2,1)S(1)} %collective-permute-done.6.rest_4_), channel_id=1, source_target_pairs={{0,64},{64,128},{128,192},{192,0},{1,65},{65,129},{129,193},{193,1... | collective-permute-start | bytes 1572872 | tf_op jit(solution)/shard_map/ppermute | solution.py:36
  101.9 34.0 %copy-start = (s32[1,2]{1,0:T(1,128)S(1)}, s32[1,2]{1,0:T(1,128)}, u32[]{:S(2)}) copy-start(s32[1,2]{1,0:T(1,128)} %global_ref.1) | copy-start | bytes 28
  103.6 24.7 %collective-permute-start.1 = (bf16[256,256]{1,0:T(8,128)(2,1)}, bf16[256,256]{1,0:T(8,128)(2,1)}, u32[]{:S(2)}, u32[]{:S(2)}) collective-permute-start(bf16[256,256]{1,0:T(8,128)(2,1)} %get-tuple-element.9), channel_id=1, source_target_pairs={{0,32},{32,0},{1,33},{33,1},{2,34},{34,2},{3,35},{35,3},{4,36},{36... | collective-permute-start | bytes 393224 | tf_op jit(solution)/shard_map/ppermute | solution.py:36
  115.5 13.9 %collective-permute-start.4 = (bf16[4,64,512]{2,1,0:T(8,128)(2,1)}, bf16[4,64,512]{2,1,0:T(8,128)(2,1)}, u32[]{:S(2)}, u32[]{:S(2)}) collective-permute-start(bf16[4,64,512]{2,1,0:T(8,128)(2,1)} %slice.52), channel_id=1, source_target_pairs={{0,64},{64,128},{128,192},{192,0},{1,65},{65,129},{129,193},{193,1... | collective-permute-start | bytes 786440 | tf_op jit(solution)/shard_map/ppermute | solution.py:36
  118.4 11.0 %collective-permute-start.5 = (bf16[4,64,512]{2,1,0:T(8,128)(2,1)}, bf16[4,64,512]{2,1,0:T(8,128)(2,1)}, u32[]{:S(2)}, u32[]{:S(2)}) collective-permute-start(bf16[4,64,512]{2,1,0:T(8,128)(2,1)} %slice.53), channel_id=1, source_target_pairs={{0,192},{64,0},{128,64},{192,128},{1,193},{65,1},{129,65},{193,129... | collective-permute-start | bytes 786440 | tf_op jit(solution)/shard_map/ppermute | solution.py:36
  123.0 10.9 %collective-permute-start.10 = (bf16[4,64,512]{2,1,0:T(8,128)(2,1)S(1)}, bf16[4,64,512]{2,1,0:T(8,128)(2,1)S(1)}, u32[]{:S(2)}, u32[]{:S(2)}) collective-permute-start(bf16[4,64,512]{2,1,0:T(8,128)(2,1)S(1)} %slice.55), channel_id=1, source_target_pairs={{0,192},{64,0},{128,64},{192,128},{1,193},{65,1},{129,65},{193,129... | collective-permute-start | bytes 786440 | tf_op jit(solution)/shard_map/ppermute | solution.py:36
  125.8 10.1 %collective-permute-start.9 = (bf16[4,64,512]{2,1,0:T(8,128)(2,1)S(1)}, bf16[4,64,512]{2,1,0:T(8,128)(2,1)S(1)}, u32[]{:S(2)}, u32[]{:S(2)}) collective-permute-start(bf16[4,64,512]{2,1,0:T(8,128)(2,1)S(1)} %slice.54), channel_id=1, source_target_pairs={{0,64},{64,128},{128,192},{192,0},{1,65},{65,129},{129,193},{193,1... | collective-permute-start | bytes 786440 | tf_op jit(solution)/shard_map/ppermute | solution.py:36
  136.0 14.9 %copy-start.2 = (bf16[1,256,2048]{2,1,0:T(8,128)(2,1)S(1)}, bf16[1,256,2048]{2,1,0:T(8,128)(2,1)}, u32[]{:S(2)}) copy-start(bf16[1,256,2048]{2,1,0:T(8,128)(2,1)} %param.8) | copy-start | bytes 3145732
  171.7 25.5 %all-to-all-start.4 = ((bf16[16,8,256]{2,1,0:T(8,128)(2,1)}), bf16[16,8,256]{2,1,0:T(8,128)(2,1)S(1)}, u32[]{:S(2)}, u32[]{:S(2)}) async-start(bf16[16,8,256]{2,1,0:T(8,128)(2,1)} %bitcast.20), calls=%async_computation.4 | async-start | bytes 131072 | tf_op jit(solution)/shard_map/all_to_all | solution.py:191
  185.7 19.5 %collective-permute-start.11 = (bf16[256,256]{1,0:T(8,128)(2,1)S(1)}, bf16[256,256]{1,0:T(8,128)(2,1)S(1)}, u32[]{:S(2)}, u32[]{:S(2)}) collective-permute-start(bf16[256,256]{1,0:T(8,128)(2,1)S(1)} %get-tuple-element.7), channel_id=1, source_target_pairs={{0,32},{32,0},{1,33},{33,1},{2,34},{34,2},{3,35},{35,3},{4,36},{36... | collective-permute-start | bytes 393224 | tf_op jit(solution)/shard_map/ppermute | solution.py:36
  197.9 14.9 %all-to-all-start.5 = ((f32[16,8,256]{2,1,0:T(8,128)}), f32[16,8,256]{2,1,0:T(8,128)S(1)}, u32[]{:S(2)}, u32[]{:S(2)}) async-start(f32[16,8,256]{2,1,0:T(8,128)} %broadcast_in_dim.11), calls=%async_computation.5 | async-start | bytes 262144 | tf_op jit(solution)/shard_map/all_to_all | solution.py:29

commit v2 on v1

v2 whole, which is shorter than its diff:
```python
import jax
import jax.numpy as jnp
from jax import lax
from jax.experimental import pallas as pl
from jax.experimental.pallas import tpu as pltpu
from jax.sharding import Mesh
from jax.sharding import PartitionSpec as P

HD = 128
BLK = 64
RND = 3
GLB = 2
NBL = 4
PIECE_BLOCKS = 16
PIECES = 4
HEADS = 4
MASKED = -1e30

NT = (((1,), (1,)), ((), ()))
NN = (((1,), (0,)), ((), ()))
TN = (((0,), (0,)), ((), ()))


def dot32(a, b, dims):
    return lax.dot_general(a, b, dims, preferred_element_type=jnp.float32)


def spread(block, axes):
    count = lax.axis_size(axes)
    return lax.all_to_all(
        jnp.broadcast_to(block[None], (count, *block.shape)), axes, 0, 0, tiled=True
    )


def shifted(block, axis, step):
    count = lax.axis_size(axis)
    return lax.ppermute(block, axis, [(i, (i + step) % count) for i in range(count)])


def attention_kernel(where_ref, owner_ref, offset_ref, global_ref, g_ref, *rest):
    q_refs, pieces = rest[:HEADS], rest[HEADS : HEADS + PIECES]
    out_ref, *gq_refs = rest[HEADS + PIECES : 2 * HEADS + PIECES + 1]
    kv_ref, sems = rest[2 * HEADS + PIECES + 1 :]
    copies = [
        pltpu.make_async_copy(
            piece, kv_ref.at[pl.ds(slot * PIECE_BLOCKS, PIECE_BLOCKS)], sems.at[slot]
        )
        for slot, piece in enumerate(pieces)
    ]
    for copy in copies:
        copy.start()
    my_yh, my_x, my_core = where_ref[0], where_ref[1], where_ref[2]

    def place(block):
        shard, inside = block // NBL, lax.rem(block, NBL)
        yh, x, core = shard // 8, lax.rem(shard // 2, 4), lax.rem(shard, 2)
        piece = jnp.where(core == my_core, 0, 1) + jnp.where(yh == my_yh, 0, 2)
        slot = lax.rem(my_x + 4 - x, 4)
        return piece * PIECE_BLOCKS + slot * NBL + inside

    for copy in copies:
        copy.wait()

    lane = lax.broadcasted_iota(jnp.int32, (1, 2 * BLK), 1)
    total = PIECES * PIECE_BLOCKS
    scale = HD**-0.5

    def one_block(slot, inside):
        x = lax.rem(my_x + 4 - slot, 4)
        block = ((my_yh * 4 + x) * 2 + my_core) * NBL + inside
        left = jnp.maximum(block - 1, 0)
        right = jnp.minimum(block + 1, total - 1)
        named = [left, right, block]
        for r in range(RND):
            named.append(owner_ref[block, r] * NBL + offset_ref[block, r])
        for r in range(GLB):
            named.append(global_ref[0, r])
        spots = [place(b) for b in named]
        kv = jnp.concatenate([kv_ref[s] for s in spots], axis=0)
        k, v = kv[:, :HD], kv[:, HD:]
        allowed = ((lane < BLK) & (block > 0)) | ((lane >= BLK) & (block < total - 1))
        rows = pl.ds(pl.multiple_of(inside * BLK, BLK), BLK)
        q = q_refs[slot][rows, :]
        g = g_ref[x, rows, :]
        s = dot32(q, k, NT) * scale
        s = jnp.concatenate(
            [jnp.where(allowed, s[:, : 2 * BLK], MASKED), s[:, 2 * BLK :]], axis=1
        )
        e = jnp.exp(s - jnp.max(s, axis=1, keepdims=True))
        p = e / jnp.sum(e, axis=1, keepdims=True)
        out_ref[x, rows, :] = dot32(p.astype(jnp.bfloat16), v, NN).astype(jnp.bfloat16)
        gp = dot32(g, v, NT)
        delta = jnp.sum(p * gp, axis=1, keepdims=True)
        ds = (p * (gp - delta) * scale).astype(jnp.bfloat16)
        gq_refs[slot][rows, :] = dot32(ds, k, NN).astype(jnp.bfloat16)

    def step(inside, carry):
        for slot in range(HEADS):
            one_block(slot, inside)
        return carry

    lax.fori_loop(0, NBL, step, 0)


def attention(where, owners, offsets, global_list, grads, queries, pieces):
    rows, width = queries[0].shape
    smem = pl.BlockSpec(memory_space=pltpu.SMEM)
    vmem = pl.BlockSpec(memory_space=pltpu.VMEM)
    return pl.pallas_call(
        attention_kernel,
        out_shape=(jax.ShapeDtypeStruct(grads.shape, jnp.bfloat16),)
        + (jax.ShapeDtypeStruct((rows, width), jnp.bfloat16),) * HEADS,
        in_specs=[smem] * 4
        + [vmem] * (1 + HEADS)
        + [pl.BlockSpec(memory_space=pl.ANY)] * PIECES,
        out_specs=(vmem,) * (1 + HEADS),
        scratch_shapes=[
            pltpu.VMEM((PIECES * PIECE_BLOCKS, BLK, 2 * width), jnp.bfloat16),
            pltpu.SemaphoreType.DMA((PIECES,)),
        ],
        compiler_params=pltpu.CompilerParams(vmem_limit_bytes=24 * 1024 * 1024),
        name="attention",
    )(where, owners, offsets, global_list, grads, *queries, *pieces)


def per_device(
    tokens, query_weight, key_weight, value_weight, cotangent, rand_owner, rand_offset, global_ids
):
    own = tokens[0]
    yh, x, core = lax.axis_index("yh"), lax.axis_index("x"), lax.axis_index("core")
    count, depth = own.shape

    before, after = shifted(own, "x", 1), shifted(own, "x", -1)
    cut = count // 2
    far = jnp.concatenate(
        [shifted(before[:cut], "x", 1), shifted(after[cut:], "x", -1)], axis=0
    )
    token_sets = (own, before, far, after)
    grads = cotangent[0].reshape(count, HEADS, HD).transpose(1, 0, 2)
    grads = lax.all_to_all(grads, "x", 0, 0, tiled=True)

    rows = query_weight.shape[0] // 4
    weight = jnp.concatenate(
        [
            lax.dynamic_slice(w, ((yh * 2 + core) * rows, x * HD), (rows, HD))
            for w in (key_weight, value_weight, query_weight)
        ],
        axis=1,
    )
    weight = spread(weight, "z").reshape(16, rows, 3 * HD)
    weight = spread(weight, ("yh", "yl")).reshape(2, 2, 16, rows, 3 * HD)
    weight = weight.transpose(2, 1, 0, 3, 4)
    partner = shifted(weight, "core", 1)
    weight = jnp.where(
        core == 0,
        jnp.stack([weight, partner], axis=3),
        jnp.stack([partner, weight], axis=3),
    ).reshape(depth, 3 * HD)

    kv = jnp.concatenate(
        [dot32(t, weight[:, : 2 * HD], NN).astype(jnp.bfloat16) for t in token_sets], axis=0
    ).reshape(PIECE_BLOCKS, BLK, 2 * HD)
    queries = [dot32(t, weight[:, 2 * HD :], NN).astype(jnp.bfloat16) for t in token_sets]
    across = shifted(kv, "yh", 1)
    pieces = [kv, shifted(kv, "core", 1), across, shifted(across, "core", 1)]

    where = jnp.stack([yh, x, core]).astype(jnp.int32)
    attended, *grad_queries = attention(
        where, rand_owner[0], rand_offset[0], global_ids, grads, queries, pieces
    )
    attn = lax.all_to_all(attended, "x", 0, 0, tiled=True)
    attn = attn.transpose(1, 0, 2).reshape(count, HEADS * HD)

    partial = sum(dot32(t, g, TN) for t, g in zip(token_sets, grad_queries))
    partial = partial.astype(jnp.bfloat16).reshape(16, 2, 2, 2, rows, HD)
    partial = partial.transpose(2, 1, 3, 0, 4, 5).reshape(8, 16 * rows, HD)
    partial = lax.all_to_all(partial, ("yh", "yl", "core"), 0, 0, tiled=True)
    partial = jnp.sum(partial.astype(jnp.float32), axis=0).astype(jnp.bfloat16)
    partial = lax.all_to_all(partial.reshape(16, rows, HD), "z", 0, 0, tiled=True)
    partial = jnp.sum(partial.astype(jnp.float32), axis=0)
    final = spread(partial, ("yh", "x", "core")).reshape(2, 4, 2, rows, HD)
    query_grad = final.transpose(0, 2, 3, 1, 4).reshape(4 * rows, HEADS * HD)
    return attn[None], query_grad


def solution(mesh):
    fine = Mesh(
        mesh.devices.reshape(2, 4, 2, 16, 2),
        ("yh", "x", "core", "z", "yl"),
        axis_types=(jax.sharding.AxisType.Auto,) * 5,
    )
    ctx, fsdp = ("yh", "x", "core"), ("z", "yl")
    placed = (
        P(fsdp, ctx, None),
        P(fsdp, None),
        P(fsdp, None),
        P(fsdp, None),
        P(fsdp, ctx, None),
        P(fsdp, None, None),
        P(fsdp, None, None),
        P(fsdp, None),
    )
    return jax.shard_map(
        per_device,
        mesh=fine,
        in_specs=placed,
        out_specs=(P(fsdp, ctx, None), P(fsdp, None)),
        check_vma=False,
    )
```

time: 215 us -> 185 us (0.86)
  blocking collectives: 59.4 us -> 36.9 us
  starting transfers between devices: 75.5 us -> 64.4 us
  local copies, waits for them, and re-layouts: 10.7 us -> 16.1 us
    all_to_all x3 -> x2, blocking collectives: 59.4 us -> 36.9 us  [the longest x1 22.8 us: per_device(): lax.all_to_all(partial.reshape(16, rows, HD), 'z', 0, 0, tiled=True)]
    ppermute x12 -> x8, starting transfers between devices: 50.2 us -> 28.8 us  [shifted(): lax.ppermute(block, axis, [(i, (i + step) % count) for i in range(count)])]
    ppermute x12 -> x8, waiting for transfers between devices: 7.92 us -> 27 us  [shifted(): lax.ppermute(block, axis, [(i, (i + step) % count) for i in range(count)])]
    all_to_all x2 -> x3, waiting for transfers between devices: 29.4 us -> 12.7 us  [spread(): lax.all_to_all(jnp.broadcast_to(block[None], (count, *block.shape)), axes...]
    all_to_all x2 -> x3, starting transfers between devices: 11.3 us -> 27.3 us  [spread(): lax.all_to_all(jnp.broadcast_to(block[None], (count, *block.shape)), axes...]
    all_to_all x1 -> x2, starting transfers between devices: 14 us -> 8.23 us  [the longest x1 4.82 us: per_device(): attn = lax.all_to_all(attended, 'x', 0, 0, tiled=True)]
    unnamed x17 -> x34, local copies, waits for them, and re-layouts: 1.69 us -> 7.16 us
    all_to_all x1 -> x2, waiting for transfers between devices: 7.03 us -> 5.51 us  [the longest x1 5.51 us: per_device(): attn = lax.all_to_all(attended, 'x', 0, 0, tiled=True)]
  transfers between devices with their start and end apart: 15 -> 13, of which waited for: 6 -> 7; matrix products, arithmetic and copies ran while one was open for 4% -> 7% of each run, Pallas kernels for 0% -> 0%
where the time goes in v2:
time: 185 us; the launch traced here: 184 us
  starting transfers between devices  64.4 us (35%)
  waiting for transfers between devices  45.3 us (24%)
  blocking collectives  36.9 us (20%)
  local copies, waits for them, and re-layouts  16.1 us (9%)
  Pallas kernels  12.8 us (7%)
  matrix products  4.92 us (3%)
  other arithmetic  2.28 us (1%)
    ppermute x8, starting transfers between devices, shifted(): lax.ppermute(block, axis, [(i, (i + step) % count) for i in range(count)])  28.8 us
    all_to_all x3, starting transfers between devices, spread(): lax.all_to_all(jnp.broadcast_to(block[None], (count, *block.shape)), axes...  27.3 us
    ppermute x8, waiting for transfers between devices, shifted(): lax.ppermute(block, axis, [(i, (i + step) % count) for i in range(count)])  27 us
    all_to_all x1, blocking collectives, per_device(): lax.all_to_all(partial.reshape(16, rows, HD), 'z', 0, 0, tiled=True)  22.8 us
    all_to_all x1, blocking collectives, per_device(): partial = lax.all_to_all(partial, ('yh', 'yl', 'core'), 0, 0, tiled=True)  14 us
    pallas_call x1, Pallas kernels, attention(): pl.pallas_call(attention_kernel, out_shape=(jax.ShapeDtypeStruct(grads.sh...  12.8 us
    all_to_all x3, waiting for transfers between devices, spread(): lax.all_to_all(jnp.broadcast_to(block[None], (count, *block.shape)), axes...  12.7 us
    unnamed x34, local copies, waits for them, and re-layouts  7.16 us
  transfers between devices with their start and end apart: 13, of which 7 were waited for; matrix products, arithmetic and copies ran while one was open for 7% of the time, Pallas kernels for 0%

profile of v2, /device:TPU:1, one launch (start us, length us, event | category | flops | bytes accessed | tf_op | source)
XLA Modules:
  0.0 183.6 jit_solution(11065495153535335129)
XLA Ops:
  3.4 15.7 %all-to-all-start.1 = ((bf16[16,16,384]{2,1,0:T(8,128)(2,1)}), bf16[16,16,384]{2,1,0:T(8,128)(2,1)S(1)}, u32[]{:S(2)}, u32[]{:S(2)}) async-start(bf16[16,16,384]{2,1,0:T(8,128)(2,1)} %broadcast_in_dim.6), calls=%async_computation.1 | async-start | bytes 393216 | tf_op jit(solution)/shard_map/all_to_all | solution.py:30
  19.2 3.1 %collective-permute-start.1 = (bf16[256,2048]{1,0:T(8,128)(2,1)}, bf16[256,2048]{1,0:T(8,128)(2,1)S(1)}, u32[]{:S(2)}, u32[]{:S(2)}) collective-permute-start(bf16[256,2048]{1,0:T(8,128)(2,1)} %bitcast.92), channel_id=1, source_target_pairs={{0,64},{64,128},{128,192},{192,0},{1,65},{65,129},{129,193},{193,1... | collective-permute-start | bytes 3145736 | tf_op jit(solution)/shard_map/ppermute | solution.py:37
  22.3 3.4 %collective-permute-start.3 = (bf16[256,2048]{1,0:T(8,128)(2,1)}, bf16[256,2048]{1,0:T(8,128)(2,1)S(1)}, u32[]{:S(2)}, u32[]{:S(2)}) collective-permute-start(bf16[256,2048]{1,0:T(8,128)(2,1)} %bitcast.93), channel_id=1, source_target_pairs={{0,192},{64,0},{128,64},{192,128},{1,193},{65,1},{129,65},{193,129... | collective-permute-start | bytes 3145736 | tf_op jit(solution)/shard_map/ppermute | solution.py:37
  25.7 6.0 %all-to-all-done.1 = bf16[16,16,384]{2,1,0:T(8,128)(2,1)S(1)} async-done(((bf16[16,16,384]{2,1,0:T(8,128)(2,1)}), bf16[16,16,384]{2,1,0:T(8,128)(2,1)S(1)}, u32[]{:S(2)}, u32[]{:S(2)}) %all-to-all-start.1) | async-done | bytes 196640 | tf_op jit(solution)/shard_map/all_to_all | solution.py:30
  32.7 4.3 %all-to-all-start.2 = ((bf16[4,16,16,384]{3,2,1,0:T(8,128)(2,1)}), bf16[4,16,16,384]{3,2,1,0:T(8,128)(2,1)S(1)}, u32[]{:S(2)}, u32[]{:S(2)}) async-start(bf16[4,16,16,384]{3,2,1,0:T(8,128)(2,1)} %broadcast_in_dim.7), calls=%async_computation.2 | async-start | bytes 1572864 | tf_op jit(solution)/shard_map/all_to_all | solution.py:30
  37.0 9.2 %collective-permute-done.1 = bf16[256,2048]{1,0:T(8,128)(2,1)S(1)} collective-permute-done((bf16[256,2048]{1,0:T(8,128)(2,1)}, bf16[256,2048]{1,0:T(8,128)(2,1)S(1)}, u32[]{:S(2)}, u32[]{:S(2)}) %collective-permute-start.1) | collective-permute-done | bytes 1048608 | tf_op jit(solution)/shard_map/ppermute | solution.py:37
  47.1 2.0 %collective-permute-start.2 = (bf16[128,2048]{1,0:T(8,128)(2,1)}, bf16[128,2048]{1,0:T(8,128)(2,1)}, u32[]{:S(2)}, u32[]{:S(2)}) collective-permute-start(bf16[128,2048]{1,0:T(8,128)(2,1)} %slice.23), channel_id=1, source_target_pairs={{0,64},{64,128},{128,192},{192,0},{1,65},{65,129},{129,193},{193,1... | collective-permute-start | bytes 1572872 | tf_op jit(solution)/shard_map/ppermute | solution.py:37
  49.1 4.3 %collective-permute-start = (bf16[16,2,2,16,384]{4,3,0,1,2:T(8,128)(2,1)S(1)}, bf16[16,2,2,16,384]{4,3,0,1,2:T(8,128)(2,1)}, u32[]{:S(2)}, u32[]{:S(2)}) collective-permute-start(bf16[16,2,2,16,384]{4,3,0,1,2:T(8,128)(2,1)S(1)} %bitcast.77), channel_id=1, source_target_pairs={{0,32},{32,0},{1,33},{33,1},{2,34},{34,2},{3,35},{35,3},{4,36},{36... | collective-permute-start | bytes 2359304 | tf_op jit(solution)/shard_map/ppermute | solution.py:37
  54.4 4.4 %collective-permute-start.4 = (bf16[128,2048]{1,0:T(8,128)(2,1)}, bf16[128,2048]{1,0:T(8,128)(2,1)}, u32[]{:S(2)}, u32[]{:S(2)}) collective-permute-start(bf16[128,2048]{1,0:T(8,128)(2,1)} %slice.24), channel_id=1, source_target_pairs={{0,192},{64,0},{128,64},{192,128},{1,193},{65,1},{129,65},{193,129... | collective-permute-start | bytes 1572872 | tf_op jit(solution)/shard_map/ppermute | solution.py:37
  59.8 3.4 %all-to-all-start = ((bf16[4,256,128]{2,1,0:T(8,128)(2,1)}), bf16[4,256,128]{2,1,0:T(8,128)(2,1)S(1)}, u32[]{:S(2)}, u32[]{:S(2)}) async-start(bf16[4,256,128]{2,1,0:T(8,128)(2,1)} %bitcast.6), calls=%async_computation | async-start | bytes 524288 | tf_op jit(solution)/shard_map/all_to_all | solution.py:140
  63.5 1.1 constant_dynamic-update-slice_fusion.1
  64.6 5.8 %collective-permute-done.4 = bf16[128,2048]{1,0:T(8,128)(2,1)} collective-permute-done((bf16[128,2048]{1,0:T(8,128)(2,1)}, bf16[128,2048]{1,0:T(8,128)(2,1)}, u32[]{:S(2)}, u32[]{:S(2)}) %collective-permute-start.4) | collective-permute-done | bytes 524320 | tf_op jit(solution)/shard_map/ppermute | solution.py:37
  71.6 2.1 %maximum_select_fusion = bf16[16,2,2,2,16,384]{5,4,0,1,2,3:T(8,128)(2,1)S(1)} fusion(bf16[16,2,2,1,16,384]{5,4,0,1,2,3:T(8,128)(2,1)} %bitcast.11, bf16[16,2,2,1,16,384]{5,4,0,1,2,3:T(8,128)(2,1)S(1)} %bitcast.78, pred[]{:T(512)S(6)} %eq.3), kind=kLoop, calls=%fused_computation.6 | loop fusion | flops 2359296 | bytes 3145729 | tf_op jit(solution)/shard_map/jit(_where)/select_n | solution.py:154
  78.3 3.3 %collective-permute-start.5 = (bf16[16,64,256]{2,1,0:T(8,128)(2,1)S(1)}, bf16[16,64,256]{2,1,0:T(8,128)(2,1)S(1)}, u32[]{:S(2)}, u32[]{:S(2)}) collective-permute-start(bf16[16,64,256]{2,1,0:T(8,128)(2,1)S(1)} %bitcast.72), channel_id=1, source_target_pairs={{0,32},{32,0},{1,33},{33,1},{2,34},{34,2},{3,35},{35,3},{4,36},{36... | collective-permute-start | bytes 1572872 | tf_op jit(solution)/shard_map/ppermute | solution.py:37
  81.6 5.8 %collective-permute-start.6 = (bf16[16,64,256]{2,1,0:T(8,128)(2,1)S(1)}, bf16[16,64,256]{2,1,0:T(8,128)(2,1)S(1)}, u32[]{:S(2)}, u32[]{:S(2)}) collective-permute-start(bf16[16,64,256]{2,1,0:T(8,128)(2,1)S(1)} %bitcast.73), channel_id=1, source_target_pairs={{0,256},{256,0},{1,257},{257,1},{2,258},{258,2},{3,259},{259,3},{4... | collective-permute-start | bytes 1572872 | tf_op jit(solution)/shard_map/ppermute | solution.py:37
  88.2 11.4 %collective-permute-done.6.rest_6_ = bf16[16,64,256]{2,1,0:T(8,128)(2,1)S(1)} collective-permute-done((bf16[16,64,256]{2,1,0:T(8,128)(2,1)S(1)}, bf16[16,64,256]{2,1,0:T(8,128)(2,1)S(1)}, u32[]{:S(2)}, u32[]{:S(2)}) %collective-permute-start.6) | collective-permute-done | bytes 524320 | tf_op jit(solution)/shard_map/ppermute | solution.py:37
  99.6 2.5 %collective-permute-start.7 = (bf16[16,64,256]{2,1,0:T(8,128)(2,1)S(1)}, bf16[16,64,256]{2,1,0:T(8,128)(2,1)S(1)}, u32[]{:S(2)}, u32[]{:S(2)}) collective-permute-start(bf16[16,64,256]{2,1,0:T(8,128)(2,1)S(1)} %collective-permute-done.6.rest_6_), channel_id=1, source_target_pairs={{0,32},{32,0},{1,33},{33,1},{2,34},{34,2},{3,35},{35,3},{4,36},{36... | collective-permute-start | bytes 1572872 | tf_op jit(solution)/shard_map/ppermute | solution.py:37
  103.6 12.8 %attention.1 = (bf16[4,256,128]{2,1,0:T(8,128)(2,1)}, bf16[256,128]{1,0:T(8,128)(2,1)S(1)}, bf16[256,128]{1,0:T(8,128)(2,1)S(1)}, bf16[256,128]{1,0:T(8,128)(2,1)S(1)}, bf16[256,128]{1,0:T(8,128)(2,1)S(1)}) custom-call(s32[3]{0:T(128)S(1)} %pad_add_fusion.where_ref, s32[64,3]{1,0:T(8,128)S(1)} %bitcast.75, s32[64,3]{1,0:T(8,128)S(1)} %bitcast.76, ...), custom_call_target="tpu_custom_call" | custom-call | tf_op jit(solution)/shard_map/attention/pallas_call | solution.py:109
  120.0 14.0 %all_to_all.35 = bf16[8,256,128]{2,1,0:T(8,128)(2,1)S(1)} all-to-all(bf16[8,256,128]{2,1,0:T(8,128)(2,1)S(1)} %bitcast.80), channel_id=1, replica_groups=mesh['yh'=2,'x'=4,'core'=2,'z'=16,'yl'=2] {'yh','yl','core'}, dimensions={0} | all-to-all | bytes 1048576 | tf_op jit(solution)/shard_map/all_to_all | solution.py:177
  134.1 22.8 %all_to_all.36 = bf16[16,16,128]{2,1,0:T(8,128)(2,1)S(1)} all-to-all(bf16[16,16,128]{2,1,0:T(8,128)(2,1)S(1)} %bitcast.96), channel_id=1, replica_groups=mesh['yh'=2,'x'=4,'core'=2,'z'=16,'yl'=2] {'z'}, dimensions={0} | all-to-all | bytes 131072 | tf_op jit(solution)/shard_map/all_to_all | solution.py:179
  156.9 4.8 %all-to-all-start.3 = ((bf16[4,256,128]{2,1,0:T(8,128)(2,1)}), bf16[4,256,128]{2,1,0:T(8,128)(2,1)S(1)}, u32[]{:S(2)}, u32[]{:S(2)}) async-start(bf16[4,256,128]{2,1,0:T(8,128)(2,1)} %get-tuple-element.7), calls=%async_computation.3 | async-start | bytes 524288 | tf_op jit(solution)/shard_map/all_to_all | solution.py:171
  161.8 5.5 %all-to-all-done.3 = bf16[4,256,128]{2,1,0:T(8,128)(2,1)S(1)} async-done(((bf16[4,256,128]{2,1,0:T(8,128)(2,1)}), bf16[4,256,128]{2,1,0:T(8,128)(2,1)S(1)}, u32[]{:S(2)}, u32[]{:S(2)}) %all-to-all-start.3) | async-done | bytes 262176 | tf_op jit(solution)/shard_map/all_to_all | solution.py:171
  167.9 7.2 %all-to-all-start.6 = ((f32[16,16,128]{2,1,0:T(8,128)}), f32[16,16,128]{2,1,0:T(8,128)S(1)}, u32[]{:S(2)}, u32[]{:S(2)}) async-start(f32[16,16,128]{2,1,0:T(8,128)} %broadcast_in_dim.8), calls=%async_computation.6 | async-start | bytes 262144 | tf_op jit(solution)/shard_map/all_to_all | solution.py:30
  176.2 6.7 %all-to-all-done.6 = f32[16,16,128]{2,1,0:T(8,128)S(1)} async-done(((f32[16,16,128]{2,1,0:T(8,128)}), f32[16,16,128]{2,1,0:T(8,128)S(1)}, u32[]{:S(2)}, u32[]{:S(2)}) %all-to-all-start.6) | async-done | bytes 131104 | tf_op jit(solution)/shard_map/all_to_all | solution.py:30
  (72 shorter events, 20.7 us)
Async XLA Ops:
  3.4 28.3 %all-to-all-start.1 = ((bf16[16,16,384]{2,1,0:T(8,128)(2,1)}), bf16[16,16,384]{2,1,0:T(8,128)(2,1)S(1)}, u32[]{:S(2)}, u32[]{:S(2)}) async-start(bf16[16,16,384]{2,1,0:T(8,128)(2,1)} %broadcast_in_dim.6), calls=%async_computation.1 | async-start | bytes 393216 | tf_op jit(solution)/shard_map/all_to_all | solution.py:30
  19.2 27.0 %collective-permute-start.1 = (bf16[256,2048]{1,0:T(8,128)(2,1)}, bf16[256,2048]{1,0:T(8,128)(2,1)S(1)}, u32[]{:S(2)}, u32[]{:S(2)}) collective-permute-start(bf16[256,2048]{1,0:T(8,128)(2,1)} %bitcast.92), channel_id=1, source_target_pairs={{0,64},{64,128},{128,192},{192,0},{1,65},{65,129},{129,193},{193,1... | collective-permute-start | bytes 3145736 | tf_op jit(solution)/shard_map/ppermute | solution.py:37
  22.3 31.2 %collective-permute-start.3 = (bf16[256,2048]{1,0:T(8,128)(2,1)}, bf16[256,2048]{1,0:T(8,128)(2,1)S(1)}, u32[]{:S(2)}, u32[]{:S(2)}) collective-permute-start(bf16[256,2048]{1,0:T(8,128)(2,1)} %bitcast.93), channel_id=1, source_target_pairs={{0,192},{64,0},{128,64},{192,128},{1,193},{65,1},{129,65},{193,129... | collective-permute-start | bytes 3145736 | tf_op jit(solution)/shard_map/ppermute | solution.py:37
  32.7 26.2 %copy-start.11 = (bf16[1,256,512]{2,1,0:T(8,128)(2,1)S(1)}, bf16[1,256,512]{2,1,0:T(8,128)(2,1)}, u32[]{:S(2)}) copy-start(bf16[1,256,512]{2,1,0:T(8,128)(2,1)} %param.12) | copy-start | bytes 786436
  32.7 16.5 %all-to-all-start.2 = ((bf16[4,16,16,384]{3,2,1,0:T(8,128)(2,1)}), bf16[4,16,16,384]{3,2,1,0:T(8,128)(2,1)S(1)}, u32[]{:S(2)}, u32[]{:S(2)}) async-start(bf16[4,16,16,384]{3,2,1,0:T(8,128)(2,1)} %broadcast_in_dim.7), calls=%async_computation.2 | async-start | bytes 1572864 | tf_op jit(solution)/shard_map/all_to_all | solution.py:30
  46.2 13.6 %copy-start.1 = (bf16[256,2048]{1,0:T(8,128)(2,1)}, bf16[256,2048]{1,0:T(8,128)(2,1)S(1)}, u32[]{:S(2)}) copy-start(bf16[256,2048]{1,0:T(8,128)(2,1)S(1)} %collective-permute-done.1) | copy-start | bytes 3145732
  47.1 16.2 %copy-start.12 = (s32[1,64,3]{1,0,2:T(1,128)S(1)}, s32[1,64,3]{1,0,2:T(1,128)}, u32[]{:S(2)}) copy-start(s32[1,64,3]{1,0,2:T(1,128)} %param.13) | copy-start | bytes 2308
  47.1 16.3 %copy-start.13 = (s32[1,64,3]{1,0,2:T(1,128)S(1)}, s32[1,64,3]{1,0,2:T(1,128)}, u32[]{:S(2)}) copy-start(s32[1,64,3]{1,0,2:T(1,128)} %param.14) | copy-start | bytes 2308
  47.1 16.4 %collective-permute-start.2 = (bf16[128,2048]{1,0:T(8,128)(2,1)}, bf16[128,2048]{1,0:T(8,128)(2,1)}, u32[]{:S(2)}, u32[]{:S(2)}) collective-permute-start(bf16[128,2048]{1,0:T(8,128)(2,1)} %slice.23), channel_id=1, source_target_pairs={{0,64},{64,128},{128,192},{192,0},{1,65},{65,129},{129,193},{193,1... | collective-permute-start | bytes 1572872 | tf_op jit(solution)/shard_map/ppermute | solution.py:37
  49.1 22.4 %collective-permute-start = (bf16[16,2,2,16,384]{4,3,0,1,2:T(8,128)(2,1)S(1)}, bf16[16,2,2,16,384]{4,3,0,1,2:T(8,128)(2,1)}, u32[]{:S(2)}, u32[]{:S(2)}) collective-permute-start(bf16[16,2,2,16,384]{4,3,0,1,2:T(8,128)(2,1)S(1)} %bitcast.77), channel_id=1, source_target_pairs={{0,32},{32,0},{1,33},{33,1},{2,34},{34,2},{3,35},{35,3},{4,36},{36... | collective-permute-start | bytes 2359304 | tf_op jit(solution)/shard_map/ppermute | solution.py:37
  53.5 11.1 %copy-start.4 = (bf16[256,2048]{1,0:T(8,128)(2,1)}, bf16[256,2048]{1,0:T(8,128)(2,1)S(1)}, u32[]{:S(2)}) copy-start(bf16[256,2048]{1,0:T(8,128)(2,1)S(1)} %collective-permute-done.3) | copy-start | bytes 3145732
  54.4 16.0 %collective-permute-start.4 = (bf16[128,2048]{1,0:T(8,128)(2,1)}, bf16[128,2048]{1,0:T(8,128)(2,1)}, u32[]{:S(2)}, u32[]{:S(2)}) collective-permute-start(bf16[128,2048]{1,0:T(8,128)(2,1)} %slice.24), channel_id=1, source_target_pairs={{0,192},{64,0},{128,64},{192,128},{1,193},{65,1},{129,65},{193,129... | collective-permute-start | bytes 1572872 | tf_op jit(solution)/shard_map/ppermute | solution.py:37
  59.8 43.2 %all-to-all-start = ((bf16[4,256,128]{2,1,0:T(8,128)(2,1)}), bf16[4,256,128]{2,1,0:T(8,128)(2,1)S(1)}, u32[]{:S(2)}, u32[]{:S(2)}) async-start(bf16[4,256,128]{2,1,0:T(8,128)(2,1)} %bitcast.6), calls=%async_computation | async-start | bytes 524288 | tf_op jit(solution)/shard_map/all_to_all | solution.py:140
  71.5 16.2 %copy-start.7 = (bf16[256,2048]{1,0:T(8,128)(2,1)}, bf16[256,2048]{1,0:T(8,128)(2,1)S(1)}, u32[]{:S(2)}) copy-start(bf16[256,2048]{1,0:T(8,128)(2,1)S(1)} %constant_dynamic-update-slice_fusion) | copy-start | bytes 3145732
  73.6 1.2 copy-start.9
  78.3 24.8 %collective-permute-start.5 = (bf16[16,64,256]{2,1,0:T(8,128)(2,1)S(1)}, bf16[16,64,256]{2,1,0:T(8,128)(2,1)S(1)}, u32[]{:S(2)}, u32[]{:S(2)}) collective-permute-start(bf16[16,64,256]{2,1,0:T(8,128)(2,1)S(1)} %bitcast.72), channel_id=1, source_target_pairs={{0,32},{32,0},{1,33},{33,1},{2,34},{34,2},{3,35},{35,3},{4,36},{36... | collective-permute-start | bytes 1572872 | tf_op jit(solution)/shard_map/ppermute | solution.py:37
  81.6 18.1 %collective-permute-start.6 = (bf16[16,64,256]{2,1,0:T(8,128)(2,1)S(1)}, bf16[16,64,256]{2,1,0:T(8,128)(2,1)S(1)}, u32[]{:S(2)}, u32[]{:S(2)}) collective-permute-start(bf16[16,64,256]{2,1,0:T(8,128)(2,1)S(1)} %bitcast.73), channel_id=1, source_target_pairs={{0,256},{256,0},{1,257},{257,1},{2,258},{258,2},{3,259},{259,3},{4... | collective-permute-start | bytes 1572872 | tf_op jit(solution)/shard_map/ppermute | solution.py:37
  88.2 15.4 %copy-start = (s32[1,2]{1,0:T(1,128)S(1)}, s32[1,2]{1,0:T(1,128)}, u32[]{:S(2)}) copy-start(s32[1,2]{1,0:T(1,128)} %global_ref.1) | copy-start | bytes 28
  99.6 4.0 %collective-permute-start.7 = (bf16[16,64,256]{2,1,0:T(8,128)(2,1)S(1)}, bf16[16,64,256]{2,1,0:T(8,128)(2,1)S(1)}, u32[]{:S(2)}, u32[]{:S(2)}) collective-permute-start(bf16[16,64,256]{2,1,0:T(8,128)(2,1)S(1)} %collective-permute-done.6.rest_6_), channel_id=1, source_target_pairs={{0,32},{32,0},{1,33},{33,1},{2,34},{34,2},{3,35},{35,3},{4,36},{36... | collective-permute-start | bytes 1572872 | tf_op jit(solution)/shard_map/ppermute | solution.py:37
  103.0 13.4 %copy-start.8 = (bf16[256,2048]{1,0:T(8,128)(2,1)S(1)}, bf16[256,2048]{1,0:T(8,128)(2,1)}, u32[]{:S(2)}) copy-start(bf16[256,2048]{1,0:T(8,128)(2,1)} %copy-done.7) | copy-start | bytes 3145732
  116.8 1.3 copy-start.3
  118.0 1.3 copy-start.10
  156.9 10.3 %all-to-all-start.3 = ((bf16[4,256,128]{2,1,0:T(8,128)(2,1)}), bf16[4,256,128]{2,1,0:T(8,128)(2,1)S(1)}, u32[]{:S(2)}, u32[]{:S(2)}) async-start(bf16[4,256,128]{2,1,0:T(8,128)(2,1)} %get-tuple-element.7), calls=%async_computation.3 | async-start | bytes 524288 | tf_op jit(solution)/shard_map/all_to_all | solution.py:171
  167.9 14.9 %all-to-all-start.6 = ((f32[16,16,128]{2,1,0:T(8,128)}), f32[16,16,128]{2,1,0:T(8,128)S(1)}, u32[]{:S(2)}, u32[]{:S(2)}) async-start(f32[16,16,128]{2,1,0:T(8,128)} %broadcast_in_dim.8), calls=%async_computation.6 | async-start | bytes 262144 | tf_op jit(solution)/shard_map/all_to_all | solution.py:30
  (3 other events, 3.7 us)

commit v3 on v2

v3 whole, which is shorter than its diff:
```python
import jax
import jax.numpy as jnp
from jax import lax
from jax.experimental import pallas as pl
from jax.experimental.pallas import tpu as pltpu
from jax.sharding import Mesh
from jax.sharding import PartitionSpec as P

HD = 128
BLK = 64
RND = 3
GLB = 2
NBL = 4
PIECE_BLOCKS = 16
PIECES = 4
HEADS = 4
MASKED = -1e30

NT = (((1,), (1,)), ((), ()))
NN = (((1,), (0,)), ((), ()))
TN = (((0,), (0,)), ((), ()))


def dot32(a, b, dims):
    return lax.dot_general(a, b, dims, preferred_element_type=jnp.float32)


def spread(block, axes):
    count = lax.axis_size(axes)
    return lax.all_to_all(
        jnp.broadcast_to(block[None], (count, *block.shape)), axes, 0, 0, tiled=True
    )


def shifted(block, axis, step):
    count = lax.axis_size(axis)
    return lax.ppermute(block, axis, [(i, (i + step) % count) for i in range(count)])


def slice_kernel(where_ref, key_ref, value_ref, query_ref, out_ref):
    count, rows, _ = out_ref.shape
    start = pl.multiple_of((where_ref[0] * 2 + where_ref[2]) * rows, rows)
    col = pl.multiple_of(where_ref[1] * HD, HD)
    for i, ref in enumerate((key_ref, value_ref, query_ref)):
        part = ref[pl.ds(start, rows), pl.ds(col, HD)]
        for copy in range(count):
            out_ref[copy, :, i * HD : (i + 1) * HD] = part


def project_kernel(where_ref, mine_ref, theirs_ref, *rest):
    token_refs, (q_ref, kv_ref, w_ref) = rest[:-3], rest[-3:]
    core = where_ref[2]
    _, _, depth, rows, width = mine_ref.shape

    def assemble(z, carry):
        for yl in range(2):
            for yh in range(2):
                base = (z * 2 + yl) * 4 * rows + yh * 2 * rows
                here = pl.multiple_of(base + core * rows, rows)
                there = pl.multiple_of(base + (1 - core) * rows, rows)
                w_ref[pl.ds(here, rows), :] = mine_ref[yh, yl, z]
                w_ref[pl.ds(there, rows), :] = theirs_ref[yh, yl, z]
        return carry

    lax.fori_loop(0, depth, assemble, 0)
    for slot, group in token_groups(token_refs):
        tokens = jnp.concatenate([ref[...] for ref in group], axis=0)
        size = tokens.shape[0]
        out = dot32(tokens, w_ref[...], NN).astype(jnp.bfloat16)
        kv_ref[slot * NBL : (slot + 1) * NBL] = out[:, : 2 * HD].reshape(NBL, BLK, 2 * HD)
        q_ref[slot * size : (slot + 1) * size, :] = out[:, 2 * HD :]


def token_groups(refs):
    own, before, after, low_far, high_far = refs
    return [(0, (own,)), (1, (before,)), (3, (after,)), (2, (low_far, high_far))]


def project(where, mine, theirs, token_sets):
    count, depth = token_sets[0].shape
    total = count * HEADS
    vmem = pl.BlockSpec(memory_space=pltpu.VMEM)
    return pl.pallas_call(
        project_kernel,
        out_shape=(
            jax.ShapeDtypeStruct((total, HD), jnp.bfloat16),
            jax.ShapeDtypeStruct((PIECE_BLOCKS, BLK, 2 * HD), jnp.bfloat16),
        ),
        in_specs=[pl.BlockSpec(memory_space=pltpu.SMEM)] + [vmem] * (2 + len(token_sets)),
        out_specs=(vmem, vmem),
        scratch_shapes=[pltpu.VMEM((depth, 3 * HD), jnp.bfloat16)],
        compiler_params=pltpu.CompilerParams(vmem_limit_bytes=24 * 1024 * 1024),
        name="project",
    )(where, mine, theirs, *token_sets)


def attention_kernel(where_ref, owner_ref, offset_ref, global_ref, *rest):
    given, pieces, token_refs = rest[:2], rest[2 : 2 + PIECES], rest[2 + PIECES : -8]
    out_ref, part_ref, kv_ref, g_ref, q_ref, gq_ref, t_ref, sems = rest[-8:]
    pairs = [
        (piece, kv_ref.at[pl.ds(slot * PIECE_BLOCKS, PIECE_BLOCKS)])
        for slot, piece in enumerate(pieces)
    ]
    pairs += list(zip(given, (g_ref, q_ref)))
    first = len(pairs)
    for slot, group in token_groups(token_refs):
        size = group[0].shape[0]
        pairs += [
            (ref, t_ref.at[slot, pl.ds(i * size, size)]) for i, ref in enumerate(group)
        ]
    copies = [
        pltpu.make_async_copy(source, target, sems.at[i])
        for i, (source, target) in enumerate(pairs)
    ]
    for copy in copies:
        copy.start()
    copies, later = copies[:first], copies[first:]
    my_yh, my_x, my_core = where_ref[0], where_ref[1], where_ref[2]

    def place(block):
        shard, inside = block // NBL, lax.rem(block, NBL)
        yh, x, core = shard // 8, lax.rem(shard // 2, 4), lax.rem(shard, 2)
        piece = jnp.where(core == my_core, 0, 1) + jnp.where(yh == my_yh, 0, 2)
        slot = lax.rem(my_x + 4 - x, 4)
        return piece * PIECE_BLOCKS + slot * NBL + inside

    for copy in copies:
        copy.wait()

    lane = lax.broadcasted_iota(jnp.int32, (1, 2 * BLK), 1)
    total = PIECES * PIECE_BLOCKS
    scale = HD**-0.5

    def step(inside, carry):
        rows = pl.ds(pl.multiple_of(inside * BLK, BLK), BLK)
        ks, vs, ss, gps = [], [], [], []
        for slot in range(HEADS):
            x = lax.rem(my_x + 4 - slot, 4)
            block = ((my_yh * 4 + x) * 2 + my_core) * NBL + inside
            left = jnp.maximum(block - 1, 0)
            right = jnp.minimum(block + 1, total - 1)
            named = [left, right, block]
            for r in range(RND):
                named.append(owner_ref[block, r] * NBL + offset_ref[block, r])
            for r in range(GLB):
                named.append(global_ref[0, r])
            kv = jnp.concatenate([kv_ref[place(b)] for b in named], axis=0)
            k, v = kv[:, :HD], kv[:, HD:]
            allowed = ((lane < BLK) & (block > 0)) | ((lane >= BLK) & (block < total - 1))
            place_rows = pl.ds(pl.multiple_of(slot * NBL * BLK + inside * BLK, BLK), BLK)
            s = dot32(q_ref[place_rows, :], k, NT) * scale
            s = jnp.concatenate(
                [jnp.where(allowed, s[:, : 2 * BLK], MASKED), s[:, 2 * BLK :]], axis=1
            )
            ks.append(k)
            vs.append(v)
            ss.append(s)
            gps.append(dot32(g_ref[x, rows, :], v, NT))
        for slot in range(HEADS):
            s, gp = ss[slot], gps[slot]
            e = jnp.exp(s - jnp.max(s, axis=1, keepdims=True))
            p = e * (1.0 / jnp.sum(e, axis=1, keepdims=True))
            delta = jnp.sum(p * gp, axis=1, keepdims=True)
            ds = (p * (gp - delta) * scale).astype(jnp.bfloat16)
            out_ref[slot, rows, :] = dot32(p.astype(jnp.bfloat16), vs[slot], NN).astype(
                jnp.bfloat16
            )
            gq_ref[slot, rows, :] = dot32(ds, ks[slot], NN).astype(jnp.bfloat16)
        return carry

    lax.fori_loop(0, NBL, step, 0)

    acc = None
    for copy in later:
        copy.wait()
    for slot in range(HEADS):
        term = dot32(gq_ref[slot], t_ref[slot], TN)
        acc = term if acc is None else acc + term
    rows = part_ref.shape[2]
    for z in range(16):
        turned = acc[:, z * HD : (z + 1) * HD].T.astype(jnp.bfloat16)
        for yl in range(2):
            for q in range(4):
                at = yl * 4 * rows + q * rows
                part_ref[((q // 2) * 2 + yl) * 2 + q % 2, z] = turned[at : at + rows]


def attention(where, owners, offsets, global_list, grads, queries, pieces, token_sets):
    smem = pl.BlockSpec(memory_space=pltpu.SMEM)
    vmem = pl.BlockSpec(memory_space=pltpu.VMEM)
    return pl.pallas_call(
        attention_kernel,
        out_shape=(
            jax.ShapeDtypeStruct(grads.shape, jnp.bfloat16),
            jax.ShapeDtypeStruct((8, 16, 16, HD), jnp.bfloat16),
        ),
        in_specs=[smem] * 4
        + [pl.BlockSpec(memory_space=pl.ANY)] * (2 + PIECES + len(token_sets)),
        out_specs=(vmem, vmem),
        scratch_shapes=[
            pltpu.VMEM((PIECES * PIECE_BLOCKS, BLK, 2 * HD), jnp.bfloat16),
            pltpu.VMEM(grads.shape, jnp.bfloat16),
            pltpu.VMEM(queries.shape, jnp.bfloat16),
            pltpu.VMEM(grads.shape, jnp.bfloat16),
            pltpu.VMEM((HEADS, *token_sets[0].shape), jnp.bfloat16),
            pltpu.SemaphoreType.DMA((2 + PIECES + len(token_sets),)),
        ],
        compiler_params=pltpu.CompilerParams(vmem_limit_bytes=32 * 1024 * 1024),
        name="attention",
    )(where, owners, offsets, global_list, grads, queries, *pieces, *token_sets)


def merge_kernel(where_ref, *refs):
    out_ref = refs[-1]
    for slot, ref in enumerate(refs[:-1]):
        head = lax.rem(where_ref[1] + slot, HEADS)
        out_ref[:, pl.ds(pl.multiple_of(head * HD, HD), HD)] = ref[...]


def per_device(
    tokens, query_weight, key_weight, value_weight, cotangent, rand_owner, rand_offset, global_ids
):
    own = tokens[0]
    count, depth = own.shape
    where = jnp.stack(
        [lax.axis_index("yh"), lax.axis_index("x"), lax.axis_index("core")]
    ).astype(jnp.int32)
    smem = pl.BlockSpec(memory_space=pltpu.SMEM)
    vmem = pl.BlockSpec(memory_space=pltpu.VMEM)

    rows = query_weight.shape[0] // 4
    weight = pl.pallas_call(
        slice_kernel,
        out_shape=jax.ShapeDtypeStruct((16, rows, 3 * HD), jnp.bfloat16),
        in_specs=[smem] + [vmem] * 3,
        out_specs=vmem,
        name="slice",
    )(where, key_weight, value_weight, query_weight)
    weight = lax.all_to_all(weight, "z", 0, 0, tiled=True)
    weight = spread(weight, ("yh", "yl")).reshape(2, 2, 16, rows, 3 * HD)
    partner = shifted(weight, "core", 1)

    cut = count // 2
    before, after = shifted(own, "x", 1), shifted(own, "x", -1)
    low_far, high_far = shifted(before[:cut], "x", 1), shifted(after[cut:], "x", -1)
    token_sets = (own, before, after, low_far, high_far)
    grads = cotangent[0].reshape(count, HEADS, HD).transpose(1, 0, 2)
    grads = lax.all_to_all(grads, "x", 0, 0, tiled=True)

    queries, kv = project(where, weight, partner, token_sets)
    across = shifted(kv, "yh", 1)
    across, grads = lax.optimization_barrier((across, grads))
    pieces = [kv, shifted(kv, "core", 1), across, shifted(across, "core", 1)]

    attended, partial = attention(
        where, rand_owner[0], rand_offset[0], global_ids, grads, queries, pieces, token_sets
    )
    returned = [attended[0]] + [shifted(attended[s], "x", -s) for s in range(1, HEADS)]
    attn = pl.pallas_call(
        merge_kernel,
        out_shape=jax.ShapeDtypeStruct((count, HEADS * HD), jnp.bfloat16),
        in_specs=[smem] + [vmem] * HEADS,
        out_specs=vmem,
        name="merge",
    )(where, *returned)

    partial = lax.all_to_all(partial, ("yh", "yl", "core"), 0, 0, tiled=True)
    partial = jnp.sum(partial.astype(jnp.float32), axis=0).astype(jnp.bfloat16)
    partial, attn = lax.optimization_barrier((partial, attn))
    partial = lax.all_to_all(partial, "z", 0, 0, tiled=True)
    partial = jnp.sum(partial.astype(jnp.float32), axis=0)
    final = spread(partial, ("yh", "x", "core")).reshape(2, 4, 2, rows, HD)
    query_grad = final.transpose(0, 2, 3, 1, 4).reshape(4 * rows, HEADS * HD)
    return attn[None], query_grad


def solution(mesh):
    fine = Mesh(
        mesh.devices.reshape(2, 4, 2, 16, 2),
        ("yh", "x", "core", "z", "yl"),
        axis_types=(jax.sharding.AxisType.Auto,) * 5,
    )
    ctx, fsdp = ("yh", "x", "core"), ("z", "yl")
    placed = (
        P(fsdp, ctx, None),
        P(fsdp, None),
        P(fsdp, None),
        P(fsdp, None),
        P(fsdp, ctx, None),
        P(fsdp, None, None),
        P(fsdp, None, None),
        P(fsdp, None),
    )
    return jax.shard_map(
        per_device,
        mesh=fine,
        in_specs=placed,
        out_specs=(P(fsdp, ctx, None), P(fsdp, None)),
        check_vma=False,
    )
```

time: 185 us -> 168 us (0.908)
  waiting for transfers between devices: 45.3 us -> 29.2 us
  blocking collectives: 36.9 us -> 48.1 us
  local copies, waits for them, and re-layouts: 16.1 us -> 10.2 us
  matrix products: 4.92 us -> 0 us
  Pallas kernels: 12.8 us -> 15.8 us
  starting transfers between devices: 64.4 us -> 62.2 us
    all_to_all x4 -> x2, starting transfers between devices: 32.1 us -> 19.6 us  [the longest x1 15.7 us: per_device(): weight = lax.all_to_all(weight, 'z', 0, 0, tiled=True)]
    all_to_all x4 -> x2, waiting for transfers between devices: 18.2 us -> 6.23 us  [the longest x1 6.23 us: per_device(): weight = lax.all_to_all(weight, 'z', 0, 0, tiled=True)]
    all_to_all x2 -> x3, blocking collectives: 36.9 us -> 48.1 us  [the longest x2 29.3 us: spread(): lax.all_to_all(jnp.broadcast_to(block[None], (count, *block.shape)), axes...]
    ppermute x8 -> x11, starting transfers between devices: 28.8 us -> 39 us  [shifted(): lax.ppermute(block, axis, [(i, (i + step) % count) for i in range(count)])]
    pallas_call x0 -> x3, Pallas kernels: none -> 7.33 us  [the longest x1 3.99 us: project(): pl.pallas_call(project_kernel, out_shape=(jax.ShapeDtypeStruct((total, HD...]
    ppermute x8 -> x11, waiting for transfers between devices: 27 us -> 20.4 us  [shifted(): lax.ppermute(block, axis, [(i, (i + step) % count) for i in range(count)])]
    dot_general x12 -> x0, matrix products: 4.92 us -> none  [dot32(): return lax.dot_general(a, b, dims, preferred_element_type=jnp.float32)]
    pallas_call x1, Pallas kernels: 12.8 us -> 8.51 us  [attention(): pl.pallas_call(attention_kernel, out_shape=(jax.ShapeDtypeStruct(grads.sh...]
  transfers between devices with their start and end apart: 13 -> 14, of which waited for: 7 -> 8; matrix products, arithmetic and copies ran while one was open for 7% -> 2% of each run, Pallas kernels for 0% -> 1%
where the time goes in v3:
time: 168 us; the launch traced here: 167 us
  starting transfers between devices  62.2 us (37%)
  blocking collectives  48.1 us (29%)
  waiting for transfers between devices  29.2 us (17%)
  Pallas kernels  15.8 us (9%)
  local copies, waits for them, and re-layouts  10.2 us (6%)
    ppermute x11, starting transfers between devices, shifted(): lax.ppermute(block, axis, [(i, (i + step) % count) for i in range(count)])  39 us
    all_to_all x2, blocking collectives, spread(): lax.all_to_all(jnp.broadcast_to(block[None], (count, *block.shape)), axes...  29.3 us
    ppermute x11, waiting for transfers between devices, shifted(): lax.ppermute(block, axis, [(i, (i + step) % count) for i in range(count)])  20.4 us
    all_to_all x1, blocking collectives, per_device(): partial = lax.all_to_all(partial, 'z', 0, 0, tiled=True)  18.8 us
    all_to_all x1, starting transfers between devices, per_device(): weight = lax.all_to_all(weight, 'z', 0, 0, tiled=True)  15.7 us
    pallas_call x1, Pallas kernels, attention(): pl.pallas_call(attention_kernel, out_shape=(jax.ShapeDtypeStruct(grads.sh...  8.51 us
    unnamed x38, local copies, waits for them, and re-layouts  8.48 us
    all_to_all x1, waiting for transfers between devices, per_device(): weight = lax.all_to_all(weight, 'z', 0, 0, tiled=True)  6.23 us
  transfers between devices with their start and end apart: 14, of which 8 were waited for; matrix products, arithmetic and copies ran while one was open for 2% of the time, Pallas kernels for 1%

profile of v3, /device:TPU:1, one launch (start us, length us, event | category | flops | bytes accessed | tf_op | source)
XLA Modules:
  0.0 167.2 jit_solution(2319831975898976903)
XLA Ops:
  2.9 15.7 %all-to-all-start = ((bf16[16,16,384]{2,1,0:T(8,128)(2,1)}), bf16[16,16,384]{2,1,0:T(8,128)(2,1)S(1)}, u32[]{:S(2)}, u32[]{:S(2)}) async-start(bf16[16,16,384]{2,1,0:T(8,128)(2,1)} %slice.31), calls=%async_computation | async-start | bytes 393216 | tf_op jit(solution)/shard_map/all_to_all | solution.py:239
  18.6 4.4 %collective-permute-start.2 = (bf16[256,2048]{1,0:T(8,128)(2,1)}, bf16[256,2048]{1,0:T(8,128)(2,1)S(1)}, u32[]{:S(2)}, u32[]{:S(2)}) collective-permute-start(bf16[256,2048]{1,0:T(8,128)(2,1)} %bitcast.26), channel_id=1, source_target_pairs={{0,192},{64,0},{128,64},{192,128},{1,193},{65,1},{129,65},{193,129... | collective-permute-start | bytes 3145736 | tf_op jit(solution)/shard_map/ppermute | solution.py:37
  23.0 1.9 %collective-permute-start.1 = (bf16[256,2048]{1,0:T(8,128)(2,1)}, bf16[256,2048]{1,0:T(8,128)(2,1)S(1)}, u32[]{:S(2)}, u32[]{:S(2)}) collective-permute-start(bf16[256,2048]{1,0:T(8,128)(2,1)} %bitcast.27), channel_id=1, source_target_pairs={{0,64},{64,128},{128,192},{192,0},{1,65},{65,129},{129,193},{193,1... | collective-permute-start | bytes 3145736 | tf_op jit(solution)/shard_map/ppermute | solution.py:37
  24.9 6.2 %all-to-all-done = bf16[16,16,384]{2,1,0:T(8,128)(2,1)S(1)} async-done(((bf16[16,16,384]{2,1,0:T(8,128)(2,1)}), bf16[16,16,384]{2,1,0:T(8,128)(2,1)S(1)}, u32[]{:S(2)}, u32[]{:S(2)}) %all-to-all-start) | async-done | bytes 196640 | tf_op jit(solution)/shard_map/all_to_all | solution.py:239
  31.2 12.3 %all_to_all.30 = bf16[4,16,16,384]{3,2,1,0:T(8,128)(2,1)S(1)} all-to-all(bf16[4,16,16,384]{3,2,1,0:T(8,128)(2,1)S(1)} %broadcast_in_dim.6), channel_id=1, replica_groups=mesh['yh'=2,'x'=4,'core'=2,'z'=16,'yl'=2] {'yh','yl'}, dimensions={0} | all-to-all | bytes 1572864 | tf_op jit(solution)/shard_map/all_to_all | solution.py:30
  43.6 8.3 %collective-permute-start = (bf16[2,2,16,16,384]{4,3,2,1,0:T(8,128)(2,1)S(1)}, bf16[2,2,16,16,384]{4,3,2,1,0:T(8,128)(2,1)S(1)}, u32[]{:S(2)}, u32[]{:S(2)}) collective-permute-start(bf16[2,2,16,16,384]{4,3,2,1,0:T(8,128)(2,1)S(1)} %bitcast.30), channel_id=1, source_target_pairs={{0,32},{32,0},{1,33},{33,1},{2,34},{34,2},{3,35},{35,3},{4,36},{36... | collective-permute-start | bytes 2359304 | tf_op jit(solution)/shard_map/ppermute | solution.py:37
  51.9 4.4 %collective-permute-start.4 = (bf16[128,2048]{1,0:T(8,128)(2,1)S(1)}, bf16[128,2048]{1,0:T(8,128)(2,1)S(1)}, u32[]{:S(2)}, u32[]{:S(2)}) collective-permute-start(bf16[128,2048]{1,0:T(8,128)(2,1)S(1)} %slice.26), channel_id=1, source_target_pairs={{0,192},{64,0},{128,64},{192,128},{1,193},{65,1},{129,65},{193,129... | collective-permute-start | bytes 1572872 | tf_op jit(solution)/shard_map/ppermute | solution.py:37
  56.4 1.9 %collective-permute-start.3 = (bf16[128,2048]{1,0:T(8,128)(2,1)S(1)}, bf16[128,2048]{1,0:T(8,128)(2,1)S(1)}, u32[]{:S(2)}, u32[]{:S(2)}) collective-permute-start(bf16[128,2048]{1,0:T(8,128)(2,1)S(1)} %slice.25), channel_id=1, source_target_pairs={{0,64},{64,128},{128,192},{192,0},{1,65},{65,129},{129,193},{193,1... | collective-permute-start | bytes 1572872 | tf_op jit(solution)/shard_map/ppermute | solution.py:37
  58.3 9.3 %collective-permute-done.4.rest_4_.rest_10_ = bf16[128,2048]{1,0:T(8,128)(2,1)S(1)} collective-permute-done((bf16[128,2048]{1,0:T(8,128)(2,1)S(1)}, bf16[128,2048]{1,0:T(8,128)(2,1)S(1)}, u32[]{:S(2)}, u32[]{:S(2)}) %collective-permute-start.4) | collective-permute-done | bytes 524320 | tf_op jit(solution)/shard_map/ppermute | solution.py:37
  67.7 5.1 %collective-permute-done.3.rest_3_.rest_9_ = bf16[128,2048]{1,0:T(8,128)(2,1)S(1)} collective-permute-done((bf16[128,2048]{1,0:T(8,128)(2,1)S(1)}, bf16[128,2048]{1,0:T(8,128)(2,1)S(1)}, u32[]{:S(2)}, u32[]{:S(2)}) %collective-permute-start.3) | collective-permute-done | bytes 524320 | tf_op jit(solution)/shard_map/ppermute | solution.py:37
  72.7 4.0 %project.1 = (bf16[1024,128]{1,0:T(8,128)(2,1)S(1)}, bf16[16,64,256]{2,1,0:T(8,128)(2,1)}) custom-call(s32[3]{0:T(128)S(1)} %copy-done.10, bf16[2,2,16,16,384]{4,3,2,1,0:T(8,128)(2,1)S(1)} %bitcast.31, bf16[2,2,16,16,384]{4,3,2,1,0:T(8,128)(2,1)S(1)} %collective-permute-done.theirs_ref, bf16[256,2048]{1,0:T(8,128)(2,1)S(1)} %bitcast.28, ...), custom_call_target="tpu_custom_call" | custom-call | tf_op jit(solution)/shard_map/project/pallas_call | solution.py:83
  77.4 2.4 %collective-permute-start.5 = (bf16[16,64,256]{2,1,0:T(8,128)(2,1)}, bf16[16,64,256]{2,1,0:T(8,128)(2,1)}, u32[]{:S(2)}, u32[]{:S(2)}) collective-permute-start(bf16[16,64,256]{2,1,0:T(8,128)(2,1)} %get-tuple-element.10.rest_2_), channel_id=1, source_target_pairs={{0,256},{256,0},{1,257},{257,1},{2,258},{258,2},{3,259},{259,3},{4... | collective-permute-start | bytes 1572872 | tf_op jit(solution)/shard_map/ppermute | solution.py:37
  81.8 3.5 %all-to-all-start.2 = ((bf16[4,256,128]{2,1,0:T(8,128)(2,1)}), bf16[4,256,128]{2,1,0:T(8,128)(2,1)S(1)}, u32[]{:S(2)}, u32[]{:S(2)}) async-start(bf16[4,256,128]{2,1,0:T(8,128)(2,1)} %bitcast.34), calls=%async_computation.2 | async-start | bytes 524288 | tf_op jit(solution)/shard_map/all_to_all | solution.py:248
  85.4 3.3 %collective-permute-start.6 = (bf16[16,64,256]{2,1,0:T(8,128)(2,1)}, bf16[16,64,256]{2,1,0:T(8,128)(2,1)}, u32[]{:S(2)}, u32[]{:S(2)}) collective-permute-start(bf16[16,64,256]{2,1,0:T(8,128)(2,1)} %get-tuple-element.10.rest_2_), channel_id=1, source_target_pairs={{0,32},{32,0},{1,33},{33,1},{2,34},{34,2},{3,35},{35,3},{4,36},{36... | collective-permute-start | bytes 1572872 | tf_op jit(solution)/shard_map/ppermute | solution.py:37
  88.7 2.6 %all-to-all-done.2.rest_0_ = bf16[4,256,128]{2,1,0:T(8,128)(2,1)S(1)} async-done(((bf16[4,256,128]{2,1,0:T(8,128)(2,1)}), bf16[4,256,128]{2,1,0:T(8,128)(2,1)S(1)}, u32[]{:S(2)}, u32[]{:S(2)}) %all-to-all-start.2) | async-done | bytes 262176 | tf_op jit(solution)/shard_map/all_to_all | solution.py:248
  91.2 2.2 %collective-permute-done.5.rest_4_ = bf16[16,64,256]{2,1,0:T(8,128)(2,1)} collective-permute-done((bf16[16,64,256]{2,1,0:T(8,128)(2,1)}, bf16[16,64,256]{2,1,0:T(8,128)(2,1)}, u32[]{:S(2)}, u32[]{:S(2)}) %collective-permute-start.5) | collective-permute-done | bytes 524320 | tf_op jit(solution)/shard_map/ppermute | solution.py:37
  93.4 3.9 %collective-permute-start.7 = (bf16[16,64,256]{2,1,0:T(8,128)(2,1)}, bf16[16,64,256]{2,1,0:T(8,128)(2,1)}, u32[]{:S(2)}, u32[]{:S(2)}) collective-permute-start(bf16[16,64,256]{2,1,0:T(8,128)(2,1)} %collective-permute-done.5.rest_4_), channel_id=1, source_target_pairs={{0,32},{32,0},{1,33},{33,1},{2,34},{34,2},{3,35},{35,3},{4,36},{36... | collective-permute-start | bytes 1572872 | tf_op jit(solution)/shard_map/ppermute | solution.py:37
  102.9 8.5 %attention.1 = (bf16[4,256,128]{2,1,0:T(8,128)(2,1)S(1)}, bf16[8,16,16,128]{3,2,1,0:T(8,128)(2,1)S(1)}) custom-call(s32[3]{0:T(128)S(1)} %copy-done.10, s32[64,3]{1,0:T(8,128)S(1)} %bitcast.32, s32[64,3]{1,0:T(8,128)S(1)} %bitcast.33, s32[1,2]{1,0:T(1,128)S(1)} %copy-done.11, bf16[4,256,128]{2,1,0:T(8,128)(2,1)S(1)} %all-to-all-done.2.rest_0_, ...), custom_call_target="tpu_custom_call" | custom-call | tf_op jit(solution)/shard_map/attention/pallas_call | solution.py:191
  113.0 3.9 %all-to-all-start.3 = ((bf16[8,16,16,128]{3,2,1,0:T(8,128)(2,1)}), bf16[8,16,16,128]{3,2,1,0:T(8,128)(2,1)S(1)}, u32[]{:S(2)}, u32[]{:S(2)}) async-start(bf16[8,16,16,128]{3,2,1,0:T(8,128)(2,1)} %copy-done.5), calls=%async_computation.3 | async-start | bytes 1048576 | tf_op jit(solution)/shard_map/all_to_all | solution.py:267
  117.5 1.9 %collective-permute-start.10 = (bf16[256,128]{1,0:T(8,128)(2,1)S(1)}, bf16[256,128]{1,0:T(8,128)(2,1)S(1)}, u32[]{:S(2)}, u32[]{:S(2)}) collective-permute-start(bf16[256,128]{1,0:T(8,128)(2,1)S(1)} %get-tuple-element.18), channel_id=1, source_target_pairs={{0,64},{64,128},{128,192},{192,0},{1,65},{65,129},{129,193},{193,1... | collective-permute-start | bytes 196616 | tf_op jit(solution)/shard_map/ppermute | solution.py:37
  119.4 2.5 %collective-permute-start.9 = (bf16[256,128]{1,0:T(8,128)(2,1)S(1)}, bf16[256,128]{1,0:T(8,128)(2,1)S(1)}, u32[]{:S(2)}, u32[]{:S(2)}) collective-permute-start(bf16[256,128]{1,0:T(8,128)(2,1)S(1)} %get-tuple-element.19), channel_id=1, source_target_pairs={{0,128},{64,192},{128,0},{192,64},{1,129},{65,193},{129,1},{193,65... | collective-permute-start | bytes 196616 | tf_op jit(solution)/shard_map/ppermute | solution.py:37
  121.9 4.0 %collective-permute-start.8 = (bf16[256,128]{1,0:T(8,128)(2,1)S(1)}, bf16[256,128]{1,0:T(8,128)(2,1)S(1)}, u32[]{:S(2)}, u32[]{:S(2)}) collective-permute-start(bf16[256,128]{1,0:T(8,128)(2,1)S(1)} %get-tuple-element.20), channel_id=1, source_target_pairs={{0,192},{64,0},{128,64},{192,128},{1,193},{65,1},{129,65},{193,129... | collective-permute-start | bytes 196616 | tf_op jit(solution)/shard_map/ppermute | solution.py:37
  130.6 18.8 %all_to_all.31 = bf16[16,16,128]{2,1,0:T(8,128)(2,1)S(1)} all-to-all(bf16[16,16,128]{2,1,0:T(8,128)(2,1)S(1)} %reduce_sum.21), channel_id=1, replica_groups=mesh['yh'=2,'x'=4,'core'=2,'z'=16,'yl'=2] {'z'}, dimensions={0} | all-to-all | bytes 131072 | tf_op jit(solution)/shard_map/all_to_all | solution.py:270
  149.5 17.0 %all_to_all.32 = f32[16,16,128]{2,1,0:T(8,128)S(1)} all-to-all(f32[16,16,128]{2,1,0:T(8,128)S(1)} %broadcast_in_dim.8), channel_id=1, replica_groups=mesh['yh'=2,'x'=4,'core'=2,'z'=16,'yl'=2] {'yh','x','core'}, dimensions={0} | all-to-all | bytes 262144 | tf_op jit(solution)/shard_map/all_to_all | solution.py:30
  (59 shorter events, 18.1 us)
Async XLA Ops:
  2.9 28.3 %all-to-all-start = ((bf16[16,16,384]{2,1,0:T(8,128)(2,1)}), bf16[16,16,384]{2,1,0:T(8,128)(2,1)S(1)}, u32[]{:S(2)}, u32[]{:S(2)}) async-start(bf16[16,16,384]{2,1,0:T(8,128)(2,1)} %slice.31), calls=%async_computation | async-start | bytes 393216 | tf_op jit(solution)/shard_map/all_to_all | solution.py:239
  18.6 33.3 %collective-permute-start.2 = (bf16[256,2048]{1,0:T(8,128)(2,1)}, bf16[256,2048]{1,0:T(8,128)(2,1)S(1)}, u32[]{:S(2)}, u32[]{:S(2)}) collective-permute-start(bf16[256,2048]{1,0:T(8,128)(2,1)} %bitcast.26), channel_id=1, source_target_pairs={{0,192},{64,0},{128,64},{192,128},{1,193},{65,1},{129,65},{193,129... | collective-permute-start | bytes 3145736 | tf_op jit(solution)/shard_map/ppermute | solution.py:37
  23.0 33.3 %collective-permute-start.1 = (bf16[256,2048]{1,0:T(8,128)(2,1)}, bf16[256,2048]{1,0:T(8,128)(2,1)S(1)}, u32[]{:S(2)}, u32[]{:S(2)}) collective-permute-start(bf16[256,2048]{1,0:T(8,128)(2,1)} %bitcast.27), channel_id=1, source_target_pairs={{0,64},{64,128},{128,192},{192,0},{1,65},{65,129},{129,193},{193,1... | collective-permute-start | bytes 3145736 | tf_op jit(solution)/shard_map/ppermute | solution.py:37
  43.6 29.2 %copy-start = (bf16[1,256,2048]{2,1,0:T(8,128)(2,1)S(1)}, bf16[1,256,2048]{2,1,0:T(8,128)(2,1)}, u32[]{:S(2)}) copy-start(bf16[1,256,2048]{2,1,0:T(8,128)(2,1)} %param.8) | copy-start | bytes 3145732
  43.6 29.1 %collective-permute-start = (bf16[2,2,16,16,384]{4,3,2,1,0:T(8,128)(2,1)S(1)}, bf16[2,2,16,16,384]{4,3,2,1,0:T(8,128)(2,1)S(1)}, u32[]{:S(2)}, u32[]{:S(2)}) collective-permute-start(bf16[2,2,16,16,384]{4,3,2,1,0:T(8,128)(2,1)S(1)} %bitcast.30), channel_id=1, source_target_pairs={{0,32},{32,0},{1,33},{33,1},{2,34},{34,2},{3,35},{35,3},{4,36},{36... | collective-permute-start | bytes 2359304 | tf_op jit(solution)/shard_map/ppermute | solution.py:37
  51.9 20.8 %copy-start.10 = (s32[3]{0:T(128)S(1)}, s32[3]{0:T(128)}, u32[]{:S(2)}) copy-start(s32[3]{0:T(128)} %pad_add_fusion.where_ref) | copy-start | bytes 40
  51.9 15.7 %collective-permute-start.4 = (bf16[128,2048]{1,0:T(8,128)(2,1)S(1)}, bf16[128,2048]{1,0:T(8,128)(2,1)S(1)}, u32[]{:S(2)}, u32[]{:S(2)}) collective-permute-start(bf16[128,2048]{1,0:T(8,128)(2,1)S(1)} %slice.26), channel_id=1, source_target_pairs={{0,192},{64,0},{128,64},{192,128},{1,193},{65,1},{129,65},{193,129... | collective-permute-start | bytes 1572872 | tf_op jit(solution)/shard_map/ppermute | solution.py:37
  56.4 16.3 %collective-permute-start.3 = (bf16[128,2048]{1,0:T(8,128)(2,1)S(1)}, bf16[128,2048]{1,0:T(8,128)(2,1)S(1)}, u32[]{:S(2)}, u32[]{:S(2)}) collective-permute-start(bf16[128,2048]{1,0:T(8,128)(2,1)S(1)} %slice.25), channel_id=1, source_target_pairs={{0,64},{64,128},{128,192},{192,0},{1,65},{65,129},{129,193},{193,1... | collective-permute-start | bytes 1572872 | tf_op jit(solution)/shard_map/ppermute | solution.py:37
  67.7 9.1 %copy-start.1 = (bf16[128,2048]{1,0:T(8,128)(2,1)}, bf16[128,2048]{1,0:T(8,128)(2,1)S(1)}, u32[]{:S(2)}) copy-start(bf16[128,2048]{1,0:T(8,128)(2,1)S(1)} %collective-permute-done.4.rest_4_.rest_10_) | copy-start | bytes 1572868
  72.7 4.0 %copy-start.3 = (bf16[128,2048]{1,0:T(8,128)(2,1)}, bf16[128,2048]{1,0:T(8,128)(2,1)S(1)}, u32[]{:S(2)}) copy-start(bf16[128,2048]{1,0:T(8,128)(2,1)S(1)} %collective-permute-done.3.rest_3_.rest_9_) | copy-start | bytes 1572868
  77.4 16.0 %collective-permute-start.5 = (bf16[16,64,256]{2,1,0:T(8,128)(2,1)}, bf16[16,64,256]{2,1,0:T(8,128)(2,1)}, u32[]{:S(2)}, u32[]{:S(2)}) collective-permute-start(bf16[16,64,256]{2,1,0:T(8,128)(2,1)} %get-tuple-element.10.rest_2_), channel_id=1, source_target_pairs={{0,256},{256,0},{1,257},{257,1},{2,258},{258,2},{3,259},{259,3},{4... | collective-permute-start | bytes 1572872 | tf_op jit(solution)/shard_map/ppermute | solution.py:37
  81.8 15.6 %copy-start.15 = (s32[1,64,3]{1,0,2:T(1,128)S(1)}, s32[1,64,3]{1,0,2:T(1,128)}, u32[]{:S(2)}) copy-start(s32[1,64,3]{1,0,2:T(1,128)} %param.13) | copy-start | bytes 2308
  81.8 9.4 %all-to-all-start.2 = ((bf16[4,256,128]{2,1,0:T(8,128)(2,1)}), bf16[4,256,128]{2,1,0:T(8,128)(2,1)S(1)}, u32[]{:S(2)}, u32[]{:S(2)}) async-start(bf16[4,256,128]{2,1,0:T(8,128)(2,1)} %bitcast.34), calls=%async_computation.2 | async-start | bytes 524288 | tf_op jit(solution)/shard_map/all_to_all | solution.py:248
  85.4 12.1 %copy-start.16 = (s32[1,64,3]{1,0,2:T(1,128)S(1)}, s32[1,64,3]{1,0,2:T(1,128)}, u32[]{:S(2)}) copy-start(s32[1,64,3]{1,0,2:T(1,128)} %param.14) | copy-start | bytes 2308
  85.4 12.2 %collective-permute-start.6 = (bf16[16,64,256]{2,1,0:T(8,128)(2,1)}, bf16[16,64,256]{2,1,0:T(8,128)(2,1)}, u32[]{:S(2)}, u32[]{:S(2)}) collective-permute-start(bf16[16,64,256]{2,1,0:T(8,128)(2,1)} %get-tuple-element.10.rest_2_), channel_id=1, source_target_pairs={{0,32},{32,0},{1,33},{33,1},{2,34},{34,2},{3,35},{35,3},{4,36},{36... | collective-permute-start | bytes 1572872 | tf_op jit(solution)/shard_map/ppermute | solution.py:37
  93.4 5.8 %collective-permute-start.7 = (bf16[16,64,256]{2,1,0:T(8,128)(2,1)}, bf16[16,64,256]{2,1,0:T(8,128)(2,1)}, u32[]{:S(2)}, u32[]{:S(2)}) collective-permute-start(bf16[16,64,256]{2,1,0:T(8,128)(2,1)} %collective-permute-done.5.rest_4_), channel_id=1, source_target_pairs={{0,32},{32,0},{1,33},{33,1},{2,34},{34,2},{3,35},{35,3},{4,36},{36... | collective-permute-start | bytes 1572872 | tf_op jit(solution)/shard_map/ppermute | solution.py:37
  99.9 1.0 copy-start.2
  113.0 3.9 %copy-start.9 = (bf16[4,256,128]{2,1,0:T(8,128)(2,1)S(1)}, bf16[4,256,128]{2,1,0:T(8,128)(2,1)}, u32[]{:S(2)}) copy-start(bf16[4,256,128]{2,1,0:T(8,128)(2,1)} %copy-done.8) | copy-start | bytes 786436
  113.0 17.6 %all-to-all-start.3 = ((bf16[8,16,16,128]{3,2,1,0:T(8,128)(2,1)}), bf16[8,16,16,128]{3,2,1,0:T(8,128)(2,1)S(1)}, u32[]{:S(2)}, u32[]{:S(2)}) async-start(bf16[8,16,16,128]{3,2,1,0:T(8,128)(2,1)} %copy-done.5), calls=%async_computation.3 | async-start | bytes 1048576 | tf_op jit(solution)/shard_map/all_to_all | solution.py:267
  117.5 8.5 %collective-permute-start.10 = (bf16[256,128]{1,0:T(8,128)(2,1)S(1)}, bf16[256,128]{1,0:T(8,128)(2,1)S(1)}, u32[]{:S(2)}, u32[]{:S(2)}) collective-permute-start(bf16[256,128]{1,0:T(8,128)(2,1)S(1)} %get-tuple-element.18), channel_id=1, source_target_pairs={{0,64},{64,128},{128,192},{192,0},{1,65},{65,129},{129,193},{193,1... | collective-permute-start | bytes 196616 | tf_op jit(solution)/shard_map/ppermute | solution.py:37
  119.4 7.1 %collective-permute-start.9 = (bf16[256,128]{1,0:T(8,128)(2,1)S(1)}, bf16[256,128]{1,0:T(8,128)(2,1)S(1)}, u32[]{:S(2)}, u32[]{:S(2)}) collective-permute-start(bf16[256,128]{1,0:T(8,128)(2,1)S(1)} %get-tuple-element.19), channel_id=1, source_target_pairs={{0,128},{64,192},{128,0},{192,64},{1,129},{65,193},{129,1},{193,65... | collective-permute-start | bytes 196616 | tf_op jit(solution)/shard_map/ppermute | solution.py:37
  121.9 6.3 %collective-permute-start.8 = (bf16[256,128]{1,0:T(8,128)(2,1)S(1)}, bf16[256,128]{1,0:T(8,128)(2,1)S(1)}, u32[]{:S(2)}, u32[]{:S(2)}) collective-permute-start(bf16[256,128]{1,0:T(8,128)(2,1)S(1)} %get-tuple-element.20), channel_id=1, source_target_pairs={{0,192},{64,0},{128,64},{192,128},{1,193},{65,1},{129,65},{193,129... | collective-permute-start | bytes 196616 | tf_op jit(solution)/shard_map/ppermute | solution.py:37
  126.0 2.2 %copy-start.12 = (bf16[256,128]{1,0:T(8,128)(2,1)}, bf16[256,128]{1,0:T(8,128)(2,1)S(1)}, u32[]{:S(2)}) copy-start(bf16[256,128]{1,0:T(8,128)(2,1)S(1)} %collective-permute-done.10.refs_3_) | copy-start | bytes 196612
  126.5 1.7 %copy-start.13 = (bf16[256,128]{1,0:T(8,128)(2,1)}, bf16[256,128]{1,0:T(8,128)(2,1)S(1)}, u32[]{:S(2)}) copy-start(bf16[256,128]{1,0:T(8,128)(2,1)S(1)} %collective-permute-done.9.refs_2_) | copy-start | bytes 196612
  (7 other events, 5.5 us)

commit v4 on v3

--- a/solution.py
+++ b/solution.py
@@ -47,7 +47,8 @@
             out_ref[copy, :, i * HD : (i + 1) * HD] = part
 
 
-def project_kernel(where_ref, mine_ref, theirs_ref, *rest):
+def project_kernel(where_ref, mine_ref, theirs_a_ref, theirs_b_ref, *rest):
+    theirs = (theirs_a_ref, theirs_b_ref)
     token_refs, (q_ref, kv_ref, w_ref) = rest[:-3], rest[-3:]
     core = where_ref[2]
     _, _, depth, rows, width = mine_ref.shape
@@ -59,7 +60,7 @@
                 here = pl.multiple_of(base + core * rows, rows)
                 there = pl.multiple_of(base + (1 - core) * rows, rows)
                 w_ref[pl.ds(here, rows), :] = mine_ref[yh, yl, z]
-                w_ref[pl.ds(there, rows), :] = theirs_ref[yh, yl, z]
+                w_ref[pl.ds(there, rows), :] = theirs[yh][yl, z]
         return carry
 
     lax.fori_loop(0, depth, assemble, 0)
@@ -76,7 +77,7 @@
     return [(0, (own,)), (1, (before,)), (3, (after,)), (2, (low_far, high_far))]
 
 
-def project(where, mine, theirs, token_sets):
+def project(where, mine, theirs_a, theirs_b, token_sets):
     count, depth = token_sets[0].shape
     total = count * HEADS
     vmem = pl.BlockSpec(memory_space=pltpu.VMEM)
@@ -86,12 +87,12 @@
             jax.ShapeDtypeStruct((total, HD), jnp.bfloat16),
             jax.ShapeDtypeStruct((PIECE_BLOCKS, BLK, 2 * HD), jnp.bfloat16),
         ),
-        in_specs=[pl.BlockSpec(memory_space=pltpu.SMEM)] + [vmem] * (2 + len(token_sets)),
+        in_specs=[pl.BlockSpec(memory_space=pltpu.SMEM)] + [vmem] * (3 + len(token_sets)),
         out_specs=(vmem, vmem),
         scratch_shapes=[pltpu.VMEM((depth, 3 * HD), jnp.bfloat16)],
         compiler_params=pltpu.CompilerParams(vmem_limit_bytes=24 * 1024 * 1024),
         name="project",
-    )(where, mine, theirs, *token_sets)
+    )(where, mine, theirs_a, theirs_b, *token_sets)
 
 
 def attention_kernel(where_ref, owner_ref, offset_ref, global_ref, *rest):
@@ -205,7 +206,7 @@
             pltpu.VMEM((HEADS, *token_sets[0].shape), jnp.bfloat16),
             pltpu.SemaphoreType.DMA((2 + PIECES + len(token_sets),)),
         ],
-        compiler_params=pltpu.CompilerParams(vmem_limit_bytes=32 * 1024 * 1024),
+        compiler_params=pltpu.CompilerParams(vmem_limit_bytes=56 * 1024 * 1024),
         name="attention",
     )(where, owners, offsets, global_list, grads, queries, *pieces, *token_sets)
 
@@ -237,17 +238,18 @@
         name="slice",
     )(where, key_weight, value_weight, query_weight)
     weight = lax.all_to_all(weight, "z", 0, 0, tiled=True)
-    weight = spread(weight, ("yh", "yl")).reshape(2, 2, 16, rows, 3 * HD)
-    partner = shifted(weight, "core", 1)
 
     cut = count // 2
     before, after = shifted(own, "x", 1), shifted(own, "x", -1)
+    weight, before, after = lax.optimization_barrier((weight, before, after))
+    weight = spread(weight, ("yh", "yl")).reshape(2, 2, 16, rows, 3 * HD)
+    partner = [shifted(part, "core", 1) for part in weight]
     low_far, high_far = shifted(before[:cut], "x", 1), shifted(after[cut:], "x", -1)
     token_sets = (own, before, after, low_far, high_far)
     grads = cotangent[0].reshape(count, HEADS, HD).transpose(1, 0, 2)
     grads = lax.all_to_all(grads, "x", 0, 0, tiled=True)
 
-    queries, kv = project(where, weight, partner, token_sets)
+    queries, kv = project(where, weight, *partner, token_sets)
     across = shifted(kv, "yh", 1)
     across, grads = lax.optimization_barrier((across, grads))
     pieces = [kv, shifted(kv, "core", 1), across, shifted(across, "core", 1)]
@@ -256,6 +258,14 @@
         where, rand_owner[0], rand_offset[0], global_ids, grads, queries, pieces, token_sets
     )
     returned = [attended[0]] + [shifted(attended[s], "x", -s) for s in range(1, HEADS)]
+    partial = lax.all_to_all(partial, ("yh", "yl", "core"), 0, 0, tiled=True)
+    partial = jnp.sum(partial.astype(jnp.float32), axis=0).astype(jnp.bfloat16)
+    partial, returned[1], returned[3] = lax.optimization_barrier(
+        (partial, returned[1], returned[3])
+    )
+    partial = lax.all_to_all(partial, "z", 0, 0, tiled=True)
+    partial = jnp.sum(partial.astype(jnp.float32), axis=0)
+    partial, returned[2] = lax.optimization_barrier((partial, returned[2]))
     attn = pl.pallas_call(
         merge_kernel,
         out_shape=jax.ShapeDtypeStruct((count, HEADS * HD), jnp.bfloat16),
@@ -264,11 +274,6 @@
         name="merge",
     )(where, *returned)
 
-    partial = lax.all_to_all(partial, ("yh", "yl", "core"), 0, 0, tiled=True)
-    partial = jnp.sum(partial.astype(jnp.float32), axis=0).astype(jnp.bfloat16)
-    partial, attn = lax.optimization_barrier((partial, attn))
-    partial = lax.all_to_all(partial, "z", 0, 0, tiled=True)
-    partial = jnp.sum(partial.astype(jnp.float32), axis=0)
     final = spread(partial, ("yh", "x", "core")).reshape(2, 4, 2, rows, HD)
     query_grad = final.transpose(0, 2, 3, 1, 4).reshape(4 * rows, HEADS * HD)
     return attn[None], query_grad

time: 168 us -> 157 us (0.935)
  blocking collectives: 48.1 us -> 27.3 us
  starting transfers between devices: 62.2 us -> 78.5 us
  waiting for transfers between devices: 29.2 us -> 19.5 us
    all_to_all x3 -> x1, blocking collectives: 48.1 us -> 27.3 us  [per_device(): weight = lax.all_to_all(weight, 'z', 0, 0, tiled=True)]
    ppermute x11 -> x12, waiting for transfers between devices: 20.4 us -> 1.75 us  [shifted(): lax.ppermute(block, axis, [(i, (i + step) % count) for i in range(count)])]
    ppermute x11 -> x12, starting transfers between devices: 39 us -> 49.8 us  [shifted(): lax.ppermute(block, axis, [(i, (i + step) % count) for i in range(count)])]
    all_to_all x1 -> x3, waiting for transfers between devices: 6.23 us -> 15.5 us  [the longest x1 9.4 us: per_device(): partial = lax.all_to_all(partial, 'z', 0, 0, tiled=True)]
    all_to_all x1 -> x3, starting transfers between devices: 15.7 us -> 20.6 us  [the longest x2 12.8 us: spread(): lax.all_to_all(jnp.broadcast_to(block[None], (count, *block.shape)), axes...]
    unnamed x38 -> x36, local copies, waits for them, and re-layouts: 8.48 us -> 5.49 us
    all_to_all x1, waiting for transfers between devices: 2.57 us -> 0.01 us  [per_device(): grads = lax.all_to_all(grads, 'x', 0, 0, tiled=True)]
    all_to_all x1, waiting for transfers between devices: 0.01 us -> 2.32 us  [per_device(): partial = lax.all_to_all(partial, ('yh', 'yl', 'core'), 0, 0, tiled=True)]
  transfers between devices with their start and end apart: 14 -> 17, of which waited for: 8 -> 6; matrix products, arithmetic and copies ran while one was open for 2% -> 5% of each run, Pallas kernels for 1% -> 2%
where the time goes in v4:
time: 157 us; the launch traced here: 155 us
  starting transfers between devices  78.5 us (50%)
  blocking collectives  27.3 us (17%)
  waiting for transfers between devices  19.5 us (12%)
  Pallas kernels  17.3 us (11%)
  local copies, waits for them, and re-layouts  10.5 us (7%)
    ppermute x12, starting transfers between devices, shifted(): lax.ppermute(block, axis, [(i, (i + step) % count) for i in range(count)])  49.8 us
    all_to_all x1, blocking collectives, per_device(): weight = lax.all_to_all(weight, 'z', 0, 0, tiled=True)  27.3 us
    all_to_all x2, starting transfers between devices, spread(): lax.all_to_all(jnp.broadcast_to(block[None], (count, *block.shape)), axes...  12.8 us
    pallas_call x1, Pallas kernels, attention(): pl.pallas_call(attention_kernel, out_shape=(jax.ShapeDtypeStruct(grads.sh...  9.5 us
    all_to_all x1, waiting for transfers between devices, per_device(): partial = lax.all_to_all(partial, 'z', 0, 0, tiled=True)  9.4 us
    all_to_all x1, starting transfers between devices, per_device(): partial = lax.all_to_all(partial, 'z', 0, 0, tiled=True)  7.74 us
    all_to_all x2, waiting for transfers between devices, spread(): lax.all_to_all(jnp.broadcast_to(block[None], (count, *block.shape)), axes...  6.08 us
    unnamed x36, local copies, waits for them, and re-layouts  5.49 us
  transfers between devices with their start and end apart: 17, of which 6 were waited for; matrix products, arithmetic and copies ran while one was open for 5% of the time, Pallas kernels for 2%

profile of v4, /device:TPU:1, one launch (start us, length us, event | category | flops | bytes accessed | tf_op | source)
XLA Modules:
  0.0 155.5 jit_solution(11148160048473919248)
XLA Ops:
  0.6 5.2 %collective-permute-start.1 = (bf16[256,2048]{1,0:T(8,128)(2,1)}, bf16[256,2048]{1,0:T(8,128)(2,1)S(1)}, u32[]{:S(2)}, u32[]{:S(2)}) collective-permute-start(bf16[256,2048]{1,0:T(8,128)(2,1)} %bitcast.27), channel_id=1, source_target_pairs={{0,192},{64,0},{128,64},{192,128},{1,193},{65,1},{129,65},{193,129... | collective-permute-start | bytes 3145736 | tf_op jit(solution)/shard_map/ppermute | solution.py:37
  5.9 1.9 %collective-permute-start = (bf16[256,2048]{1,0:T(8,128)(2,1)}, bf16[256,2048]{1,0:T(8,128)(2,1)S(1)}, u32[]{:S(2)}, u32[]{:S(2)}) collective-permute-start(bf16[256,2048]{1,0:T(8,128)(2,1)} %bitcast.28), channel_id=1, source_target_pairs={{0,64},{64,128},{128,192},{192,0},{1,65},{65,129},{129,193},{193,1... | collective-permute-start | bytes 3145736 | tf_op jit(solution)/shard_map/ppermute | solution.py:37
  10.0 27.3 %all_to_all.30 = bf16[16,16,384]{2,1,0:T(8,128)(2,1)S(1)} all-to-all(bf16[16,16,384]{2,1,0:T(8,128)(2,1)} %slice.31), channel_id=1, replica_groups=mesh['yh'=2,'x'=4,'core'=2,'z'=16,'yl'=2] {'z'}, dimensions={0} | all-to-all | bytes 393216 | tf_op jit(solution)/shard_map/all_to_all | solution.py:240
  38.4 4.2 %all-to-all-start.1 = ((bf16[4,16,16,384]{3,2,1,0:T(8,128)(2,1)}), bf16[4,16,16,384]{3,2,1,0:T(8,128)(2,1)S(1)}, u32[]{:S(2)}, u32[]{:S(2)}) async-start(bf16[4,16,16,384]{3,2,1,0:T(8,128)(2,1)} %broadcast_in_dim.6), calls=%async_computation.1 | async-start | bytes 1572864 | tf_op jit(solution)/shard_map/all_to_all | solution.py:30
  44.2 4.5 %collective-permute-start.5 = (bf16[128,2048]{1,0:T(8,128)(2,1)}, bf16[128,2048]{1,0:T(8,128)(2,1)S(1)}, u32[]{:S(2)}, u32[]{:S(2)}) collective-permute-start(bf16[128,2048]{1,0:T(8,128)(2,1)} %slice.22), channel_id=1, source_target_pairs={{0,192},{64,0},{128,64},{192,128},{1,193},{65,1},{129,65},{193,129... | collective-permute-start | bytes 1572872 | tf_op jit(solution)/shard_map/ppermute | solution.py:37
  48.8 1.9 %collective-permute-start.4 = (bf16[128,2048]{1,0:T(8,128)(2,1)}, bf16[128,2048]{1,0:T(8,128)(2,1)}, u32[]{:S(2)}, u32[]{:S(2)}) collective-permute-start(bf16[128,2048]{1,0:T(8,128)(2,1)} %slice.21), channel_id=1, source_target_pairs={{0,64},{64,128},{128,192},{192,0},{1,65},{65,129},{129,193},{193,1... | collective-permute-start | bytes 1572872 | tf_op jit(solution)/shard_map/ppermute | solution.py:37
  51.0 8.6 %collective-permute-start.3 = (bf16[2,16,16,384]{3,2,1,0:T(8,128)(2,1)S(1)}, bf16[2,16,16,384]{3,2,1,0:T(8,128)(2,1)S(1)}, u32[]{:S(2)}, u32[]{:S(2)}) collective-permute-start(bf16[2,16,16,384]{3,2,1,0:T(8,128)(2,1)S(1)} %get-tuple-element.30), channel_id=1, source_target_pairs={{0,32},{32,0},{1,33},{33,1},{2,34},{34,2},{3,35},{35,3},{4,36},{36... | collective-permute-start | bytes 1179656 | tf_op jit(solution)/shard_map/ppermute | solution.py:37
  59.6 1.9 %collective-permute-start.2 = (bf16[2,16,16,384]{3,2,1,0:T(8,128)(2,1)S(1)}, bf16[2,16,16,384]{3,2,1,0:T(8,128)(2,1)S(1)}, u32[]{:S(2)}, u32[]{:S(2)}) collective-permute-start(bf16[2,16,16,384]{3,2,1,0:T(8,128)(2,1)S(1)} %get-tuple-element.31), channel_id=1, source_target_pairs={{0,32},{32,0},{1,33},{33,1},{2,34},{34,2},{3,35},{35,3},{4,36},{36... | collective-permute-start | bytes 1179656 | tf_op jit(solution)/shard_map/ppermute | solution.py:37
  63.2 4.5 %project.1 = (bf16[1024,128]{1,0:T(8,128)(2,1)S(1)}, bf16[16,64,256]{2,1,0:T(8,128)(2,1)}) custom-call(s32[3]{0:T(128)S(1)} %copy-done.5, bf16[2,2,16,16,384]{4,3,2,1,0:T(8,128)(2,1)S(1)} %bitcast.26, bf16[2,16,16,384]{3,2,1,0:T(8,128)(2,1)S(1)} %collective-permute-done.2.theirs_a_ref, bf16[2,16,16,384]{3,2,1,0:T(8,128)(2,1)S(1)} %collective-permute-done.3.theirs_b_ref, ...), custom_call_target="tpu_custom_call" | custom-call | tf_op jit(solution)/shard_map/project/pallas_call | solution.py:84
  68.4 4.1 %collective-permute-start.6 = (bf16[16,64,256]{2,1,0:T(8,128)(2,1)}, bf16[16,64,256]{2,1,0:T(8,128)(2,1)S(1)}, u32[]{:S(2)}, u32[]{:S(2)}) collective-permute-start(bf16[16,64,256]{2,1,0:T(8,128)(2,1)} %get-tuple-element.19.rest_2_), channel_id=1, source_target_pairs={{0,256},{256,0},{1,257},{257,1},{2,258},{258,2},{3,259},{259,3},{4... | collective-permute-start | bytes 1572872 | tf_op jit(solution)/shard_map/ppermute | solution.py:37
  74.5 4.3 %all-to-all-start.2 = ((bf16[4,256,128]{2,1,0:T(8,128)(2,1)}), bf16[4,256,128]{2,1,0:T(8,128)(2,1)S(1)}, u32[]{:S(2)}, u32[]{:S(2)}) async-start(bf16[4,256,128]{2,1,0:T(8,128)(2,1)} %bitcast.8), calls=%async_computation.2 | async-start | bytes 524288 | tf_op jit(solution)/shard_map/all_to_all | solution.py:250
  78.8 6.3 %collective-permute-start.7 = (bf16[16,64,256]{2,1,0:T(8,128)(2,1)}, bf16[16,64,256]{2,1,0:T(8,128)(2,1)S(1)}, u32[]{:S(2)}, u32[]{:S(2)}) collective-permute-start(bf16[16,64,256]{2,1,0:T(8,128)(2,1)} %get-tuple-element.19.rest_2_), channel_id=1, source_target_pairs={{0,32},{32,0},{1,33},{33,1},{2,34},{34,2},{3,35},{35,3},{4,36},{36... | collective-permute-start | bytes 1572872 | tf_op jit(solution)/shard_map/ppermute | solution.py:37
  85.2 6.6 %collective-permute-start.8 = (bf16[16,64,256]{2,1,0:T(8,128)(2,1)S(1)}, bf16[16,64,256]{2,1,0:T(8,128)(2,1)S(1)}, u32[]{:S(2)}, u32[]{:S(2)}) collective-permute-start(bf16[16,64,256]{2,1,0:T(8,128)(2,1)S(1)} %collective-permute-done.6.rest_4_), channel_id=1, source_target_pairs={{0,32},{32,0},{1,33},{33,1},{2,34},{34,2},{3,35},{35,3},{4,36},{36... | collective-permute-start | bytes 1572872 | tf_op jit(solution)/shard_map/ppermute | solution.py:37
  94.2 9.5 %attention.1 = (bf16[4,256,128]{2,1,0:T(8,128)(2,1)}, bf16[8,16,16,128]{3,2,1,0:T(8,128)(2,1)}) custom-call(s32[3]{0:T(128)} %pad_add_fusion.where_ref, s32[64,3]{1,0:T(8,128)} %bitcast.35, s32[64,3]{1,0:T(8,128)} %bitcast.36, s32[1,2]{1,0:T(1,128)} %global_ref.1, bf16[4,256,128]{2,1,0:T(8,128)(2,1)} %copy-done.6, bf16[1024,128]{1,0:T(8,128)(2,1)} %copy-done.4, ...), custom_call_target="tpu_custom_call" | custom-call | tf_op jit(solution)/shard_map/attention/pallas_call | solution.py:192
  103.7 3.8 %all-to-all-start.3 = ((bf16[8,16,16,128]{3,2,1,0:T(8,128)(2,1)}), bf16[8,16,16,128]{3,2,1,0:T(8,128)(2,1)S(1)}, u32[]{:S(2)}, u32[]{:S(2)}) async-start(bf16[8,16,16,128]{3,2,1,0:T(8,128)(2,1)} %get-tuple-element.24), calls=%async_computation.3 | async-start | bytes 1048576 | tf_op jit(solution)/shard_map/all_to_all | solution.py:261
  108.2 2.2 %collective-permute-start.10 = (bf16[256,128]{1,0:T(8,128)(2,1)S(1)}, bf16[256,128]{1,0:T(8,128)(2,1)S(1)}, u32[]{:S(2)}, u32[]{:S(2)}) collective-permute-start(bf16[256,128]{1,0:T(8,128)(2,1)S(1)} %get-tuple-element.33), channel_id=1, source_target_pairs={{0,64},{64,128},{128,192},{192,0},{1,65},{65,129},{129,193},{193,1... | collective-permute-start | bytes 196616 | tf_op jit(solution)/shard_map/ppermute | solution.py:37
  110.4 4.3 %collective-permute-start.9 = (bf16[256,128]{1,0:T(8,128)(2,1)S(1)}, bf16[256,128]{1,0:T(8,128)(2,1)S(1)}, u32[]{:S(2)}, u32[]{:S(2)}) collective-permute-start(bf16[256,128]{1,0:T(8,128)(2,1)S(1)} %get-tuple-element.34), channel_id=1, source_target_pairs={{0,192},{64,0},{128,64},{192,128},{1,193},{65,1},{129,65},{193,129... | collective-permute-start | bytes 196616 | tf_op jit(solution)/shard_map/ppermute | solution.py:37
  114.7 2.3 %all-to-all-done.3 = bf16[8,16,16,128]{3,2,1,0:T(8,128)(2,1)S(1)} async-done(((bf16[8,16,16,128]{3,2,1,0:T(8,128)(2,1)}), bf16[8,16,16,128]{3,2,1,0:T(8,128)(2,1)S(1)}, u32[]{:S(2)}, u32[]{:S(2)}) %all-to-all-start.3) | async-done | bytes 524320 | tf_op jit(solution)/shard_map/all_to_all | solution.py:261
  118.4 7.7 %all-to-all-start.4 = ((bf16[16,16,128]{2,1,0:T(8,128)(2,1)}), bf16[16,16,128]{2,1,0:T(8,128)(2,1)S(1)}, u32[]{:S(2)}, u32[]{:S(2)}) async-start(bf16[16,16,128]{2,1,0:T(8,128)(2,1)} %reduce_sum.21), calls=%async_computation.4 | async-start | bytes 131072 | tf_op jit(solution)/shard_map/all_to_all | solution.py:266
  126.2 2.2 %collective-permute-start.11 = (bf16[256,128]{1,0:T(8,128)(2,1)S(1)}, bf16[256,128]{1,0:T(8,128)(2,1)S(1)}, u32[]{:S(2)}, u32[]{:S(2)}) collective-permute-start(bf16[256,128]{1,0:T(8,128)(2,1)S(1)} %get-tuple-element.32), channel_id=1, source_target_pairs={{0,128},{64,192},{128,0},{192,64},{1,129},{65,193},{129,1},{193,65... | collective-permute-start | bytes 196616 | tf_op jit(solution)/shard_map/ppermute | solution.py:37
  128.4 9.4 %all-to-all-done.4 = bf16[16,16,128]{2,1,0:T(8,128)(2,1)S(1)} async-done(((bf16[16,16,128]{2,1,0:T(8,128)(2,1)}), bf16[16,16,128]{2,1,0:T(8,128)(2,1)S(1)}, u32[]{:S(2)}, u32[]{:S(2)}) %all-to-all-start.4) | async-done | bytes 65568 | tf_op jit(solution)/shard_map/all_to_all | solution.py:266
  138.5 8.7 %all-to-all-start.5 = ((f32[16,16,128]{2,1,0:T(8,128)}), f32[16,16,128]{2,1,0:T(8,128)S(1)}, u32[]{:S(2)}, u32[]{:S(2)}) async-start(f32[16,16,128]{2,1,0:T(8,128)} %broadcast_in_dim.8), calls=%async_computation.5 | async-start | bytes 262144 | tf_op jit(solution)/shard_map/all_to_all | solution.py:30
  147.1 1.7 %merge.1 = bf16[256,512]{1,0:T(8,128)(2,1)} custom-call(s32[3]{0:T(128)} %pad_add_fusion.where_ref, bf16[256,128]{1,0:T(8,128)(2,1)} %get-tuple-element.35.refs_0_, bf16[256,128]{1,0:T(8,128)(2,1)} %copy-done.12, bf16[256,128]{1,0:T(8,128)(2,1)} %copy-done.13, bf16[256,128]{1,0:T(8,128)(2,1)} %copy-done.11), custom_call_target="tpu_custom_call" | custom-call | tf_op jit(solution)/shard_map/merge/pallas_call | solution.py:269
  148.8 5.9 %all-to-all-done.5 = f32[16,16,128]{2,1,0:T(8,128)S(1)} async-done(((f32[16,16,128]{2,1,0:T(8,128)}), f32[16,16,128]{2,1,0:T(8,128)S(1)}, u32[]{:S(2)}, u32[]{:S(2)}) %all-to-all-start.5) | async-done | bytes 131104 | tf_op jit(solution)/shard_map/all_to_all | solution.py:30
  (62 shorter events, 15.5 us)
Async XLA Ops:
  0.6 36.7 %collective-permute-start.1 = (bf16[256,2048]{1,0:T(8,128)(2,1)}, bf16[256,2048]{1,0:T(8,128)(2,1)S(1)}, u32[]{:S(2)}, u32[]{:S(2)}) collective-permute-start(bf16[256,2048]{1,0:T(8,128)(2,1)} %bitcast.27), channel_id=1, source_target_pairs={{0,192},{64,0},{128,64},{192,128},{1,193},{65,1},{129,65},{193,129... | collective-permute-start | bytes 3145736 | tf_op jit(solution)/shard_map/ppermute | solution.py:37
  5.9 31.5 %collective-permute-start = (bf16[256,2048]{1,0:T(8,128)(2,1)}, bf16[256,2048]{1,0:T(8,128)(2,1)S(1)}, u32[]{:S(2)}, u32[]{:S(2)}) collective-permute-start(bf16[256,2048]{1,0:T(8,128)(2,1)} %bitcast.28), channel_id=1, source_target_pairs={{0,64},{64,128},{128,192},{192,0},{1,65},{65,129},{129,193},{193,1... | collective-permute-start | bytes 3145736 | tf_op jit(solution)/shard_map/ppermute | solution.py:37
  37.3 25.9 %copy-start = (bf16[256,2048]{1,0:T(8,128)(2,1)}, bf16[256,2048]{1,0:T(8,128)(2,1)S(1)}, u32[]{:S(2)}) copy-start(bf16[256,2048]{1,0:T(8,128)(2,1)S(1)} %collective-permute-done.1.rest_2_.rest_8_) | copy-start | bytes 3145732
  37.3 25.9 %copy-start.1 = (bf16[256,2048]{1,0:T(8,128)(2,1)}, bf16[256,2048]{1,0:T(8,128)(2,1)S(1)}, u32[]{:S(2)}) copy-start(bf16[256,2048]{1,0:T(8,128)(2,1)S(1)} %collective-permute-done.rest_1_.rest_7_) | copy-start | bytes 3145732
  38.4 12.5 %all-to-all-start.1 = ((bf16[4,16,16,384]{3,2,1,0:T(8,128)(2,1)}), bf16[4,16,16,384]{3,2,1,0:T(8,128)(2,1)S(1)}, u32[]{:S(2)}, u32[]{:S(2)}) async-start(bf16[4,16,16,384]{3,2,1,0:T(8,128)(2,1)} %broadcast_in_dim.6), calls=%async_computation.1 | async-start | bytes 1572864 | tf_op jit(solution)/shard_map/all_to_all | solution.py:30
  44.2 17.3 %collective-permute-start.5 = (bf16[128,2048]{1,0:T(8,128)(2,1)}, bf16[128,2048]{1,0:T(8,128)(2,1)S(1)}, u32[]{:S(2)}, u32[]{:S(2)}) collective-permute-start(bf16[128,2048]{1,0:T(8,128)(2,1)} %slice.22), channel_id=1, source_target_pairs={{0,192},{64,0},{128,64},{192,128},{1,193},{65,1},{129,65},{193,129... | collective-permute-start | bytes 1572872 | tf_op jit(solution)/shard_map/ppermute | solution.py:37
  48.8 12.7 %collective-permute-start.4 = (bf16[128,2048]{1,0:T(8,128)(2,1)}, bf16[128,2048]{1,0:T(8,128)(2,1)}, u32[]{:S(2)}, u32[]{:S(2)}) collective-permute-start(bf16[128,2048]{1,0:T(8,128)(2,1)} %slice.21), channel_id=1, source_target_pairs={{0,64},{64,128},{128,192},{192,0},{1,65},{65,129},{129,193},{193,1... | collective-permute-start | bytes 1572872 | tf_op jit(solution)/shard_map/ppermute | solution.py:37
  50.9 12.3 %copy-start.2 = (bf16[1,256,2048]{2,1,0:T(8,128)(2,1)S(1)}, bf16[1,256,2048]{2,1,0:T(8,128)(2,1)}, u32[]{:S(2)}) copy-start(bf16[1,256,2048]{2,1,0:T(8,128)(2,1)} %param.8) | copy-start | bytes 3145732
  51.0 10.5 %collective-permute-start.3 = (bf16[2,16,16,384]{3,2,1,0:T(8,128)(2,1)S(1)}, bf16[2,16,16,384]{3,2,1,0:T(8,128)(2,1)S(1)}, u32[]{:S(2)}, u32[]{:S(2)}) collective-permute-start(bf16[2,16,16,384]{3,2,1,0:T(8,128)(2,1)S(1)} %get-tuple-element.30), channel_id=1, source_target_pairs={{0,32},{32,0},{1,33},{33,1},{2,34},{34,2},{3,35},{35,3},{4,36},{36... | collective-permute-start | bytes 1179656 | tf_op jit(solution)/shard_map/ppermute | solution.py:37
  59.6 3.6 %collective-permute-start.2 = (bf16[2,16,16,384]{3,2,1,0:T(8,128)(2,1)S(1)}, bf16[2,16,16,384]{3,2,1,0:T(8,128)(2,1)S(1)}, u32[]{:S(2)}, u32[]{:S(2)}) collective-permute-start(bf16[2,16,16,384]{3,2,1,0:T(8,128)(2,1)S(1)} %get-tuple-element.31), channel_id=1, source_target_pairs={{0,32},{32,0},{1,33},{33,1},{2,34},{34,2},{3,35},{35,3},{4,36},{36... | collective-permute-start | bytes 1179656 | tf_op jit(solution)/shard_map/ppermute | solution.py:37
  68.4 16.8 %collective-permute-start.6 = (bf16[16,64,256]{2,1,0:T(8,128)(2,1)}, bf16[16,64,256]{2,1,0:T(8,128)(2,1)S(1)}, u32[]{:S(2)}, u32[]{:S(2)}) collective-permute-start(bf16[16,64,256]{2,1,0:T(8,128)(2,1)} %get-tuple-element.19.rest_2_), channel_id=1, source_target_pairs={{0,256},{256,0},{1,257},{257,1},{2,258},{258,2},{3,259},{259,3},{4... | collective-permute-start | bytes 1572872 | tf_op jit(solution)/shard_map/ppermute | solution.py:37
  74.5 17.3 %copy-start.14 = (s32[1,64,3]{1,0,2:T(1,128)S(1)}, s32[1,64,3]{1,0,2:T(1,128)}, u32[]{:S(2)}) copy-start(s32[1,64,3]{1,0,2:T(1,128)} %param.13) | copy-start | bytes 2308
  74.5 10.7 %all-to-all-start.2 = ((bf16[4,256,128]{2,1,0:T(8,128)(2,1)}), bf16[4,256,128]{2,1,0:T(8,128)(2,1)S(1)}, u32[]{:S(2)}, u32[]{:S(2)}) async-start(bf16[4,256,128]{2,1,0:T(8,128)(2,1)} %bitcast.8), calls=%async_computation.2 | async-start | bytes 524288 | tf_op jit(solution)/shard_map/all_to_all | solution.py:250
  78.8 13.7 %copy-start.15 = (s32[1,64,3]{1,0,2:T(1,128)S(1)}, s32[1,64,3]{1,0,2:T(1,128)}, u32[]{:S(2)}) copy-start(s32[1,64,3]{1,0,2:T(1,128)} %param.14) | copy-start | bytes 2308
  78.8 14.4 %collective-permute-start.7 = (bf16[16,64,256]{2,1,0:T(8,128)(2,1)}, bf16[16,64,256]{2,1,0:T(8,128)(2,1)S(1)}, u32[]{:S(2)}, u32[]{:S(2)}) collective-permute-start(bf16[16,64,256]{2,1,0:T(8,128)(2,1)} %get-tuple-element.19.rest_2_), channel_id=1, source_target_pairs={{0,32},{32,0},{1,33},{33,1},{2,34},{34,2},{3,35},{35,3},{4,36},{36... | collective-permute-start | bytes 1572872 | tf_op jit(solution)/shard_map/ppermute | solution.py:37
  85.2 8.1 %copy-start.6 = (bf16[4,256,128]{2,1,0:T(8,128)(2,1)}, bf16[4,256,128]{2,1,0:T(8,128)(2,1)S(1)}, u32[]{:S(2)}) copy-start(bf16[4,256,128]{2,1,0:T(8,128)(2,1)S(1)} %all-to-all-done.2.rest_0_) | copy-start | bytes 786436
  85.2 8.1 %copy-start.7 = (bf16[16,64,256]{2,1,0:T(8,128)(2,1)}, bf16[16,64,256]{2,1,0:T(8,128)(2,1)S(1)}, u32[]{:S(2)}) copy-start(bf16[16,64,256]{2,1,0:T(8,128)(2,1)S(1)} %collective-permute-done.6.rest_4_) | copy-start | bytes 1572868
  85.2 8.1 %collective-permute-start.8 = (bf16[16,64,256]{2,1,0:T(8,128)(2,1)S(1)}, bf16[16,64,256]{2,1,0:T(8,128)(2,1)S(1)}, u32[]{:S(2)}, u32[]{:S(2)}) collective-permute-start(bf16[16,64,256]{2,1,0:T(8,128)(2,1)S(1)} %collective-permute-done.6.rest_4_), channel_id=1, source_target_pairs={{0,32},{32,0},{1,33},{33,1},{2,34},{34,2},{3,35},{35,3},{4,36},{36... | collective-permute-start | bytes 1572872 | tf_op jit(solution)/shard_map/ppermute | solution.py:37
  103.7 13.3 %all-to-all-start.3 = ((bf16[8,16,16,128]{3,2,1,0:T(8,128)(2,1)}), bf16[8,16,16,128]{3,2,1,0:T(8,128)(2,1)S(1)}, u32[]{:S(2)}, u32[]{:S(2)}) async-start(bf16[8,16,16,128]{3,2,1,0:T(8,128)(2,1)} %get-tuple-element.24), calls=%async_computation.3 | async-start | bytes 1048576 | tf_op jit(solution)/shard_map/all_to_all | solution.py:261
  108.2 9.6 %collective-permute-start.10 = (bf16[256,128]{1,0:T(8,128)(2,1)S(1)}, bf16[256,128]{1,0:T(8,128)(2,1)S(1)}, u32[]{:S(2)}, u32[]{:S(2)}) collective-permute-start(bf16[256,128]{1,0:T(8,128)(2,1)S(1)} %get-tuple-element.33), channel_id=1, source_target_pairs={{0,64},{64,128},{128,192},{192,0},{1,65},{65,129},{129,193},{193,1... | collective-permute-start | bytes 196616 | tf_op jit(solution)/shard_map/ppermute | solution.py:37
  110.4 7.3 %collective-permute-start.9 = (bf16[256,128]{1,0:T(8,128)(2,1)S(1)}, bf16[256,128]{1,0:T(8,128)(2,1)S(1)}, u32[]{:S(2)}, u32[]{:S(2)}) collective-permute-start(bf16[256,128]{1,0:T(8,128)(2,1)S(1)} %get-tuple-element.34), channel_id=1, source_target_pairs={{0,192},{64,0},{128,64},{192,128},{1,193},{65,1},{129,65},{193,129... | collective-permute-start | bytes 196616 | tf_op jit(solution)/shard_map/ppermute | solution.py:37
  118.4 19.3 %all-to-all-start.4 = ((bf16[16,16,128]{2,1,0:T(8,128)(2,1)}), bf16[16,16,128]{2,1,0:T(8,128)(2,1)S(1)}, u32[]{:S(2)}, u32[]{:S(2)}) async-start(bf16[16,16,128]{2,1,0:T(8,128)(2,1)} %reduce_sum.21), calls=%async_computation.4 | async-start | bytes 131072 | tf_op jit(solution)/shard_map/all_to_all | solution.py:266
  126.2 11.6 %collective-permute-start.11 = (bf16[256,128]{1,0:T(8,128)(2,1)S(1)}, bf16[256,128]{1,0:T(8,128)(2,1)S(1)}, u32[]{:S(2)}, u32[]{:S(2)}) collective-permute-start(bf16[256,128]{1,0:T(8,128)(2,1)S(1)} %get-tuple-element.32), channel_id=1, source_target_pairs={{0,128},{64,192},{128,0},{192,64},{1,129},{65,193},{129,1},{193,65... | collective-permute-start | bytes 196616 | tf_op jit(solution)/shard_map/ppermute | solution.py:37
  138.5 16.2 %all-to-all-start.5 = ((f32[16,16,128]{2,1,0:T(8,128)}), f32[16,16,128]{2,1,0:T(8,128)S(1)}, u32[]{:S(2)}, u32[]{:S(2)}) async-start(f32[16,16,128]{2,1,0:T(8,128)} %broadcast_in_dim.8), calls=%async_computation.5 | async-start | bytes 262144 | tf_op jit(solution)/shard_map/all_to_all | solution.py:30
  (9 other events, 18.0 us)

commit v5 on v4

--- a/solution.py
+++ b/solution.py
@@ -96,8 +96,8 @@
 
 
 def attention_kernel(where_ref, owner_ref, offset_ref, global_ref, *rest):
-    given, pieces, token_refs = rest[:2], rest[2 : 2 + PIECES], rest[2 + PIECES : -8]
-    out_ref, part_ref, kv_ref, g_ref, q_ref, gq_ref, t_ref, sems = rest[-8:]
+    given, pieces, token_refs = rest[:2], rest[2 : 2 + PIECES], rest[2 + PIECES : -9]
+    keep_ref, send_ref, part_ref, kv_ref, g_ref, q_ref, gq_ref, t_ref, sems = rest[-9:]
     pairs = [
         (piece, kv_ref.at[pl.ds(slot * PIECE_BLOCKS, PIECE_BLOCKS)])
         for slot, piece in enumerate(pieces)
@@ -113,9 +113,9 @@
         pltpu.make_async_copy(source, target, sems.at[i])
         for i, (source, target) in enumerate(pairs)
     ]
+    copies, later = copies[:first], copies[first:]
     for copy in copies:
         copy.start()
-    copies, later = copies[:first], copies[first:]
     my_yh, my_x, my_core = where_ref[0], where_ref[1], where_ref[2]
 
     def place(block):
@@ -127,10 +127,13 @@
 
     for copy in copies:
         copy.wait()
+    for copy in later:
+        copy.start()
 
     lane = lax.broadcasted_iota(jnp.int32, (1, 2 * BLK), 1)
     total = PIECES * PIECE_BLOCKS
     scale = HD**-0.5
+    odd = lax.rem(my_x, 2)
 
     def step(inside, carry):
         rows = pl.ds(pl.multiple_of(inside * BLK, BLK), BLK)
@@ -163,9 +166,12 @@
             p = e * (1.0 / jnp.sum(e, axis=1, keepdims=True))
             delta = jnp.sum(p * gp, axis=1, keepdims=True)
             ds = (p * (gp - delta) * scale).astype(jnp.bfloat16)
-            out_ref[slot, rows, :] = dot32(p.astype(jnp.bfloat16), vs[slot], NN).astype(
-                jnp.bfloat16
-            )
+            out = dot32(p.astype(jnp.bfloat16), vs[slot], NN).astype(jnp.bfloat16)
+            if slot % 2 == 0:
+                keep_ref[slot // 2, rows, :] = out
+            else:
+                near = 1 - odd if slot == 1 else odd
+                send_ref[near, rows, :] = out
             gq_ref[slot, rows, :] = dot32(ds, ks[slot], NN).astype(jnp.bfloat16)
         return carry
 
@@ -192,12 +198,13 @@
     return pl.pallas_call(
         attention_kernel,
         out_shape=(
-            jax.ShapeDtypeStruct(grads.shape, jnp.bfloat16),
+            jax.ShapeDtypeStruct((2, *grads.shape[1:]), jnp.bfloat16),
+            jax.ShapeDtypeStruct((2, *grads.shape[1:]), jnp.bfloat16),
             jax.ShapeDtypeStruct((8, 16, 16, HD), jnp.bfloat16),
         ),
         in_specs=[smem] * 4
         + [pl.BlockSpec(memory_space=pl.ANY)] * (2 + PIECES + len(token_sets)),
-        out_specs=(vmem, vmem),
+        out_specs=(vmem,) * 3,
         scratch_shapes=[
             pltpu.VMEM((PIECES * PIECE_BLOCKS, BLK, 2 * HD), jnp.bfloat16),
             pltpu.VMEM(grads.shape, jnp.bfloat16),
@@ -211,11 +218,19 @@
     )(where, owners, offsets, global_list, grads, queries, *pieces, *token_sets)
 
 
-def merge_kernel(where_ref, *refs):
-    out_ref = refs[-1]
-    for slot, ref in enumerate(refs[:-1]):
-        head = lax.rem(where_ref[1] + slot, HEADS)
+def merge_kernel(where_ref, keep_ref, next_ref, far_ref, out_ref):
+    x = where_ref[1]
+    odd, high = lax.rem(x, 2), x // 2
+    parts = (keep_ref.at[0], next_ref.at[0], far_ref.at[0], far_ref.at[1])
+    for flip, ref in enumerate(parts):
+        low = odd if flip % 2 == 0 else 1 - odd
+        top = high if flip < 2 else 1 - high
+        head = top * 2 + low
         out_ref[:, pl.ds(pl.multiple_of(head * HD, HD), HD)] = ref[...]
+
+
+def exchanged(block, flip):
+    return lax.ppermute(block, "x", [(i, i ^ flip) for i in range(HEADS)])
 
 
 def per_device(
@@ -254,25 +269,24 @@
     across, grads = lax.optimization_barrier((across, grads))
     pieces = [kv, shifted(kv, "core", 1), across, shifted(across, "core", 1)]
 
-    attended, partial = attention(
+    kept, sent, partial = attention(
         where, rand_owner[0], rand_offset[0], global_ids, grads, queries, pieces, token_sets
     )
-    returned = [attended[0]] + [shifted(attended[s], "x", -s) for s in range(1, HEADS)]
+    from_next = exchanged(sent, 1)
     partial = lax.all_to_all(partial, ("yh", "yl", "core"), 0, 0, tiled=True)
     partial = jnp.sum(partial.astype(jnp.float32), axis=0).astype(jnp.bfloat16)
-    partial, returned[1], returned[3] = lax.optimization_barrier(
-        (partial, returned[1], returned[3])
-    )
+    partial, from_next = lax.optimization_barrier((partial, from_next))
+    from_far = exchanged(jnp.stack([kept[1], from_next[1]]), 2)
     partial = lax.all_to_all(partial, "z", 0, 0, tiled=True)
     partial = jnp.sum(partial.astype(jnp.float32), axis=0)
-    partial, returned[2] = lax.optimization_barrier((partial, returned[2]))
+    partial, from_far = lax.optimization_barrier((partial, from_far))
     attn = pl.pallas_call(
         merge_kernel,
         out_shape=jax.ShapeDtypeStruct((count, HEADS * HD), jnp.bfloat16),
-        in_specs=[smem] + [vmem] * HEADS,
+        in_specs=[smem] + [vmem] * 3,
         out_specs=vmem,
         name="merge",
-    )(where, *returned)
+    )(where, kept, from_next, from_far)
 
     final = spread(partial, ("yh", "x", "core")).reshape(2, 4, 2, rows, HD)
     query_grad = final.transpose(0, 2, 3, 1, 4).reshape(4 * rows, HEADS * HD)

time: 157 us -> 153 us (0.975)
  starting transfers between devices: 78.5 us -> 71.3 us
  waiting for transfers between devices: 19.5 us -> 24.5 us
    ppermute x12 -> x9, starting transfers between devices: 49.8 us -> 41.1 us  [shifted(): lax.ppermute(block, axis, [(i, (i + step) % count) for i in range(count)])]
    all_to_all x1, waiting for transfers between devices: 2.32 us -> 7.3 us  [per_device(): partial = lax.all_to_all(partial, ('yh', 'yl', 'core'), 0, 0, tiled=True)]
    ppermute x0 -> x2, starting transfers between devices: none -> 4.38 us  [exchanged(): return lax.ppermute(block, 'x', [(i, i ^ flip) for i in range(HEADS)])]
    all_to_all x2, starting transfers between devices: 12.8 us -> 9.77 us  [spread(): lax.all_to_all(jnp.broadcast_to(block[None], (count, *block.shape)), axes...]
  transfers between devices with their start and end apart: 17 -> 16, of which waited for: 6 -> 6; matrix products, arithmetic and copies ran while one was open for 5% -> 4% of each run, Pallas kernels for 2% -> 2%
where the time goes in v5:
time: 153 us; the launch traced here: 152 us
  starting transfers between devices  71.3 us (47%)
  blocking collectives  27.3 us (18%)
  waiting for transfers between devices  24.5 us (16%)
  Pallas kernels  17.4 us (11%)
  local copies, waits for them, and re-layouts  9.26 us (6%)
    ppermute x9, starting transfers between devices, shifted(): lax.ppermute(block, axis, [(i, (i + step) % count) for i in range(count)])  41.1 us
    all_to_all x1, blocking collectives, per_device(): weight = lax.all_to_all(weight, 'z', 0, 0, tiled=True)  27.3 us
    all_to_all x2, starting transfers between devices, spread(): lax.all_to_all(jnp.broadcast_to(block[None], (count, *block.shape)), axes...  9.77 us
    pallas_call x1, Pallas kernels, attention(): pl.pallas_call(attention_kernel, out_shape=(jax.ShapeDtypeStruct((2, *gra...  9.54 us
    all_to_all x1, waiting for transfers between devices, per_device(): partial = lax.all_to_all(partial, 'z', 0, 0, tiled=True)  9.32 us
    all_to_all x1, starting transfers between devices, per_device(): partial = lax.all_to_all(partial, 'z', 0, 0, tiled=True)  7.88 us
    all_to_all x1, waiting for transfers between devices, per_device(): partial = lax.all_to_all(partial, ('yh', 'yl', 'core'), 0, 0, tiled=True)  7.3 us
    all_to_all x2, waiting for transfers between devices, spread(): lax.all_to_all(jnp.broadcast_to(block[None], (count, *block.shape)), axes...  6.07 us
  transfers between devices with their start and end apart: 16, of which 6 were waited for; matrix products, arithmetic and copies ran while one was open for 4% of the time, Pallas kernels for 2%

profile of v5, /device:TPU:1, one launch (start us, length us, event | category | flops | bytes accessed | tf_op | source)
XLA Modules:
  0.0 152.0 jit_solution(18251451604653367859)
XLA Ops:
  0.6 5.2 %collective-permute-start.1 = (bf16[256,2048]{1,0:T(8,128)(2,1)}, bf16[256,2048]{1,0:T(8,128)(2,1)S(1)}, u32[]{:S(2)}, u32[]{:S(2)}) collective-permute-start(bf16[256,2048]{1,0:T(8,128)(2,1)} %bitcast.19), channel_id=1, source_target_pairs={{0,192},{64,0},{128,64},{192,128},{1,193},{65,1},{129,65},{193,129... | collective-permute-start | bytes 3145736 | tf_op jit(solution)/shard_map/ppermute | solution.py:37
  5.9 1.9 %collective-permute-start = (bf16[256,2048]{1,0:T(8,128)(2,1)}, bf16[256,2048]{1,0:T(8,128)(2,1)S(1)}, u32[]{:S(2)}, u32[]{:S(2)}) collective-permute-start(bf16[256,2048]{1,0:T(8,128)(2,1)} %bitcast.20), channel_id=1, source_target_pairs={{0,64},{64,128},{128,192},{192,0},{1,65},{65,129},{129,193},{193,1... | collective-permute-start | bytes 3145736 | tf_op jit(solution)/shard_map/ppermute | solution.py:37
  10.0 27.3 %all_to_all.30 = bf16[16,16,384]{2,1,0:T(8,128)(2,1)S(1)} all-to-all(bf16[16,16,384]{2,1,0:T(8,128)(2,1)} %slice.19), channel_id=1, replica_groups=mesh['yh'=2,'x'=4,'core'=2,'z'=16,'yl'=2] {'z'}, dimensions={0} | all-to-all | bytes 393216 | tf_op jit(solution)/shard_map/all_to_all | solution.py:255
  38.4 4.2 %all-to-all-start.1 = ((bf16[4,16,16,384]{3,2,1,0:T(8,128)(2,1)}), bf16[4,16,16,384]{3,2,1,0:T(8,128)(2,1)S(1)}, u32[]{:S(2)}, u32[]{:S(2)}) async-start(bf16[4,16,16,384]{3,2,1,0:T(8,128)(2,1)} %broadcast_in_dim.6), calls=%async_computation.1 | async-start | bytes 1572864 | tf_op jit(solution)/shard_map/all_to_all | solution.py:30
  44.2 4.5 %collective-permute-start.5 = (bf16[128,2048]{1,0:T(8,128)(2,1)}, bf16[128,2048]{1,0:T(8,128)(2,1)S(1)}, u32[]{:S(2)}, u32[]{:S(2)}) collective-permute-start(bf16[128,2048]{1,0:T(8,128)(2,1)} %slice.16), channel_id=1, source_target_pairs={{0,192},{64,0},{128,64},{192,128},{1,193},{65,1},{129,65},{193,129... | collective-permute-start | bytes 1572872 | tf_op jit(solution)/shard_map/ppermute | solution.py:37
  48.8 1.9 %collective-permute-start.4 = (bf16[128,2048]{1,0:T(8,128)(2,1)}, bf16[128,2048]{1,0:T(8,128)(2,1)}, u32[]{:S(2)}, u32[]{:S(2)}) collective-permute-start(bf16[128,2048]{1,0:T(8,128)(2,1)} %slice.15), channel_id=1, source_target_pairs={{0,64},{64,128},{128,192},{192,0},{1,65},{65,129},{129,193},{193,1... | collective-permute-start | bytes 1572872 | tf_op jit(solution)/shard_map/ppermute | solution.py:37
  51.0 8.6 %collective-permute-start.3 = (bf16[2,16,16,384]{3,2,1,0:T(8,128)(2,1)S(1)}, bf16[2,16,16,384]{3,2,1,0:T(8,128)(2,1)S(1)}, u32[]{:S(2)}, u32[]{:S(2)}) collective-permute-start(bf16[2,16,16,384]{3,2,1,0:T(8,128)(2,1)S(1)} %get-tuple-element.30), channel_id=1, source_target_pairs={{0,32},{32,0},{1,33},{33,1},{2,34},{34,2},{3,35},{35,3},{4,36},{36... | collective-permute-start | bytes 1179656 | tf_op jit(solution)/shard_map/ppermute | solution.py:37
  59.5 1.9 %collective-permute-start.2 = (bf16[2,16,16,384]{3,2,1,0:T(8,128)(2,1)S(1)}, bf16[2,16,16,384]{3,2,1,0:T(8,128)(2,1)S(1)}, u32[]{:S(2)}, u32[]{:S(2)}) collective-permute-start(bf16[2,16,16,384]{3,2,1,0:T(8,128)(2,1)S(1)} %get-tuple-element.31), channel_id=1, source_target_pairs={{0,32},{32,0},{1,33},{33,1},{2,34},{34,2},{3,35},{35,3},{4,36},{36... | collective-permute-start | bytes 1179656 | tf_op jit(solution)/shard_map/ppermute | solution.py:37
  61.5 1.6 %collective-permute-done.2.theirs_a_ref = bf16[2,16,16,384]{3,2,1,0:T(8,128)(2,1)S(1)} collective-permute-done((bf16[2,16,16,384]{3,2,1,0:T(8,128)(2,1)S(1)}, bf16[2,16,16,384]{3,2,1,0:T(8,128)(2,1)S(1)}, u32[]{:S(2)}, u32[]{:S(2)}) %collective-permute-start.2) | collective-permute-done | bytes 393248 | tf_op jit(solution)/shard_map/ppermute | solution.py:37
  63.2 4.5 %project.1 = (bf16[1024,128]{1,0:T(8,128)(2,1)S(1)}, bf16[16,64,256]{2,1,0:T(8,128)(2,1)}) custom-call(s32[3]{0:T(128)S(1)} %copy-done.5, bf16[2,2,16,16,384]{4,3,2,1,0:T(8,128)(2,1)S(1)} %bitcast.18, bf16[2,16,16,384]{3,2,1,0:T(8,128)(2,1)S(1)} %collective-permute-done.2.theirs_a_ref, bf16[2,16,16,384]{3,2,1,0:T(8,128)(2,1)S(1)} %collective-permute-done.3.theirs_b_ref, ...), custom_call_target="tpu_custom_call" | custom-call | tf_op jit(solution)/shard_map/project/pallas_call | solution.py:84
  68.4 4.2 %collective-permute-start.6 = (bf16[16,64,256]{2,1,0:T(8,128)(2,1)}, bf16[16,64,256]{2,1,0:T(8,128)(2,1)S(1)}, u32[]{:S(2)}, u32[]{:S(2)}) collective-permute-start(bf16[16,64,256]{2,1,0:T(8,128)(2,1)} %get-tuple-element.19.rest_2_), channel_id=1, source_target_pairs={{0,256},{256,0},{1,257},{257,1},{2,258},{258,2},{3,259},{259,3},{4... | collective-permute-start | bytes 1572872 | tf_op jit(solution)/shard_map/ppermute | solution.py:37
  74.5 4.3 %all-to-all-start.2 = ((bf16[4,256,128]{2,1,0:T(8,128)(2,1)}), bf16[4,256,128]{2,1,0:T(8,128)(2,1)S(1)}, u32[]{:S(2)}, u32[]{:S(2)}) async-start(bf16[4,256,128]{2,1,0:T(8,128)(2,1)} %bitcast.8), calls=%async_computation.2 | async-start | bytes 524288 | tf_op jit(solution)/shard_map/all_to_all | solution.py:265
  78.8 6.3 %collective-permute-start.7 = (bf16[16,64,256]{2,1,0:T(8,128)(2,1)}, bf16[16,64,256]{2,1,0:T(8,128)(2,1)S(1)}, u32[]{:S(2)}, u32[]{:S(2)}) collective-permute-start(bf16[16,64,256]{2,1,0:T(8,128)(2,1)} %get-tuple-element.19.rest_2_), channel_id=1, source_target_pairs={{0,32},{32,0},{1,33},{33,1},{2,34},{34,2},{3,35},{35,3},{4,36},{36... | collective-permute-start | bytes 1572872 | tf_op jit(solution)/shard_map/ppermute | solution.py:37
  85.2 6.6 %collective-permute-start.8 = (bf16[16,64,256]{2,1,0:T(8,128)(2,1)S(1)}, bf16[16,64,256]{2,1,0:T(8,128)(2,1)S(1)}, u32[]{:S(2)}, u32[]{:S(2)}) collective-permute-start(bf16[16,64,256]{2,1,0:T(8,128)(2,1)S(1)} %collective-permute-done.6.rest_4_), channel_id=1, source_target_pairs={{0,32},{32,0},{1,33},{33,1},{2,34},{34,2},{3,35},{35,3},{4,36},{36... | collective-permute-start | bytes 1572872 | tf_op jit(solution)/shard_map/ppermute | solution.py:37
  94.2 9.5 %attention.1 = (bf16[2,256,128]{2,1,0:T(8,128)(2,1)}, bf16[2,256,128]{2,1,0:T(8,128)(2,1)}, bf16[8,16,16,128]{3,2,1,0:T(8,128)(2,1)}) custom-call(s32[3]{0:T(128)} %pad_add_fusion.where_ref, s32[64,3]{1,0:T(8,128)} %bitcast.27, s32[64,3]{1,0:T(8,128)} %bitcast.28, s32[1,2]{1,0:T(1,128)} %global_ref.1, bf16[4,256,128]{2,1,0:T(8,128)(2,1)} %copy-done.6, ...), custom_call_target="tpu_custom_call" | custom-call | tf_op jit(solution)/shard_map/attention/pallas_call | solution.py:198
  103.8 3.8 %all-to-all-start.3 = ((bf16[8,16,16,128]{3,2,1,0:T(8,128)(2,1)}), bf16[8,16,16,128]{3,2,1,0:T(8,128)(2,1)S(1)}, u32[]{:S(2)}, u32[]{:S(2)}) async-start(bf16[8,16,16,128]{3,2,1,0:T(8,128)(2,1)} %get-tuple-element.24), calls=%async_computation.3 | async-start | bytes 1048576 | tf_op jit(solution)/shard_map/all_to_all | solution.py:276
  107.6 2.2 %collective-permute-start.9 = (bf16[2,256,128]{2,1,0:T(8,128)(2,1)S(1)}, bf16[2,256,128]{2,1,0:T(8,128)(2,1)S(1)}, u32[]{:S(2)}, u32[]{:S(2)}) collective-permute-start(bf16[2,256,128]{2,1,0:T(8,128)(2,1)S(1)} %copy-done.15), channel_id=1, source_target_pairs={{0,64},{64,0},{128,192},{192,128},{1,65},{65,1},{129,193},{193,129... | collective-permute-start | bytes 393224 | tf_op jit(solution)/shard_map/ppermute | solution.py:233
  109.8 7.3 %all-to-all-done.3 = bf16[8,16,16,128]{3,2,1,0:T(8,128)(2,1)S(1)} async-done(((bf16[8,16,16,128]{3,2,1,0:T(8,128)(2,1)}), bf16[8,16,16,128]{3,2,1,0:T(8,128)(2,1)S(1)}, u32[]{:S(2)}, u32[]{:S(2)}) %all-to-all-start.3) | async-done | bytes 524320 | tf_op jit(solution)/shard_map/all_to_all | solution.py:276
  117.8 7.9 %all-to-all-start.4 = ((bf16[16,16,128]{2,1,0:T(8,128)(2,1)}), bf16[16,16,128]{2,1,0:T(8,128)(2,1)S(1)}, u32[]{:S(2)}, u32[]{:S(2)}) async-start(bf16[16,16,128]{2,1,0:T(8,128)(2,1)} %reduce_sum.21), calls=%async_computation.4 | async-start | bytes 131072 | tf_op jit(solution)/shard_map/all_to_all | solution.py:280
  125.7 2.2 %collective-permute-start.10 = (bf16[2,256,128]{2,1,0:T(8,128)(2,1)S(1)}, bf16[2,256,128]{2,1,0:T(8,128)(2,1)S(1)}, u32[]{:S(2)}, u32[]{:S(2)}) collective-permute-start(bf16[2,256,128]{2,1,0:T(8,128)(2,1)S(1)} %pad_maximum_fusion), channel_id=1, source_target_pairs={{0,128},{64,192},{128,0},{192,64},{1,129},{65,193},{129,1},{193,65... | collective-permute-start | bytes 393224 | tf_op jit(solution)/shard_map/ppermute | solution.py:233
  127.9 9.3 %all-to-all-done.4 = bf16[16,16,128]{2,1,0:T(8,128)(2,1)S(1)} async-done(((bf16[16,16,128]{2,1,0:T(8,128)(2,1)}), bf16[16,16,128]{2,1,0:T(8,128)(2,1)S(1)}, u32[]{:S(2)}, u32[]{:S(2)}) %all-to-all-start.4) | async-done | bytes 65568 | tf_op jit(solution)/shard_map/all_to_all | solution.py:280
  138.0 5.6 %all-to-all-start.5 = ((f32[16,16,128]{2,1,0:T(8,128)}), f32[16,16,128]{2,1,0:T(8,128)S(1)}, u32[]{:S(2)}, u32[]{:S(2)}) async-start(f32[16,16,128]{2,1,0:T(8,128)} %broadcast_in_dim.8), calls=%async_computation.5 | async-start | bytes 262144 | tf_op jit(solution)/shard_map/all_to_all | solution.py:30
  143.6 1.8 %merge.1 = bf16[256,512]{1,0:T(8,128)(2,1)} custom-call(s32[3]{0:T(128)} %pad_add_fusion.where_ref, bf16[2,256,128]{2,1,0:T(8,128)(2,1)} %get-tuple-element.23.keep_ref, bf16[2,256,128]{2,1,0:T(8,128)(2,1)} %copy-done.11, bf16[2,256,128]{2,1,0:T(8,128)(2,1)} %copy-done.12), custom_call_target="tpu_custom_call" | custom-call | tf_op jit(solution)/shard_map/merge/pallas_call | solution.py:283
  145.4 5.9 %all-to-all-done.5 = f32[16,16,128]{2,1,0:T(8,128)S(1)} async-done(((f32[16,16,128]{2,1,0:T(8,128)}), f32[16,16,128]{2,1,0:T(8,128)S(1)}, u32[]{:S(2)}, u32[]{:S(2)}) %all-to-all-start.5) | async-done | bytes 131104 | tf_op jit(solution)/shard_map/all_to_all | solution.py:30
  (62 shorter events, 12.5 us)
Async XLA Ops:
  0.6 36.7 %collective-permute-start.1 = (bf16[256,2048]{1,0:T(8,128)(2,1)}, bf16[256,2048]{1,0:T(8,128)(2,1)S(1)}, u32[]{:S(2)}, u32[]{:S(2)}) collective-permute-start(bf16[256,2048]{1,0:T(8,128)(2,1)} %bitcast.19), channel_id=1, source_target_pairs={{0,192},{64,0},{128,64},{192,128},{1,193},{65,1},{129,65},{193,129... | collective-permute-start | bytes 3145736 | tf_op jit(solution)/shard_map/ppermute | solution.py:37
  5.9 31.4 %collective-permute-start = (bf16[256,2048]{1,0:T(8,128)(2,1)}, bf16[256,2048]{1,0:T(8,128)(2,1)S(1)}, u32[]{:S(2)}, u32[]{:S(2)}) collective-permute-start(bf16[256,2048]{1,0:T(8,128)(2,1)} %bitcast.20), channel_id=1, source_target_pairs={{0,64},{64,128},{128,192},{192,0},{1,65},{65,129},{129,193},{193,1... | collective-permute-start | bytes 3145736 | tf_op jit(solution)/shard_map/ppermute | solution.py:37
  37.3 25.9 %copy-start = (bf16[256,2048]{1,0:T(8,128)(2,1)}, bf16[256,2048]{1,0:T(8,128)(2,1)S(1)}, u32[]{:S(2)}) copy-start(bf16[256,2048]{1,0:T(8,128)(2,1)S(1)} %collective-permute-done.1.rest_2_.rest_8_) | copy-start | bytes 3145732
  37.3 25.9 %copy-start.1 = (bf16[256,2048]{1,0:T(8,128)(2,1)}, bf16[256,2048]{1,0:T(8,128)(2,1)S(1)}, u32[]{:S(2)}) copy-start(bf16[256,2048]{1,0:T(8,128)(2,1)S(1)} %collective-permute-done.rest_1_.rest_7_) | copy-start | bytes 3145732
  38.4 12.5 %all-to-all-start.1 = ((bf16[4,16,16,384]{3,2,1,0:T(8,128)(2,1)}), bf16[4,16,16,384]{3,2,1,0:T(8,128)(2,1)S(1)}, u32[]{:S(2)}, u32[]{:S(2)}) async-start(bf16[4,16,16,384]{3,2,1,0:T(8,128)(2,1)} %broadcast_in_dim.6), calls=%async_computation.1 | async-start | bytes 1572864 | tf_op jit(solution)/shard_map/all_to_all | solution.py:30
  44.2 17.3 %collective-permute-start.5 = (bf16[128,2048]{1,0:T(8,128)(2,1)}, bf16[128,2048]{1,0:T(8,128)(2,1)S(1)}, u32[]{:S(2)}, u32[]{:S(2)}) collective-permute-start(bf16[128,2048]{1,0:T(8,128)(2,1)} %slice.16), channel_id=1, source_target_pairs={{0,192},{64,0},{128,64},{192,128},{1,193},{65,1},{129,65},{193,129... | collective-permute-start | bytes 1572872 | tf_op jit(solution)/shard_map/ppermute | solution.py:37
  48.8 12.7 %collective-permute-start.4 = (bf16[128,2048]{1,0:T(8,128)(2,1)}, bf16[128,2048]{1,0:T(8,128)(2,1)}, u32[]{:S(2)}, u32[]{:S(2)}) collective-permute-start(bf16[128,2048]{1,0:T(8,128)(2,1)} %slice.15), channel_id=1, source_target_pairs={{0,64},{64,128},{128,192},{192,0},{1,65},{65,129},{129,193},{193,1... | collective-permute-start | bytes 1572872 | tf_op jit(solution)/shard_map/ppermute | solution.py:37
  50.9 12.3 %copy-start.2 = (bf16[1,256,2048]{2,1,0:T(8,128)(2,1)S(1)}, bf16[1,256,2048]{2,1,0:T(8,128)(2,1)}, u32[]{:S(2)}) copy-start(bf16[1,256,2048]{2,1,0:T(8,128)(2,1)} %param.8) | copy-start | bytes 3145732
  51.0 10.5 %collective-permute-start.3 = (bf16[2,16,16,384]{3,2,1,0:T(8,128)(2,1)S(1)}, bf16[2,16,16,384]{3,2,1,0:T(8,128)(2,1)S(1)}, u32[]{:S(2)}, u32[]{:S(2)}) collective-permute-start(bf16[2,16,16,384]{3,2,1,0:T(8,128)(2,1)S(1)} %get-tuple-element.30), channel_id=1, source_target_pairs={{0,32},{32,0},{1,33},{33,1},{2,34},{34,2},{3,35},{35,3},{4,36},{36... | collective-permute-start | bytes 1179656 | tf_op jit(solution)/shard_map/ppermute | solution.py:37
  59.5 3.6 %collective-permute-start.2 = (bf16[2,16,16,384]{3,2,1,0:T(8,128)(2,1)S(1)}, bf16[2,16,16,384]{3,2,1,0:T(8,128)(2,1)S(1)}, u32[]{:S(2)}, u32[]{:S(2)}) collective-permute-start(bf16[2,16,16,384]{3,2,1,0:T(8,128)(2,1)S(1)} %get-tuple-element.31), channel_id=1, source_target_pairs={{0,32},{32,0},{1,33},{33,1},{2,34},{34,2},{3,35},{35,3},{4,36},{36... | collective-permute-start | bytes 1179656 | tf_op jit(solution)/shard_map/ppermute | solution.py:37
  68.4 16.8 %collective-permute-start.6 = (bf16[16,64,256]{2,1,0:T(8,128)(2,1)}, bf16[16,64,256]{2,1,0:T(8,128)(2,1)S(1)}, u32[]{:S(2)}, u32[]{:S(2)}) collective-permute-start(bf16[16,64,256]{2,1,0:T(8,128)(2,1)} %get-tuple-element.19.rest_2_), channel_id=1, source_target_pairs={{0,256},{256,0},{1,257},{257,1},{2,258},{258,2},{3,259},{259,3},{4... | collective-permute-start | bytes 1572872 | tf_op jit(solution)/shard_map/ppermute | solution.py:37
  74.5 17.3 %copy-start.13 = (s32[1,64,3]{1,0,2:T(1,128)S(1)}, s32[1,64,3]{1,0,2:T(1,128)}, u32[]{:S(2)}) copy-start(s32[1,64,3]{1,0,2:T(1,128)} %param.13) | copy-start | bytes 2308
  74.5 10.7 %all-to-all-start.2 = ((bf16[4,256,128]{2,1,0:T(8,128)(2,1)}), bf16[4,256,128]{2,1,0:T(8,128)(2,1)S(1)}, u32[]{:S(2)}, u32[]{:S(2)}) async-start(bf16[4,256,128]{2,1,0:T(8,128)(2,1)} %bitcast.8), calls=%async_computation.2 | async-start | bytes 524288 | tf_op jit(solution)/shard_map/all_to_all | solution.py:265
  78.8 13.7 %copy-start.14 = (s32[1,64,3]{1,0,2:T(1,128)S(1)}, s32[1,64,3]{1,0,2:T(1,128)}, u32[]{:S(2)}) copy-start(s32[1,64,3]{1,0,2:T(1,128)} %param.14) | copy-start | bytes 2308
  78.8 14.4 %collective-permute-start.7 = (bf16[16,64,256]{2,1,0:T(8,128)(2,1)}, bf16[16,64,256]{2,1,0:T(8,128)(2,1)S(1)}, u32[]{:S(2)}, u32[]{:S(2)}) collective-permute-start(bf16[16,64,256]{2,1,0:T(8,128)(2,1)} %get-tuple-element.19.rest_2_), channel_id=1, source_target_pairs={{0,32},{32,0},{1,33},{33,1},{2,34},{34,2},{3,35},{35,3},{4,36},{36... | collective-permute-start | bytes 1572872 | tf_op jit(solution)/shard_map/ppermute | solution.py:37
  85.1 8.1 %copy-start.6 = (bf16[4,256,128]{2,1,0:T(8,128)(2,1)}, bf16[4,256,128]{2,1,0:T(8,128)(2,1)S(1)}, u32[]{:S(2)}) copy-start(bf16[4,256,128]{2,1,0:T(8,128)(2,1)S(1)} %all-to-all-done.2.rest_0_) | copy-start | bytes 786436
  85.2 8.1 %copy-start.7 = (bf16[16,64,256]{2,1,0:T(8,128)(2,1)}, bf16[16,64,256]{2,1,0:T(8,128)(2,1)S(1)}, u32[]{:S(2)}) copy-start(bf16[16,64,256]{2,1,0:T(8,128)(2,1)S(1)} %collective-permute-done.6.rest_4_) | copy-start | bytes 1572868
  85.2 8.1 %collective-permute-start.8 = (bf16[16,64,256]{2,1,0:T(8,128)(2,1)S(1)}, bf16[16,64,256]{2,1,0:T(8,128)(2,1)S(1)}, u32[]{:S(2)}, u32[]{:S(2)}) collective-permute-start(bf16[16,64,256]{2,1,0:T(8,128)(2,1)S(1)} %collective-permute-done.6.rest_4_), channel_id=1, source_target_pairs={{0,32},{32,0},{1,33},{33,1},{2,34},{34,2},{3,35},{35,3},{4,36},{36... | collective-permute-start | bytes 1572872 | tf_op jit(solution)/shard_map/ppermute | solution.py:37
  103.8 13.3 %all-to-all-start.3 = ((bf16[8,16,16,128]{3,2,1,0:T(8,128)(2,1)}), bf16[8,16,16,128]{3,2,1,0:T(8,128)(2,1)S(1)}, u32[]{:S(2)}, u32[]{:S(2)}) async-start(bf16[8,16,16,128]{3,2,1,0:T(8,128)(2,1)} %get-tuple-element.24), calls=%async_computation.3 | async-start | bytes 1048576 | tf_op jit(solution)/shard_map/all_to_all | solution.py:276
  107.6 10.2 %collective-permute-start.9 = (bf16[2,256,128]{2,1,0:T(8,128)(2,1)S(1)}, bf16[2,256,128]{2,1,0:T(8,128)(2,1)S(1)}, u32[]{:S(2)}, u32[]{:S(2)}) collective-permute-start(bf16[2,256,128]{2,1,0:T(8,128)(2,1)S(1)} %copy-done.15), channel_id=1, source_target_pairs={{0,64},{64,0},{128,192},{192,128},{1,65},{65,1},{129,193},{193,129... | collective-permute-start | bytes 393224 | tf_op jit(solution)/shard_map/ppermute | solution.py:233
  117.8 7.9 %copy-start.11 = (bf16[2,256,128]{2,1,0:T(8,128)(2,1)}, bf16[2,256,128]{2,1,0:T(8,128)(2,1)S(1)}, u32[]{:S(2)}) copy-start(bf16[2,256,128]{2,1,0:T(8,128)(2,1)S(1)} %collective-permute-done.9.next_ref) | copy-start | bytes 393220
  117.8 19.5 %all-to-all-start.4 = ((bf16[16,16,128]{2,1,0:T(8,128)(2,1)}), bf16[16,16,128]{2,1,0:T(8,128)(2,1)S(1)}, u32[]{:S(2)}, u32[]{:S(2)}) async-start(bf16[16,16,128]{2,1,0:T(8,128)(2,1)} %reduce_sum.21), calls=%async_computation.4 | async-start | bytes 131072 | tf_op jit(solution)/shard_map/all_to_all | solution.py:280
  125.7 11.5 %collective-permute-start.10 = (bf16[2,256,128]{2,1,0:T(8,128)(2,1)S(1)}, bf16[2,256,128]{2,1,0:T(8,128)(2,1)S(1)}, u32[]{:S(2)}, u32[]{:S(2)}) collective-permute-start(bf16[2,256,128]{2,1,0:T(8,128)(2,1)S(1)} %pad_maximum_fusion), channel_id=1, source_target_pairs={{0,128},{64,192},{128,0},{192,64},{1,129},{65,193},{129,1},{193,65... | collective-permute-start | bytes 393224 | tf_op jit(solution)/shard_map/ppermute | solution.py:233
  138.0 13.3 %all-to-all-start.5 = ((f32[16,16,128]{2,1,0:T(8,128)}), f32[16,16,128]{2,1,0:T(8,128)S(1)}, u32[]{:S(2)}, u32[]{:S(2)}) async-start(f32[16,16,128]{2,1,0:T(8,128)} %broadcast_in_dim.8), calls=%async_computation.5 | async-start | bytes 262144 | tf_op jit(solution)/shard_map/all_to_all | solution.py:30
  (8 other events, 24.7 us)

commit v6 on v5

--- a/solution.py
+++ b/solution.py
@@ -1,3 +1,5 @@
+import functools
+
 import jax
 import jax.numpy as jnp
 from jax import lax
@@ -37,7 +39,10 @@
     return lax.ppermute(block, axis, [(i, (i + step) % count) for i in range(count)])
 
 
-def slice_kernel(where_ref, key_ref, value_ref, query_ref, out_ref):
+def slice_kernel(where_ref, key_ref, value_ref, query_ref, grad_ref, out_ref, *grad_outs):
+    for hop, ref in enumerate(grad_outs):
+        head = lax.rem(where_ref[1] + hop, HEADS)
+        ref[...] = grad_ref[:, pl.ds(pl.multiple_of(head * HD, HD), HD)]
     count, rows, _ = out_ref.shape
     start = pl.multiple_of((where_ref[0] * 2 + where_ref[2]) * rows, rows)
     col = pl.multiple_of(where_ref[1] * HD, HD)
@@ -47,9 +52,9 @@
             out_ref[copy, :, i * HD : (i + 1) * HD] = part
 
 
-def project_kernel(where_ref, mine_ref, theirs_a_ref, theirs_b_ref, *rest):
+def project_kernel(cols, where_ref, mine_ref, theirs_a_ref, theirs_b_ref, *rest):
     theirs = (theirs_a_ref, theirs_b_ref)
-    token_refs, (q_ref, kv_ref, w_ref) = rest[:-3], rest[-3:]
+    token_refs, (out_ref, w_ref) = rest[:-2], rest[-2:]
     core = where_ref[2]
     _, _, depth, rows, width = mine_ref.shape
 
@@ -59,8 +64,8 @@
                 base = (z * 2 + yl) * 4 * rows + yh * 2 * rows
                 here = pl.multiple_of(base + core * rows, rows)
                 there = pl.multiple_of(base + (1 - core) * rows, rows)
-                w_ref[pl.ds(here, rows), :] = mine_ref[yh, yl, z]
-                w_ref[pl.ds(there, rows), :] = theirs[yh][yl, z]
+                w_ref[pl.ds(here, rows), :] = mine_ref[yh, yl, z, :, cols]
+                w_ref[pl.ds(there, rows), :] = theirs[yh][yl, z, :, cols]
         return carry
 
     lax.fori_loop(0, depth, assemble, 0)
@@ -68,8 +73,7 @@
         tokens = jnp.concatenate([ref[...] for ref in group], axis=0)
         size = tokens.shape[0]
         out = dot32(tokens, w_ref[...], NN).astype(jnp.bfloat16)
-        kv_ref[slot * NBL : (slot + 1) * NBL] = out[:, : 2 * HD].reshape(NBL, BLK, 2 * HD)
-        q_ref[slot * size : (slot + 1) * size, :] = out[:, 2 * HD :]
+        out_ref[slot * size : (slot + 1) * size, :] = out
 
 
 def token_groups(refs):
@@ -77,32 +81,36 @@
     return [(0, (own,)), (1, (before,)), (3, (after,)), (2, (low_far, high_far))]
 
 
-def project(where, mine, theirs_a, theirs_b, token_sets):
+def project(name, cols, where, mine, theirs_a, theirs_b, token_sets):
     count, depth = token_sets[0].shape
-    total = count * HEADS
+    total, width = count * HEADS, cols.stop - cols.start
     vmem = pl.BlockSpec(memory_space=pltpu.VMEM)
     return pl.pallas_call(
-        project_kernel,
-        out_shape=(
-            jax.ShapeDtypeStruct((total, HD), jnp.bfloat16),
-            jax.ShapeDtypeStruct((PIECE_BLOCKS, BLK, 2 * HD), jnp.bfloat16),
+        functools.partial(project_kernel, cols),
+        out_shape=jax.ShapeDtypeStruct((total, width), jnp.bfloat16),
+        in_specs=[pl.BlockSpec(memory_space=pltpu.SMEM)] + [vmem] * (3 + len(token_sets)),
+        out_specs=vmem,
+        scratch_shapes=[pltpu.VMEM((depth, width), jnp.bfloat16)],
+        compiler_params=pltpu.CompilerParams(vmem_limit_bytes=24 * 1024 * 1024),
+        cost_estimate=pl.CostEstimate(
+            flops=2 * total * depth * width,
+            bytes_accessed=2 * depth * (total + width),
+            transcendentals=0,
         ),
-        in_specs=[pl.BlockSpec(memory_space=pltpu.SMEM)] + [vmem] * (3 + len(token_sets)),
-        out_specs=(vmem, vmem),
-        scratch_shapes=[pltpu.VMEM((depth, 3 * HD), jnp.bfloat16)],
-        compiler_params=pltpu.CompilerParams(vmem_limit_bytes=24 * 1024 * 1024),
-        name="project",
+        name=name,
     )(where, mine, theirs_a, theirs_b, *token_sets)
 
 
 def attention_kernel(where_ref, owner_ref, offset_ref, global_ref, *rest):
-    given, pieces, token_refs = rest[:2], rest[2 : 2 + PIECES], rest[2 + PIECES : -9]
+    given, pieces = rest[: 1 + HEADS], rest[1 + HEADS : 1 + HEADS + PIECES]
+    token_refs = rest[1 + HEADS + PIECES : -9]
     keep_ref, send_ref, part_ref, kv_ref, g_ref, q_ref, gq_ref, t_ref, sems = rest[-9:]
     pairs = [
         (piece, kv_ref.at[pl.ds(slot * PIECE_BLOCKS, PIECE_BLOCKS)])
         for slot, piece in enumerate(pieces)
     ]
-    pairs += list(zip(given, (g_ref, q_ref)))
+    pairs += [(ref, g_ref.at[slot]) for slot, ref in enumerate(given[:-1])]
+    pairs.append((given[-1], q_ref))
     first = len(pairs)
     for slot, group in token_groups(token_refs):
         size = group[0].shape[0]
@@ -159,7 +167,7 @@
             ks.append(k)
             vs.append(v)
             ss.append(s)
-            gps.append(dot32(g_ref[x, rows, :], v, NT))
+            gps.append(dot32(g_ref[slot, rows, :], v, NT))
         for slot in range(HEADS):
             s, gp = ss[slot], gps[slot]
             e = jnp.exp(s - jnp.max(s, axis=1, keepdims=True))
@@ -198,24 +206,24 @@
     return pl.pallas_call(
         attention_kernel,
         out_shape=(
-            jax.ShapeDtypeStruct((2, *grads.shape[1:]), jnp.bfloat16),
-            jax.ShapeDtypeStruct((2, *grads.shape[1:]), jnp.bfloat16),
+            jax.ShapeDtypeStruct((2, *grads[0].shape), jnp.bfloat16),
+            jax.ShapeDtypeStruct((2, *grads[0].shape), jnp.bfloat16),
             jax.ShapeDtypeStruct((8, 16, 16, HD), jnp.bfloat16),
         ),
         in_specs=[smem] * 4
-        + [pl.BlockSpec(memory_space=pl.ANY)] * (2 + PIECES + len(token_sets)),
+        + [pl.BlockSpec(memory_space=pl.ANY)] * (1 + HEADS + PIECES + len(token_sets)),
         out_specs=(vmem,) * 3,
         scratch_shapes=[
             pltpu.VMEM((PIECES * PIECE_BLOCKS, BLK, 2 * HD), jnp.bfloat16),
-            pltpu.VMEM(grads.shape, jnp.bfloat16),
+            pltpu.VMEM((HEADS, *grads[0].shape), jnp.bfloat16),
             pltpu.VMEM(queries.shape, jnp.bfloat16),
-            pltpu.VMEM(grads.shape, jnp.bfloat16),
+            pltpu.VMEM((HEADS, *grads[0].shape), jnp.bfloat16),
             pltpu.VMEM((HEADS, *token_sets[0].shape), jnp.bfloat16),
-            pltpu.SemaphoreType.DMA((2 + PIECES + len(token_sets),)),
+            pltpu.SemaphoreType.DMA((1 + HEADS + PIECES + len(token_sets),)),
         ],
         compiler_params=pltpu.CompilerParams(vmem_limit_bytes=56 * 1024 * 1024),
         name="attention",
-    )(where, owners, offsets, global_list, grads, queries, *pieces, *token_sets)
+    )(where, owners, offsets, global_list, *grads, queries, *pieces, *token_sets)
 
 
 def merge_kernel(where_ref, keep_ref, next_ref, far_ref, out_ref):
@@ -245,28 +253,34 @@
     vmem = pl.BlockSpec(memory_space=pltpu.VMEM)
 
     rows = query_weight.shape[0] // 4
-    weight = pl.pallas_call(
+    weight, *grads = pl.pallas_call(
         slice_kernel,
-        out_shape=jax.ShapeDtypeStruct((16, rows, 3 * HD), jnp.bfloat16),
-        in_specs=[smem] + [vmem] * 3,
-        out_specs=vmem,
+        out_shape=(jax.ShapeDtypeStruct((16, rows, 3 * HD), jnp.bfloat16),)
+        + (jax.ShapeDtypeStruct((count, HD), jnp.bfloat16),) * HEADS,
+        in_specs=[smem] + [vmem] * 4,
+        out_specs=(vmem,) * (1 + HEADS),
         name="slice",
-    )(where, key_weight, value_weight, query_weight)
+    )(where, key_weight, value_weight, query_weight, cotangent[0])
     weight = lax.all_to_all(weight, "z", 0, 0, tiled=True)
 
     cut = count // 2
     before, after = shifted(own, "x", 1), shifted(own, "x", -1)
-    weight, before, after = lax.optimization_barrier((weight, before, after))
+    grads = [grads[0]] + [shifted(grads[h], "x", h) for h in range(1, HEADS)]
+    weight, before, after, low_next, high_next, grads = lax.optimization_barrier(
+        (weight, before, after, before[:cut], after[cut:], grads)
+    )
     weight = spread(weight, ("yh", "yl")).reshape(2, 2, 16, rows, 3 * HD)
     partner = [shifted(part, "core", 1) for part in weight]
-    low_far, high_far = shifted(before[:cut], "x", 1), shifted(after[cut:], "x", -1)
+    low_far, high_far = shifted(low_next, "x", 1), shifted(high_next, "x", -1)
     token_sets = (own, before, after, low_far, high_far)
-    grads = cotangent[0].reshape(count, HEADS, HD).transpose(1, 0, 2)
-    grads = lax.all_to_all(grads, "x", 0, 0, tiled=True)
-
-    queries, kv = project(where, weight, *partner, token_sets)
+    kv = project(
+        "keys_values", slice(0, 2 * HD), where, weight, *partner, token_sets
+    ).reshape(PIECE_BLOCKS, BLK, 2 * HD)
+    queries = project(
+        "queries", slice(2 * HD, 3 * HD), where, weight, *partner, token_sets
+    )
     across = shifted(kv, "yh", 1)
-    across, grads = lax.optimization_barrier((across, grads))
+    across, queries = lax.optimization_barrier((across, queries))
     pieces = [kv, shifted(kv, "core", 1), across, shifted(across, "core", 1)]
 
     kept, sent, partial = attention(

time: 153 us -> 151 us (0.987)
  blocking collectives: 27.3 us -> 0 us
  starting transfers between devices: 71.3 us -> 86.6 us
  waiting for transfers between devices: 24.5 us -> 34.8 us
  local copies, waits for them, and re-layouts: 9.26 us -> 7.25 us
  Pallas kernels: 17.4 us -> 19.1 us
    all_to_all x1 -> x0, blocking collectives: 27.3 us -> none  [per_device(): weight = lax.all_to_all(weight, 'z', 0, 0, tiled=True)]
    all_to_all x1, starting transfers between devices: 4.34 us -> 15.1 us  [per_device(): weight = lax.all_to_all(weight, 'z', 0, 0, tiled=True)]
    ppermute x9 -> x12, waiting for transfers between devices: 1.75 us -> 11.1 us  [shifted(): lax.ppermute(block, axis, [(i, (i + step) % count) for i in range(count)])]
    all_to_all x1, starting transfers between devices: 7.88 us -> 10.7 us  [per_device(): partial = lax.all_to_all(partial, 'z', 0, 0, tiled=True)]
    pallas_call x2 -> x3, Pallas kernels: 6.11 us -> 7.8 us  [the longest x2 5.9 us: project(): pl.pallas_call(functools.partial(project_kernel, cols), out_shape=jax.Sha...]
    all_to_all x2, waiting for transfers between devices: 6.07 us -> 7.71 us  [spread(): lax.all_to_all(jnp.broadcast_to(block[None], (count, *block.shape)), axes...]
    unnamed x36 -> x41, local copies, waits for them, and re-layouts: 4.83 us -> 3.62 us
    ppermute x9 -> x12, starting transfers between devices: 41.1 us -> 42.2 us  [shifted(): lax.ppermute(block, axis, [(i, (i + step) % count) for i in range(count)])]
  transfers between devices with their start and end apart: 16 -> 19, of which waited for: 6 -> 8; matrix products, arithmetic and copies ran while one was open for 4% -> 3% of each run, Pallas kernels for 2% -> 4%
where the time goes in v6:
time: 151 us; the launch traced here: 150 us
  starting transfers between devices  86.6 us (57%)
  waiting for transfers between devices  34.8 us (23%)
  Pallas kernels  19.1 us (13%)
  local copies, waits for them, and re-layouts  7.25 us (5%)
    ppermute x12, starting transfers between devices, shifted(): lax.ppermute(block, axis, [(i, (i + step) % count) for i in range(count)])  42.2 us
    all_to_all x1, starting transfers between devices, per_device(): weight = lax.all_to_all(weight, 'z', 0, 0, tiled=True)  15.1 us
    ppermute x12, waiting for transfers between devices, shifted(): lax.ppermute(block, axis, [(i, (i + step) % count) for i in range(count)])  11.1 us
    all_to_all x1, starting transfers between devices, per_device(): partial = lax.all_to_all(partial, 'z', 0, 0, tiled=True)  10.7 us
    all_to_all x2, starting transfers between devices, spread(): lax.all_to_all(jnp.broadcast_to(block[None], (count, *block.shape)), axes...  9.78 us
    pallas_call x1, Pallas kernels, attention(): pl.pallas_call(attention_kernel, out_shape=(jax.ShapeDtypeStruct((2, *gra...  9.54 us
    all_to_all x1, waiting for transfers between devices, per_device(): partial = lax.all_to_all(partial, 'z', 0, 0, tiled=True)  8.58 us
    all_to_all x2, waiting for transfers between devices, spread(): lax.all_to_all(jnp.broadcast_to(block[None], (count, *block.shape)), axes...  7.71 us
  transfers between devices with their start and end apart: 19, of which 8 were waited for; matrix products, arithmetic and copies ran while one was open for 3% of the time, Pallas kernels for 4%

profile of v6, /device:TPU:1, one launch (start us, length us, event | category | flops | bytes accessed | tf_op | source)
XLA Modules:
  0.0 150.2 jit_solution(10219456701951271884)
XLA Ops:
  0.6 5.2 %collective-permute-start.1 = (bf16[256,2048]{1,0:T(8,128)(2,1)}, bf16[256,2048]{1,0:T(8,128)(2,1)S(1)}, u32[]{:S(2)}, u32[]{:S(2)}) collective-permute-start(bf16[256,2048]{1,0:T(8,128)(2,1)} %bitcast.20), channel_id=1, source_target_pairs={{0,192},{64,0},{128,64},{192,128},{1,193},{65,1},{129,65},{193,129... | collective-permute-start | bytes 3145736 | tf_op jit(solution)/shard_map/ppermute | solution.py:39
  5.9 1.9 %collective-permute-start = (bf16[256,2048]{1,0:T(8,128)(2,1)}, bf16[256,2048]{1,0:T(8,128)(2,1)S(1)}, u32[]{:S(2)}, u32[]{:S(2)}) collective-permute-start(bf16[256,2048]{1,0:T(8,128)(2,1)} %bitcast.21), channel_id=1, source_target_pairs={{0,64},{64,128},{128,192},{192,0},{1,65},{65,129},{129,193},{193,1... | collective-permute-start | bytes 3145736 | tf_op jit(solution)/shard_map/ppermute | solution.py:39
  10.3 15.1 %all-to-all-start = ((bf16[16,16,384]{2,1,0:T(8,128)(2,1)}), bf16[16,16,384]{2,1,0:T(8,128)(2,1)S(1)}, u32[]{:S(2)}, u32[]{:S(2)}) async-start(bf16[16,16,384]{2,1,0:T(8,128)(2,1)} %get-tuple-element.25), calls=%async_computation | async-start | bytes 393216 | tf_op jit(solution)/shard_map/all_to_all | solution.py:264
  25.4 2.1 %collective-permute-start.2 = (bf16[256,128]{1,0:T(8,128)(2,1)S(1)}, bf16[256,128]{1,0:T(8,128)(2,1)S(1)}, u32[]{:S(2)}, u32[]{:S(2)}) collective-permute-start(bf16[256,128]{1,0:T(8,128)(2,1)S(1)} %copy-done.18), channel_id=1, source_target_pairs={{0,64},{64,128},{128,192},{192,0},{1,65},{65,129},{129,193},{193,1... | collective-permute-start | bytes 196616 | tf_op jit(solution)/shard_map/ppermute | solution.py:39
  27.5 5.6 %collective-permute-start.3 = (bf16[256,128]{1,0:T(8,128)(2,1)S(1)}, bf16[256,128]{1,0:T(8,128)(2,1)S(1)}, u32[]{:S(2)}, u32[]{:S(2)}) collective-permute-start(bf16[256,128]{1,0:T(8,128)(2,1)S(1)} %copy-done.17), channel_id=1, source_target_pairs={{0,128},{64,192},{128,0},{192,64},{1,129},{65,193},{129,1},{193,65... | collective-permute-start | bytes 196616 | tf_op jit(solution)/shard_map/ppermute | solution.py:39
  39.4 4.2 %all-to-all-start.1 = ((bf16[4,16,16,384]{3,2,1,0:T(8,128)(2,1)}), bf16[4,16,16,384]{3,2,1,0:T(8,128)(2,1)S(1)}, u32[]{:S(2)}, u32[]{:S(2)}) async-start(bf16[4,16,16,384]{3,2,1,0:T(8,128)(2,1)} %broadcast_in_dim.6), calls=%async_computation.1 | async-start | bytes 1572864 | tf_op jit(solution)/shard_map/all_to_all | solution.py:32
  43.6 2.0 %collective-permute-start.7 = (bf16[128,2048]{1,0:T(8,128)(2,1)}, bf16[128,2048]{1,0:T(8,128)(2,1)S(1)}, u32[]{:S(2)}, u32[]{:S(2)}) collective-permute-start(bf16[128,2048]{1,0:T(8,128)(2,1)} %slice.19), channel_id=1, source_target_pairs={{0,64},{64,128},{128,192},{192,0},{1,65},{65,129},{129,193},{193,1... | collective-permute-start | bytes 1572872 | tf_op jit(solution)/shard_map/ppermute | solution.py:39
  45.6 4.5 %collective-permute-start.8 = (bf16[128,2048]{1,0:T(8,128)(2,1)}, bf16[128,2048]{1,0:T(8,128)(2,1)}, u32[]{:S(2)}, u32[]{:S(2)}) collective-permute-start(bf16[128,2048]{1,0:T(8,128)(2,1)} %slice.20), channel_id=1, source_target_pairs={{0,192},{64,0},{128,64},{192,128},{1,193},{65,1},{129,65},{193,129... | collective-permute-start | bytes 1572872 | tf_op jit(solution)/shard_map/ppermute | solution.py:39
  52.0 7.9 %collective-permute-start.6 = (bf16[2,16,16,384]{3,2,1,0:T(8,128)(2,1)S(1)}, bf16[2,16,16,384]{3,2,1,0:T(8,128)(2,1)S(1)}, u32[]{:S(2)}, u32[]{:S(2)}) collective-permute-start(bf16[2,16,16,384]{3,2,1,0:T(8,128)(2,1)S(1)} %get-tuple-element.48), channel_id=1, source_target_pairs={{0,32},{32,0},{1,33},{33,1},{2,34},{34,2},{3,35},{35,3},{4,36},{36... | collective-permute-start | bytes 1179656 | tf_op jit(solution)/shard_map/ppermute | solution.py:39
  63.6 3.3 %keys_values.1 = bf16[1024,256]{1,0:T(8,128)(2,1)} custom-call(s32[3]{0:T(128)S(1)} %copy-done.5, bf16[2,2,16,16,384]{4,3,2,1,0:T(8,128)(2,1)S(1)} %bitcast.18, bf16[2,16,16,384]{3,2,1,0:T(8,128)(2,1)S(1)} %collective-permute-done.5.theirs_a_ref, bf16[2,16,16,384]{3,2,1,0:T(8,128)(2,1)S(1)} %collective-permute-done.6.theirs_b_ref, ...), custom_call_target="tpu_custom_call" | custom-call | flops 1073741824 | bytes 5242880 | tf_op jit(solution)/shard_map/keys_values/pallas_call | solution.py:88
  66.9 2.9 %collective-permute-start.9 = (bf16[16,64,256]{2,1,0:T(8,128)(2,1)}, bf16[16,64,256]{2,1,0:T(8,128)(2,1)}, u32[]{:S(2)}, u32[]{:S(2)}) collective-permute-start(bf16[16,64,256]{2,1,0:T(8,128)(2,1)} %bitcast.8.rest_5_), channel_id=1, source_target_pairs={{0,256},{256,0},{1,257},{257,1},{2,258},{258,2},{3,259},{259,3},{4... | collective-permute-start | bytes 1572872 | tf_op jit(solution)/shard_map/ppermute | solution.py:39
  69.8 3.4 %collective-permute-start.10 = (bf16[16,64,256]{2,1,0:T(8,128)(2,1)}, bf16[16,64,256]{2,1,0:T(8,128)(2,1)}, u32[]{:S(2)}, u32[]{:S(2)}) collective-permute-start(bf16[16,64,256]{2,1,0:T(8,128)(2,1)} %bitcast.8.rest_5_), channel_id=1, source_target_pairs={{0,32},{32,0},{1,33},{33,1},{2,34},{34,2},{3,35},{35,3},{4,36},{36... | collective-permute-start | bytes 1572872 | tf_op jit(solution)/shard_map/ppermute | solution.py:39
  73.2 2.6 %queries.1.rest_4_ = bf16[1024,128]{1,0:T(8,128)(2,1)S(1)} custom-call(s32[3]{0:T(128)S(1)} %copy-done.5, bf16[2,2,16,16,384]{4,3,2,1,0:T(8,128)(2,1)S(1)} %bitcast.19, bf16[2,16,16,384]{3,2,1,0:T(8,128)(2,1)S(1)} %collective-permute-done.5.theirs_a_ref, bf16[2,16,16,384]{3,2,1,0:T(8,128)(2,1)S(1)} %collective-permute-done.6.theirs_b_ref, ...), custom_call_target="tpu_custom_call" | custom-call | flops 536870912 | bytes 4718592 | tf_op jit(solution)/shard_map/queries/pallas_call | solution.py:88
  76.5 7.6 %collective-permute-done.9.rest_7_ = bf16[16,64,256]{2,1,0:T(8,128)(2,1)} collective-permute-done((bf16[16,64,256]{2,1,0:T(8,128)(2,1)}, bf16[16,64,256]{2,1,0:T(8,128)(2,1)}, u32[]{:S(2)}, u32[]{:S(2)}) %collective-permute-start.9) | collective-permute-done | bytes 524320 | tf_op jit(solution)/shard_map/ppermute | solution.py:39
  84.1 2.9 %collective-permute-start.11 = (bf16[16,64,256]{2,1,0:T(8,128)(2,1)}, bf16[16,64,256]{2,1,0:T(8,128)(2,1)S(1)}, u32[]{:S(2)}, u32[]{:S(2)}) collective-permute-start(bf16[16,64,256]{2,1,0:T(8,128)(2,1)} %collective-permute-done.9.rest_7_), channel_id=1, source_target_pairs={{0,32},{32,0},{1,33},{33,1},{2,34},{34,2},{3,35},{35,3},{4,36},{36... | collective-permute-start | bytes 1572872 | tf_op jit(solution)/shard_map/ppermute | solution.py:39
  89.5 9.5 %attention.1 = (bf16[2,256,128]{2,1,0:T(8,128)(2,1)}, bf16[2,256,128]{2,1,0:T(8,128)(2,1)}, bf16[8,16,16,128]{3,2,1,0:T(8,128)(2,1)}) custom-call(s32[3]{0:T(128)} %pad_add_fusion.where_ref, s32[64,3]{1,0:T(8,128)} %bitcast.29, s32[64,3]{1,0:T(8,128)} %bitcast.30, s32[1,2]{1,0:T(1,128)} %global_ref.1, bf16[256,128]{1,0:T(8,128)(2,1)} %get-tuple-element.30.rest_0_, ...), custom_call_target="tpu_custom_call" | custom-call | tf_op jit(solution)/shard_map/attention/pallas_call | solution.py:206
  99.0 3.9 %all-to-all-start.2 = ((bf16[8,16,16,128]{3,2,1,0:T(8,128)(2,1)}), bf16[8,16,16,128]{3,2,1,0:T(8,128)(2,1)S(1)}, u32[]{:S(2)}, u32[]{:S(2)}) async-start(bf16[8,16,16,128]{3,2,1,0:T(8,128)(2,1)} %get-tuple-element.42), calls=%async_computation.2 | async-start | bytes 1048576 | tf_op jit(solution)/shard_map/all_to_all | solution.py:290
  103.0 2.1 %collective-permute-start.12 = (bf16[2,256,128]{2,1,0:T(8,128)(2,1)S(1)}, bf16[2,256,128]{2,1,0:T(8,128)(2,1)S(1)}, u32[]{:S(2)}, u32[]{:S(2)}) collective-permute-start(bf16[2,256,128]{2,1,0:T(8,128)(2,1)S(1)} %copy-done.15), channel_id=1, source_target_pairs={{0,64},{64,0},{128,192},{192,128},{1,65},{65,1},{129,193},{193,129... | collective-permute-start | bytes 393224 | tf_op jit(solution)/shard_map/ppermute | solution.py:241
  105.1 7.4 %all-to-all-done.2 = bf16[8,16,16,128]{3,2,1,0:T(8,128)(2,1)S(1)} async-done(((bf16[8,16,16,128]{3,2,1,0:T(8,128)(2,1)}), bf16[8,16,16,128]{3,2,1,0:T(8,128)(2,1)S(1)}, u32[]{:S(2)}, u32[]{:S(2)}) %all-to-all-start.2) | async-done | bytes 524320 | tf_op jit(solution)/shard_map/all_to_all | solution.py:290
  113.2 10.7 %all-to-all-start.3 = ((bf16[16,16,128]{2,1,0:T(8,128)(2,1)}), bf16[16,16,128]{2,1,0:T(8,128)(2,1)S(1)}, u32[]{:S(2)}, u32[]{:S(2)}) async-start(bf16[16,16,128]{2,1,0:T(8,128)(2,1)} %reduce_sum.21), calls=%async_computation.3 | async-start | bytes 131072 | tf_op jit(solution)/shard_map/all_to_all | solution.py:294
  123.9 2.9 %collective-permute-start.13 = (bf16[2,256,128]{2,1,0:T(8,128)(2,1)S(1)}, bf16[2,256,128]{2,1,0:T(8,128)(2,1)S(1)}, u32[]{:S(2)}, u32[]{:S(2)}) collective-permute-start(bf16[2,256,128]{2,1,0:T(8,128)(2,1)S(1)} %pad_maximum_fusion), channel_id=1, source_target_pairs={{0,128},{64,192},{128,0},{192,64},{1,129},{65,193},{129,1},{193,65... | collective-permute-start | bytes 393224 | tf_op jit(solution)/shard_map/ppermute | solution.py:241
  126.9 8.6 %all-to-all-done.3 = bf16[16,16,128]{2,1,0:T(8,128)(2,1)S(1)} async-done(((bf16[16,16,128]{2,1,0:T(8,128)(2,1)}), bf16[16,16,128]{2,1,0:T(8,128)(2,1)S(1)}, u32[]{:S(2)}, u32[]{:S(2)}) %all-to-all-start.3) | async-done | bytes 65568 | tf_op jit(solution)/shard_map/all_to_all | solution.py:294
  136.2 5.6 %all-to-all-start.4 = ((f32[16,16,128]{2,1,0:T(8,128)}), f32[16,16,128]{2,1,0:T(8,128)S(1)}, u32[]{:S(2)}, u32[]{:S(2)}) async-start(f32[16,16,128]{2,1,0:T(8,128)} %broadcast_in_dim.8), calls=%async_computation.4 | async-start | bytes 262144 | tf_op jit(solution)/shard_map/all_to_all | solution.py:32
  143.6 5.9 %all-to-all-done.4 = f32[16,16,128]{2,1,0:T(8,128)S(1)} async-done(((f32[16,16,128]{2,1,0:T(8,128)}), f32[16,16,128]{2,1,0:T(8,128)S(1)}, u32[]{:S(2)}, u32[]{:S(2)}) %all-to-all-start.4) | async-done | bytes 131104 | tf_op jit(solution)/shard_map/all_to_all | solution.py:32
  (72 shorter events, 21.5 us)
Async XLA Ops:
  0.6 34.4 %collective-permute-start.1 = (bf16[256,2048]{1,0:T(8,128)(2,1)}, bf16[256,2048]{1,0:T(8,128)(2,1)S(1)}, u32[]{:S(2)}, u32[]{:S(2)}) collective-permute-start(bf16[256,2048]{1,0:T(8,128)(2,1)} %bitcast.20), channel_id=1, source_target_pairs={{0,192},{64,0},{128,64},{192,128},{1,193},{65,1},{129,65},{193,129... | collective-permute-start | bytes 3145736 | tf_op jit(solution)/shard_map/ppermute | solution.py:39
  5.9 30.1 %collective-permute-start = (bf16[256,2048]{1,0:T(8,128)(2,1)}, bf16[256,2048]{1,0:T(8,128)(2,1)S(1)}, u32[]{:S(2)}, u32[]{:S(2)}) collective-permute-start(bf16[256,2048]{1,0:T(8,128)(2,1)} %bitcast.21), channel_id=1, source_target_pairs={{0,64},{64,128},{128,192},{192,0},{1,65},{65,129},{129,193},{193,1... | collective-permute-start | bytes 3145736 | tf_op jit(solution)/shard_map/ppermute | solution.py:39
  10.3 17.2 %copy-start.17 = (bf16[256,128]{1,0:T(8,128)(2,1)S(1)}, bf16[256,128]{1,0:T(8,128)(2,1)}, u32[]{:S(2)}) copy-start(bf16[256,128]{1,0:T(8,128)(2,1)} %get-tuple-element.28) | copy-start | bytes 196612
  10.3 22.8 %copy-start.16 = (bf16[256,128]{1,0:T(8,128)(2,1)S(1)}, bf16[256,128]{1,0:T(8,128)(2,1)}, u32[]{:S(2)}) copy-start(bf16[256,128]{1,0:T(8,128)(2,1)} %get-tuple-element.29) | copy-start | bytes 196612
  10.3 28.1 %all-to-all-start = ((bf16[16,16,384]{2,1,0:T(8,128)(2,1)}), bf16[16,16,384]{2,1,0:T(8,128)(2,1)S(1)}, u32[]{:S(2)}, u32[]{:S(2)}) async-start(bf16[16,16,384]{2,1,0:T(8,128)(2,1)} %get-tuple-element.25), calls=%async_computation | async-start | bytes 393216 | tf_op jit(solution)/shard_map/all_to_all | solution.py:264
  25.4 11.5 %collective-permute-start.2 = (bf16[256,128]{1,0:T(8,128)(2,1)S(1)}, bf16[256,128]{1,0:T(8,128)(2,1)S(1)}, u32[]{:S(2)}, u32[]{:S(2)}) collective-permute-start(bf16[256,128]{1,0:T(8,128)(2,1)S(1)} %copy-done.18), channel_id=1, source_target_pairs={{0,64},{64,128},{128,192},{192,0},{1,65},{65,129},{129,193},{193,1... | collective-permute-start | bytes 196616 | tf_op jit(solution)/shard_map/ppermute | solution.py:39
  27.5 9.4 %collective-permute-start.3 = (bf16[256,128]{1,0:T(8,128)(2,1)S(1)}, bf16[256,128]{1,0:T(8,128)(2,1)S(1)}, u32[]{:S(2)}, u32[]{:S(2)}) collective-permute-start(bf16[256,128]{1,0:T(8,128)(2,1)S(1)} %copy-done.17), channel_id=1, source_target_pairs={{0,128},{64,192},{128,0},{192,64},{1,129},{65,193},{129,1},{193,65... | collective-permute-start | bytes 196616 | tf_op jit(solution)/shard_map/ppermute | solution.py:39
  33.1 5.3 %collective-permute-start.4 = (bf16[256,128]{1,0:T(8,128)(2,1)S(1)}, bf16[256,128]{1,0:T(8,128)(2,1)S(1)}, u32[]{:S(2)}, u32[]{:S(2)}) collective-permute-start(bf16[256,128]{1,0:T(8,128)(2,1)S(1)} %copy-done.16), channel_id=1, source_target_pairs={{0,192},{64,0},{128,64},{192,128},{1,193},{65,1},{129,65},{193,129... | collective-permute-start | bytes 196616 | tf_op jit(solution)/shard_map/ppermute | solution.py:39
  35.1 38.1 %copy-start = (bf16[256,2048]{1,0:T(8,128)(2,1)}, bf16[256,2048]{1,0:T(8,128)(2,1)S(1)}, u32[]{:S(2)}) copy-start(bf16[256,2048]{1,0:T(8,128)(2,1)S(1)} %collective-permute-done.1.rest_2_.rest_11_) | copy-start | bytes 3145732
  36.0 37.2 %copy-start.1 = (bf16[256,2048]{1,0:T(8,128)(2,1)}, bf16[256,2048]{1,0:T(8,128)(2,1)S(1)}, u32[]{:S(2)}) copy-start(bf16[256,2048]{1,0:T(8,128)(2,1)S(1)} %collective-permute-done.rest_1_.rest_10_) | copy-start | bytes 3145732
  39.4 12.5 %all-to-all-start.1 = ((bf16[4,16,16,384]{3,2,1,0:T(8,128)(2,1)}), bf16[4,16,16,384]{3,2,1,0:T(8,128)(2,1)S(1)}, u32[]{:S(2)}, u32[]{:S(2)}) async-start(bf16[4,16,16,384]{3,2,1,0:T(8,128)(2,1)} %broadcast_in_dim.6), calls=%async_computation.1 | async-start | bytes 1572864 | tf_op jit(solution)/shard_map/all_to_all | solution.py:32
  43.6 18.3 %collective-permute-start.7 = (bf16[128,2048]{1,0:T(8,128)(2,1)}, bf16[128,2048]{1,0:T(8,128)(2,1)S(1)}, u32[]{:S(2)}, u32[]{:S(2)}) collective-permute-start(bf16[128,2048]{1,0:T(8,128)(2,1)} %slice.19), channel_id=1, source_target_pairs={{0,64},{64,128},{128,192},{192,0},{1,65},{65,129},{129,193},{193,1... | collective-permute-start | bytes 1572872 | tf_op jit(solution)/shard_map/ppermute | solution.py:39
  45.6 16.3 %collective-permute-start.8 = (bf16[128,2048]{1,0:T(8,128)(2,1)}, bf16[128,2048]{1,0:T(8,128)(2,1)}, u32[]{:S(2)}, u32[]{:S(2)}) collective-permute-start(bf16[128,2048]{1,0:T(8,128)(2,1)} %slice.20), channel_id=1, source_target_pairs={{0,192},{64,0},{128,64},{192,128},{1,193},{65,1},{129,65},{193,129... | collective-permute-start | bytes 1572872 | tf_op jit(solution)/shard_map/ppermute | solution.py:39
  52.0 9.9 %collective-permute-start.6 = (bf16[2,16,16,384]{3,2,1,0:T(8,128)(2,1)S(1)}, bf16[2,16,16,384]{3,2,1,0:T(8,128)(2,1)S(1)}, u32[]{:S(2)}, u32[]{:S(2)}) collective-permute-start(bf16[2,16,16,384]{3,2,1,0:T(8,128)(2,1)S(1)} %get-tuple-element.48), channel_id=1, source_target_pairs={{0,32},{32,0},{1,33},{33,1},{2,34},{34,2},{3,35},{35,3},{4,36},{36... | collective-permute-start | bytes 1179656 | tf_op jit(solution)/shard_map/ppermute | solution.py:39
  59.9 3.6 %collective-permute-start.5 = (bf16[2,16,16,384]{3,2,1,0:T(8,128)(2,1)S(1)}, bf16[2,16,16,384]{3,2,1,0:T(8,128)(2,1)S(1)}, u32[]{:S(2)}, u32[]{:S(2)}) collective-permute-start(bf16[2,16,16,384]{3,2,1,0:T(8,128)(2,1)S(1)} %get-tuple-element.49), channel_id=1, source_target_pairs={{0,32},{32,0},{1,33},{33,1},{2,34},{34,2},{3,35},{35,3},{4,36},{36... | collective-permute-start | bytes 1179656 | tf_op jit(solution)/shard_map/ppermute | solution.py:39
  66.9 20.1 %copy-start.13 = (s32[1,64,3]{1,0,2:T(1,128)S(1)}, s32[1,64,3]{1,0,2:T(1,128)}, u32[]{:S(2)}) copy-start(s32[1,64,3]{1,0,2:T(1,128)} %param.13) | copy-start | bytes 2308
  66.9 17.2 %collective-permute-start.9 = (bf16[16,64,256]{2,1,0:T(8,128)(2,1)}, bf16[16,64,256]{2,1,0:T(8,128)(2,1)}, u32[]{:S(2)}, u32[]{:S(2)}) collective-permute-start(bf16[16,64,256]{2,1,0:T(8,128)(2,1)} %bitcast.8.rest_5_), channel_id=1, source_target_pairs={{0,256},{256,0},{1,257},{257,1},{2,258},{258,2},{3,259},{259,3},{4... | collective-permute-start | bytes 1572872 | tf_op jit(solution)/shard_map/ppermute | solution.py:39
  69.8 18.6 %collective-permute-start.10 = (bf16[16,64,256]{2,1,0:T(8,128)(2,1)}, bf16[16,64,256]{2,1,0:T(8,128)(2,1)}, u32[]{:S(2)}, u32[]{:S(2)}) collective-permute-start(bf16[16,64,256]{2,1,0:T(8,128)(2,1)} %bitcast.8.rest_5_), channel_id=1, source_target_pairs={{0,32},{32,0},{1,33},{33,1},{2,34},{34,2},{3,35},{35,3},{4,36},{36... | collective-permute-start | bytes 1572872 | tf_op jit(solution)/shard_map/ppermute | solution.py:39
  84.1 4.6 %collective-permute-start.11 = (bf16[16,64,256]{2,1,0:T(8,128)(2,1)}, bf16[16,64,256]{2,1,0:T(8,128)(2,1)S(1)}, u32[]{:S(2)}, u32[]{:S(2)}) collective-permute-start(bf16[16,64,256]{2,1,0:T(8,128)(2,1)} %collective-permute-done.9.rest_7_), channel_id=1, source_target_pairs={{0,32},{32,0},{1,33},{33,1},{2,34},{34,2},{3,35},{35,3},{4,36},{36... | collective-permute-start | bytes 1572872 | tf_op jit(solution)/shard_map/ppermute | solution.py:39
  99.0 13.4 %all-to-all-start.2 = ((bf16[8,16,16,128]{3,2,1,0:T(8,128)(2,1)}), bf16[8,16,16,128]{3,2,1,0:T(8,128)(2,1)S(1)}, u32[]{:S(2)}, u32[]{:S(2)}) async-start(bf16[8,16,16,128]{3,2,1,0:T(8,128)(2,1)} %get-tuple-element.42), calls=%async_computation.2 | async-start | bytes 1048576 | tf_op jit(solution)/shard_map/all_to_all | solution.py:290
  103.0 10.2 %collective-permute-start.12 = (bf16[2,256,128]{2,1,0:T(8,128)(2,1)S(1)}, bf16[2,256,128]{2,1,0:T(8,128)(2,1)S(1)}, u32[]{:S(2)}, u32[]{:S(2)}) collective-permute-start(bf16[2,256,128]{2,1,0:T(8,128)(2,1)S(1)} %copy-done.15), channel_id=1, source_target_pairs={{0,64},{64,0},{128,192},{192,128},{1,65},{65,1},{129,193},{193,129... | collective-permute-start | bytes 393224 | tf_op jit(solution)/shard_map/ppermute | solution.py:241
  113.2 22.3 %all-to-all-start.3 = ((bf16[16,16,128]{2,1,0:T(8,128)(2,1)}), bf16[16,16,128]{2,1,0:T(8,128)(2,1)S(1)}, u32[]{:S(2)}, u32[]{:S(2)}) async-start(bf16[16,16,128]{2,1,0:T(8,128)(2,1)} %reduce_sum.21), calls=%async_computation.3 | async-start | bytes 131072 | tf_op jit(solution)/shard_map/all_to_all | solution.py:294
  123.9 11.5 %collective-permute-start.13 = (bf16[2,256,128]{2,1,0:T(8,128)(2,1)S(1)}, bf16[2,256,128]{2,1,0:T(8,128)(2,1)S(1)}, u32[]{:S(2)}, u32[]{:S(2)}) collective-permute-start(bf16[2,256,128]{2,1,0:T(8,128)(2,1)S(1)} %pad_maximum_fusion), channel_id=1, source_target_pairs={{0,128},{64,192},{128,0},{192,64},{1,129},{65,193},{129,1},{193,65... | collective-permute-start | bytes 393224 | tf_op jit(solution)/shard_map/ppermute | solution.py:241
  136.2 13.3 %all-to-all-start.4 = ((f32[16,16,128]{2,1,0:T(8,128)}), f32[16,16,128]{2,1,0:T(8,128)S(1)}, u32[]{:S(2)}, u32[]{:S(2)}) async-start(f32[16,16,128]{2,1,0:T(8,128)} %broadcast_in_dim.8), calls=%async_computation.4 | async-start | bytes 262144 | tf_op jit(solution)/shard_map/all_to_all | solution.py:32
  (14 other events, 86.4 us)

commit v7 on v6

--- a/solution.py
+++ b/solution.py
@@ -266,8 +266,8 @@
     cut = count // 2
     before, after = shifted(own, "x", 1), shifted(own, "x", -1)
     grads = [grads[0]] + [shifted(grads[h], "x", h) for h in range(1, HEADS)]
-    weight, before, after, low_next, high_next, grads = lax.optimization_barrier(
-        (weight, before, after, before[:cut], after[cut:], grads)
+    weight, before, after, low_next, high_next, grads[2] = lax.optimization_barrier(
+        (weight, before, after, before[:cut], after[cut:], grads[2])
     )
     weight = spread(weight, ("yh", "yl")).reshape(2, 2, 16, rows, 3 * HD)
     partner = [shifted(part, "core", 1) for part in weight]
@@ -280,7 +280,9 @@
         "queries", slice(2 * HD, 3 * HD), where, weight, *partner, token_sets
     )
     across = shifted(kv, "yh", 1)
-    across, queries = lax.optimization_barrier((across, queries))
+    across, queries, grads[1], grads[3] = lax.optimization_barrier(
+        (across, queries, grads[1], grads[3])
+    )
     pieces = [kv, shifted(kv, "core", 1), across, shifted(across, "core", 1)]
 
     kept, sent, partial = attention(

time: 151 us -> 151 us (level)
  waiting for transfers between devices: 34.8 us -> 32.4 us
  starting transfers between devices: 86.6 us -> 88.5 us
    ppermute x12, waiting for transfers between devices: 11.1 us -> 4.49 us  [shifted(): lax.ppermute(block, axis, [(i, (i + step) % count) for i in range(count)])]
    all_to_all x1, waiting for transfers between devices: 0.01 us -> 4.37 us  [per_device(): weight = lax.all_to_all(weight, 'z', 0, 0, tiled=True)]
    ppermute x12, starting transfers between devices: 42.2 us -> 44.3 us  [shifted(): lax.ppermute(block, axis, [(i, (i + step) % count) for i in range(count)])]
  transfers between devices with their start and end apart: 19 -> 19, of which waited for: 8 -> 9; matrix products, arithmetic and copies ran while one was open for 3% -> 3% of each run, Pallas kernels for 4% -> 4%
where the time goes in v7:
time: 151 us; the launch traced here: 150 us
  starting transfers between devices  88.5 us (59%)
  waiting for transfers between devices  32.4 us (21%)
  Pallas kernels  19.2 us (13%)
  local copies, waits for them, and re-layouts  7.3 us (5%)
    ppermute x12, starting transfers between devices, shifted(): lax.ppermute(block, axis, [(i, (i + step) % count) for i in range(count)])  44.3 us
    all_to_all x1, starting transfers between devices, per_device(): weight = lax.all_to_all(weight, 'z', 0, 0, tiled=True)  15 us
    all_to_all x1, starting transfers between devices, per_device(): partial = lax.all_to_all(partial, 'z', 0, 0, tiled=True)  10.3 us
    all_to_all x2, starting transfers between devices, spread(): lax.all_to_all(jnp.broadcast_to(block[None], (count, *block.shape)), axes...  9.78 us
    pallas_call x1, Pallas kernels, attention(): pl.pallas_call(attention_kernel, out_shape=(jax.ShapeDtypeStruct((2, *gra...  9.54 us
    all_to_all x1, waiting for transfers between devices, per_device(): partial = lax.all_to_all(partial, 'z', 0, 0, tiled=True)  8.42 us
    all_to_all x2, waiting for transfers between devices, spread(): lax.all_to_all(jnp.broadcast_to(block[None], (count, *block.shape)), axes...  7.71 us
    all_to_all x1, waiting for transfers between devices, per_device(): partial = lax.all_to_all(partial, ('yh', 'yl', 'core'), 0, 0, tiled=True)  7.39 us
  transfers between devices with their start and end apart: 19, of which 9 were waited for; matrix products, arithmetic and copies ran while one was open for 3% of the time, Pallas kernels for 4%

profile of v7, /device:TPU:1, one launch (start us, length us, event | category | flops | bytes accessed | tf_op | source)
XLA Modules:
  0.0 149.7 jit_solution(3931201611763725312)
XLA Ops:
  0.6 5.2 %collective-permute-start.1 = (bf16[256,2048]{1,0:T(8,128)(2,1)}, bf16[256,2048]{1,0:T(8,128)(2,1)S(1)}, u32[]{:S(2)}, u32[]{:S(2)}) collective-permute-start(bf16[256,2048]{1,0:T(8,128)(2,1)} %bitcast.20), channel_id=1, source_target_pairs={{0,192},{64,0},{128,64},{192,128},{1,193},{65,1},{129,65},{193,129... | collective-permute-start | bytes 3145736 | tf_op jit(solution)/shard_map/ppermute | solution.py:39
  10.3 15.0 %all-to-all-start = ((bf16[16,16,384]{2,1,0:T(8,128)(2,1)}), bf16[16,16,384]{2,1,0:T(8,128)(2,1)S(1)}, u32[]{:S(2)}, u32[]{:S(2)}) async-start(bf16[16,16,384]{2,1,0:T(8,128)(2,1)} %get-tuple-element.25), calls=%async_computation | async-start | bytes 393216 | tf_op jit(solution)/shard_map/all_to_all | solution.py:264
  25.4 3.6 %collective-permute-start.2 = (bf16[256,128]{1,0:T(8,128)(2,1)S(1)}, bf16[256,128]{1,0:T(8,128)(2,1)S(1)}, u32[]{:S(2)}, u32[]{:S(2)}) collective-permute-start(bf16[256,128]{1,0:T(8,128)(2,1)S(1)} %copy-done.18), channel_id=1, source_target_pairs={{0,128},{64,192},{128,0},{192,64},{1,129},{65,193},{129,1},{193,65... | collective-permute-start | bytes 196616 | tf_op jit(solution)/shard_map/ppermute | solution.py:39
  31.1 2.2 %collective-permute-done.2.rest_2_ = bf16[256,128]{1,0:T(8,128)(2,1)S(1)} collective-permute-done((bf16[256,128]{1,0:T(8,128)(2,1)S(1)}, bf16[256,128]{1,0:T(8,128)(2,1)S(1)}, u32[]{:S(2)}, u32[]{:S(2)}) %collective-permute-start.2) | collective-permute-done | bytes 65568 | tf_op jit(solution)/shard_map/ppermute | solution.py:39
  33.3 4.4 %all-to-all-done = bf16[16,16,384]{2,1,0:T(8,128)(2,1)S(1)} async-done(((bf16[16,16,384]{2,1,0:T(8,128)(2,1)}), bf16[16,16,384]{2,1,0:T(8,128)(2,1)S(1)}, u32[]{:S(2)}, u32[]{:S(2)}) %all-to-all-start) | async-done | bytes 196640 | tf_op jit(solution)/shard_map/all_to_all | solution.py:264
  38.7 4.2 %all-to-all-start.1 = ((bf16[4,16,16,384]{3,2,1,0:T(8,128)(2,1)}), bf16[4,16,16,384]{3,2,1,0:T(8,128)(2,1)S(1)}, u32[]{:S(2)}, u32[]{:S(2)}) async-start(bf16[4,16,16,384]{3,2,1,0:T(8,128)(2,1)} %broadcast_in_dim.6), calls=%async_computation.1 | async-start | bytes 1572864 | tf_op jit(solution)/shard_map/all_to_all | solution.py:32
  42.9 2.1 %collective-permute-start.5 = (bf16[128,2048]{1,0:T(8,128)(2,1)}, bf16[128,2048]{1,0:T(8,128)(2,1)S(1)}, u32[]{:S(2)}, u32[]{:S(2)}) collective-permute-start(bf16[128,2048]{1,0:T(8,128)(2,1)} %slice.19), channel_id=1, source_target_pairs={{0,64},{64,128},{128,192},{192,0},{1,65},{65,129},{129,193},{193,1... | collective-permute-start | bytes 1572872 | tf_op jit(solution)/shard_map/ppermute | solution.py:39
  44.9 4.4 %collective-permute-start.6 = (bf16[128,2048]{1,0:T(8,128)(2,1)}, bf16[128,2048]{1,0:T(8,128)(2,1)}, u32[]{:S(2)}, u32[]{:S(2)}) collective-permute-start(bf16[128,2048]{1,0:T(8,128)(2,1)} %slice.20), channel_id=1, source_target_pairs={{0,192},{64,0},{128,64},{192,128},{1,193},{65,1},{129,65},{193,129... | collective-permute-start | bytes 1572872 | tf_op jit(solution)/shard_map/ppermute | solution.py:39
  51.3 8.6 %collective-permute-start.4 = (bf16[2,16,16,384]{3,2,1,0:T(8,128)(2,1)S(1)}, bf16[2,16,16,384]{3,2,1,0:T(8,128)(2,1)S(1)}, u32[]{:S(2)}, u32[]{:S(2)}) collective-permute-start(bf16[2,16,16,384]{3,2,1,0:T(8,128)(2,1)S(1)} %get-tuple-element.46), channel_id=1, source_target_pairs={{0,32},{32,0},{1,33},{33,1},{2,34},{34,2},{3,35},{35,3},{4,36},{36... | collective-permute-start | bytes 1179656 | tf_op jit(solution)/shard_map/ppermute | solution.py:39
  63.5 3.4 %keys_values.1 = bf16[1024,256]{1,0:T(8,128)(2,1)} custom-call(s32[3]{0:T(128)S(1)} %copy-done.5, bf16[2,2,16,16,384]{4,3,2,1,0:T(8,128)(2,1)S(1)} %bitcast.18, bf16[2,16,16,384]{3,2,1,0:T(8,128)(2,1)S(1)} %collective-permute-done.3.theirs_a_ref, bf16[2,16,16,384]{3,2,1,0:T(8,128)(2,1)S(1)} %collective-permute-done.4.theirs_b_ref, ...), custom_call_target="tpu_custom_call" | custom-call | flops 1073741824 | bytes 5242880 | tf_op jit(solution)/shard_map/keys_values/pallas_call | solution.py:88
  66.9 2.7 %collective-permute-start.7 = (bf16[16,64,256]{2,1,0:T(8,128)(2,1)}, bf16[16,64,256]{2,1,0:T(8,128)(2,1)}, u32[]{:S(2)}, u32[]{:S(2)}) collective-permute-start(bf16[16,64,256]{2,1,0:T(8,128)(2,1)} %bitcast.8.rest_5_), channel_id=1, source_target_pairs={{0,256},{256,0},{1,257},{257,1},{2,258},{258,2},{3,259},{259,3},{4... | collective-permute-start | bytes 1572872 | tf_op jit(solution)/shard_map/ppermute | solution.py:39
  71.6 4.6 %collective-permute-start.9 = (bf16[256,128]{1,0:T(8,128)(2,1)S(1)}, bf16[256,128]{1,0:T(8,128)(2,1)S(1)}, u32[]{:S(2)}, u32[]{:S(2)}) collective-permute-start(bf16[256,128]{1,0:T(8,128)(2,1)S(1)} %copy-done.16), channel_id=1, source_target_pairs={{0,192},{64,0},{128,64},{192,128},{1,193},{65,1},{129,65},{193,129... | collective-permute-start | bytes 196616 | tf_op jit(solution)/shard_map/ppermute | solution.py:39
  76.2 4.5 %collective-permute-start.10 = (bf16[16,64,256]{2,1,0:T(8,128)(2,1)}, bf16[16,64,256]{2,1,0:T(8,128)(2,1)}, u32[]{:S(2)}, u32[]{:S(2)}) collective-permute-start(bf16[16,64,256]{2,1,0:T(8,128)(2,1)} %bitcast.8.rest_5_), channel_id=1, source_target_pairs={{0,32},{32,0},{1,33},{33,1},{2,34},{34,2},{3,35},{35,3},{4,36},{36... | collective-permute-start | bytes 1572872 | tf_op jit(solution)/shard_map/ppermute | solution.py:39
  80.7 2.6 %queries.1.rest_4_ = bf16[1024,128]{1,0:T(8,128)(2,1)S(1)} custom-call(s32[3]{0:T(128)S(1)} %copy-done.5, bf16[2,2,16,16,384]{4,3,2,1,0:T(8,128)(2,1)S(1)} %bitcast.19, bf16[2,16,16,384]{3,2,1,0:T(8,128)(2,1)S(1)} %collective-permute-done.3.theirs_a_ref, bf16[2,16,16,384]{3,2,1,0:T(8,128)(2,1)S(1)} %collective-permute-done.4.theirs_b_ref, ...), custom_call_target="tpu_custom_call" | custom-call | flops 536870912 | bytes 4718592 | tf_op jit(solution)/shard_map/queries/pallas_call | solution.py:88
  84.0 2.9 %collective-permute-start.11 = (bf16[16,64,256]{2,1,0:T(8,128)(2,1)}, bf16[16,64,256]{2,1,0:T(8,128)(2,1)S(1)}, u32[]{:S(2)}, u32[]{:S(2)}) collective-permute-start(bf16[16,64,256]{2,1,0:T(8,128)(2,1)} %collective-permute-done.7.rest_7_), channel_id=1, source_target_pairs={{0,32},{32,0},{1,33},{33,1},{2,34},{34,2},{3,35},{35,3},{4,36},{36... | collective-permute-start | bytes 1572872 | tf_op jit(solution)/shard_map/ppermute | solution.py:39
  89.4 9.5 %attention.1 = (bf16[2,256,128]{2,1,0:T(8,128)(2,1)}, bf16[2,256,128]{2,1,0:T(8,128)(2,1)}, bf16[8,16,16,128]{3,2,1,0:T(8,128)(2,1)}) custom-call(s32[3]{0:T(128)} %pad_add_fusion.where_ref, s32[64,3]{1,0:T(8,128)} %bitcast.29, s32[64,3]{1,0:T(8,128)} %bitcast.30, s32[1,2]{1,0:T(1,128)} %global_ref.1, bf16[256,128]{1,0:T(8,128)(2,1)} %get-tuple-element.24.rest_0_, ...), custom_call_target="tpu_custom_call" | custom-call | tf_op jit(solution)/shard_map/attention/pallas_call | solution.py:206
  98.9 3.9 %all-to-all-start.2 = ((bf16[8,16,16,128]{3,2,1,0:T(8,128)(2,1)}), bf16[8,16,16,128]{3,2,1,0:T(8,128)(2,1)S(1)}, u32[]{:S(2)}, u32[]{:S(2)}) async-start(bf16[8,16,16,128]{3,2,1,0:T(8,128)(2,1)} %get-tuple-element.40), calls=%async_computation.2 | async-start | bytes 1048576 | tf_op jit(solution)/shard_map/all_to_all | solution.py:292
  102.8 2.1 %collective-permute-start.12 = (bf16[2,256,128]{2,1,0:T(8,128)(2,1)S(1)}, bf16[2,256,128]{2,1,0:T(8,128)(2,1)S(1)}, u32[]{:S(2)}, u32[]{:S(2)}) collective-permute-start(bf16[2,256,128]{2,1,0:T(8,128)(2,1)S(1)} %copy-done.15), channel_id=1, source_target_pairs={{0,64},{64,0},{128,192},{192,128},{1,65},{65,1},{129,193},{193,129... | collective-permute-start | bytes 393224 | tf_op jit(solution)/shard_map/ppermute | solution.py:241
  104.9 7.4 %all-to-all-done.2 = bf16[8,16,16,128]{3,2,1,0:T(8,128)(2,1)S(1)} async-done(((bf16[8,16,16,128]{3,2,1,0:T(8,128)(2,1)}), bf16[8,16,16,128]{3,2,1,0:T(8,128)(2,1)S(1)}, u32[]{:S(2)}, u32[]{:S(2)}) %all-to-all-start.2) | async-done | bytes 524320 | tf_op jit(solution)/shard_map/all_to_all | solution.py:292
  113.0 10.3 %all-to-all-start.3 = ((bf16[16,16,128]{2,1,0:T(8,128)(2,1)}), bf16[16,16,128]{2,1,0:T(8,128)(2,1)S(1)}, u32[]{:S(2)}, u32[]{:S(2)}) async-start(bf16[16,16,128]{2,1,0:T(8,128)(2,1)} %reduce_sum.21), calls=%async_computation.3 | async-start | bytes 131072 | tf_op jit(solution)/shard_map/all_to_all | solution.py:296
  123.4 3.1 %collective-permute-start.13 = (bf16[2,256,128]{2,1,0:T(8,128)(2,1)S(1)}, bf16[2,256,128]{2,1,0:T(8,128)(2,1)S(1)}, u32[]{:S(2)}, u32[]{:S(2)}) collective-permute-start(bf16[2,256,128]{2,1,0:T(8,128)(2,1)S(1)} %pad_maximum_fusion), channel_id=1, source_target_pairs={{0,128},{64,192},{128,0},{192,64},{1,129},{65,193},{129,1},{193,65... | collective-permute-start | bytes 393224 | tf_op jit(solution)/shard_map/ppermute | solution.py:241
  126.5 8.4 %all-to-all-done.3 = bf16[16,16,128]{2,1,0:T(8,128)(2,1)S(1)} async-done(((bf16[16,16,128]{2,1,0:T(8,128)(2,1)}), bf16[16,16,128]{2,1,0:T(8,128)(2,1)S(1)}, u32[]{:S(2)}, u32[]{:S(2)}) %all-to-all-start.3) | async-done | bytes 65568 | tf_op jit(solution)/shard_map/all_to_all | solution.py:296
  135.6 5.6 %all-to-all-start.4 = ((f32[16,16,128]{2,1,0:T(8,128)}), f32[16,16,128]{2,1,0:T(8,128)S(1)}, u32[]{:S(2)}, u32[]{:S(2)}) async-start(f32[16,16,128]{2,1,0:T(8,128)} %broadcast_in_dim.8), calls=%async_computation.4 | async-start | bytes 262144 | tf_op jit(solution)/shard_map/all_to_all | solution.py:32
  143.0 5.9 %all-to-all-done.4 = f32[16,16,128]{2,1,0:T(8,128)S(1)} async-done(((f32[16,16,128]{2,1,0:T(8,128)}), f32[16,16,128]{2,1,0:T(8,128)S(1)}, u32[]{:S(2)}, u32[]{:S(2)}) %all-to-all-start.4) | async-done | bytes 131104 | tf_op jit(solution)/shard_map/all_to_all | solution.py:32
  (72 shorter events, 22.2 us)
Async XLA Ops:
  0.6 28.4 %collective-permute-start.1 = (bf16[256,2048]{1,0:T(8,128)(2,1)}, bf16[256,2048]{1,0:T(8,128)(2,1)S(1)}, u32[]{:S(2)}, u32[]{:S(2)}) collective-permute-start(bf16[256,2048]{1,0:T(8,128)(2,1)} %bitcast.20), channel_id=1, source_target_pairs={{0,192},{64,0},{128,64},{192,128},{1,193},{65,1},{129,65},{193,129... | collective-permute-start | bytes 3145736 | tf_op jit(solution)/shard_map/ppermute | solution.py:39
  5.9 24.4 %collective-permute-start = (bf16[256,2048]{1,0:T(8,128)(2,1)}, bf16[256,2048]{1,0:T(8,128)(2,1)S(1)}, u32[]{:S(2)}, u32[]{:S(2)}) collective-permute-start(bf16[256,2048]{1,0:T(8,128)(2,1)} %bitcast.21), channel_id=1, source_target_pairs={{0,64},{64,128},{128,192},{192,0},{1,65},{65,129},{129,193},{193,1... | collective-permute-start | bytes 3145736 | tf_op jit(solution)/shard_map/ppermute | solution.py:39
  10.3 15.1 %copy-start.18 = (bf16[256,128]{1,0:T(8,128)(2,1)S(1)}, bf16[256,128]{1,0:T(8,128)(2,1)}, u32[]{:S(2)}) copy-start(bf16[256,128]{1,0:T(8,128)(2,1)} %get-tuple-element.26) | copy-start | bytes 196612
  10.3 27.4 %all-to-all-start = ((bf16[16,16,384]{2,1,0:T(8,128)(2,1)}), bf16[16,16,384]{2,1,0:T(8,128)(2,1)S(1)}, u32[]{:S(2)}, u32[]{:S(2)}) async-start(bf16[16,16,384]{2,1,0:T(8,128)(2,1)} %get-tuple-element.25), calls=%async_computation | async-start | bytes 393216 | tf_op jit(solution)/shard_map/all_to_all | solution.py:264
  25.4 8.0 %collective-permute-start.2 = (bf16[256,128]{1,0:T(8,128)(2,1)S(1)}, bf16[256,128]{1,0:T(8,128)(2,1)S(1)}, u32[]{:S(2)}, u32[]{:S(2)}) collective-permute-start(bf16[256,128]{1,0:T(8,128)(2,1)S(1)} %copy-done.18), channel_id=1, source_target_pairs={{0,128},{64,192},{128,0},{192,64},{1,129},{65,193},{129,1},{193,65... | collective-permute-start | bytes 196616 | tf_op jit(solution)/shard_map/ppermute | solution.py:39
  29.0 51.6 %copy-start = (bf16[256,2048]{1,0:T(8,128)(2,1)}, bf16[256,2048]{1,0:T(8,128)(2,1)S(1)}, u32[]{:S(2)}) copy-start(bf16[256,2048]{1,0:T(8,128)(2,1)S(1)} %collective-permute-done.1.rest_2_.rest_11_) | copy-start | bytes 3145732
  30.2 50.4 %copy-start.1 = (bf16[256,2048]{1,0:T(8,128)(2,1)}, bf16[256,2048]{1,0:T(8,128)(2,1)S(1)}, u32[]{:S(2)}) copy-start(bf16[256,2048]{1,0:T(8,128)(2,1)S(1)} %collective-permute-done.rest_1_.rest_10_) | copy-start | bytes 3145732
  38.7 12.5 %all-to-all-start.1 = ((bf16[4,16,16,384]{3,2,1,0:T(8,128)(2,1)}), bf16[4,16,16,384]{3,2,1,0:T(8,128)(2,1)S(1)}, u32[]{:S(2)}, u32[]{:S(2)}) async-start(bf16[4,16,16,384]{3,2,1,0:T(8,128)(2,1)} %broadcast_in_dim.6), calls=%async_computation.1 | async-start | bytes 1572864 | tf_op jit(solution)/shard_map/all_to_all | solution.py:32
  42.9 18.9 %collective-permute-start.5 = (bf16[128,2048]{1,0:T(8,128)(2,1)}, bf16[128,2048]{1,0:T(8,128)(2,1)S(1)}, u32[]{:S(2)}, u32[]{:S(2)}) collective-permute-start(bf16[128,2048]{1,0:T(8,128)(2,1)} %slice.19), channel_id=1, source_target_pairs={{0,64},{64,128},{128,192},{192,0},{1,65},{65,129},{129,193},{193,1... | collective-permute-start | bytes 1572872 | tf_op jit(solution)/shard_map/ppermute | solution.py:39
  44.9 16.9 %collective-permute-start.6 = (bf16[128,2048]{1,0:T(8,128)(2,1)}, bf16[128,2048]{1,0:T(8,128)(2,1)}, u32[]{:S(2)}, u32[]{:S(2)}) collective-permute-start(bf16[128,2048]{1,0:T(8,128)(2,1)} %slice.20), channel_id=1, source_target_pairs={{0,192},{64,0},{128,64},{192,128},{1,193},{65,1},{129,65},{193,129... | collective-permute-start | bytes 1572872 | tf_op jit(solution)/shard_map/ppermute | solution.py:39
  51.3 10.5 %collective-permute-start.4 = (bf16[2,16,16,384]{3,2,1,0:T(8,128)(2,1)S(1)}, bf16[2,16,16,384]{3,2,1,0:T(8,128)(2,1)S(1)}, u32[]{:S(2)}, u32[]{:S(2)}) collective-permute-start(bf16[2,16,16,384]{3,2,1,0:T(8,128)(2,1)S(1)} %get-tuple-element.46), channel_id=1, source_target_pairs={{0,32},{32,0},{1,33},{33,1},{2,34},{34,2},{3,35},{35,3},{4,36},{36... | collective-permute-start | bytes 1179656 | tf_op jit(solution)/shard_map/ppermute | solution.py:39
  59.9 3.6 %collective-permute-start.3 = (bf16[2,16,16,384]{3,2,1,0:T(8,128)(2,1)S(1)}, bf16[2,16,16,384]{3,2,1,0:T(8,128)(2,1)S(1)}, u32[]{:S(2)}, u32[]{:S(2)}) collective-permute-start(bf16[2,16,16,384]{3,2,1,0:T(8,128)(2,1)S(1)} %get-tuple-element.47), channel_id=1, source_target_pairs={{0,32},{32,0},{1,33},{33,1},{2,34},{34,2},{3,35},{35,3},{4,36},{36... | collective-permute-start | bytes 1179656 | tf_op jit(solution)/shard_map/ppermute | solution.py:39
  61.8 18.9 %copy-start.3 = (bf16[128,2048]{1,0:T(8,128)(2,1)}, bf16[128,2048]{1,0:T(8,128)(2,1)S(1)}, u32[]{:S(2)}) copy-start(bf16[128,2048]{1,0:T(8,128)(2,1)S(1)} %collective-permute-done.5.rest_3_.rest_12_) | copy-start | bytes 1572868
  66.9 17.1 %collective-permute-start.7 = (bf16[16,64,256]{2,1,0:T(8,128)(2,1)}, bf16[16,64,256]{2,1,0:T(8,128)(2,1)}, u32[]{:S(2)}, u32[]{:S(2)}) collective-permute-start(bf16[16,64,256]{2,1,0:T(8,128)(2,1)} %bitcast.8.rest_5_), channel_id=1, source_target_pairs={{0,256},{256,0},{1,257},{257,1},{2,258},{258,2},{3,259},{259,3},{4... | collective-permute-start | bytes 1572872 | tf_op jit(solution)/shard_map/ppermute | solution.py:39
  69.6 14.3 %collective-permute-start.8 = (bf16[256,128]{1,0:T(8,128)(2,1)S(1)}, bf16[256,128]{1,0:T(8,128)(2,1)S(1)}, u32[]{:S(2)}, u32[]{:S(2)}) collective-permute-start(bf16[256,128]{1,0:T(8,128)(2,1)S(1)} %copy-done.17), channel_id=1, source_target_pairs={{0,64},{64,128},{128,192},{192,0},{1,65},{65,129},{129,193},{193,1... | collective-permute-start | bytes 196616 | tf_op jit(solution)/shard_map/ppermute | solution.py:39
  71.6 15.3 %copy-start.13 = (s32[1,64,3]{1,0,2:T(1,128)S(1)}, s32[1,64,3]{1,0,2:T(1,128)}, u32[]{:S(2)}) copy-start(s32[1,64,3]{1,0,2:T(1,128)} %param.13) | copy-start | bytes 2308
  71.6 12.4 %collective-permute-start.9 = (bf16[256,128]{1,0:T(8,128)(2,1)S(1)}, bf16[256,128]{1,0:T(8,128)(2,1)S(1)}, u32[]{:S(2)}, u32[]{:S(2)}) collective-permute-start(bf16[256,128]{1,0:T(8,128)(2,1)S(1)} %copy-done.16), channel_id=1, source_target_pairs={{0,192},{64,0},{128,64},{192,128},{1,193},{65,1},{129,65},{193,129... | collective-permute-start | bytes 196616 | tf_op jit(solution)/shard_map/ppermute | solution.py:39
  76.2 12.1 %collective-permute-start.10 = (bf16[16,64,256]{2,1,0:T(8,128)(2,1)}, bf16[16,64,256]{2,1,0:T(8,128)(2,1)}, u32[]{:S(2)}, u32[]{:S(2)}) collective-permute-start(bf16[16,64,256]{2,1,0:T(8,128)(2,1)} %bitcast.8.rest_5_), channel_id=1, source_target_pairs={{0,32},{32,0},{1,33},{33,1},{2,34},{34,2},{3,35},{35,3},{4,36},{36... | collective-permute-start | bytes 1572872 | tf_op jit(solution)/shard_map/ppermute | solution.py:39
  84.0 4.6 %collective-permute-start.11 = (bf16[16,64,256]{2,1,0:T(8,128)(2,1)}, bf16[16,64,256]{2,1,0:T(8,128)(2,1)S(1)}, u32[]{:S(2)}, u32[]{:S(2)}) collective-permute-start(bf16[16,64,256]{2,1,0:T(8,128)(2,1)} %collective-permute-done.7.rest_7_), channel_id=1, source_target_pairs={{0,32},{32,0},{1,33},{33,1},{2,34},{34,2},{3,35},{35,3},{4,36},{36... | collective-permute-start | bytes 1572872 | tf_op jit(solution)/shard_map/ppermute | solution.py:39
  98.9 13.4 %all-to-all-start.2 = ((bf16[8,16,16,128]{3,2,1,0:T(8,128)(2,1)}), bf16[8,16,16,128]{3,2,1,0:T(8,128)(2,1)S(1)}, u32[]{:S(2)}, u32[]{:S(2)}) async-start(bf16[8,16,16,128]{3,2,1,0:T(8,128)(2,1)} %get-tuple-element.40), calls=%async_computation.2 | async-start | bytes 1048576 | tf_op jit(solution)/shard_map/all_to_all | solution.py:292
  102.8 10.2 %collective-permute-start.12 = (bf16[2,256,128]{2,1,0:T(8,128)(2,1)S(1)}, bf16[2,256,128]{2,1,0:T(8,128)(2,1)S(1)}, u32[]{:S(2)}, u32[]{:S(2)}) collective-permute-start(bf16[2,256,128]{2,1,0:T(8,128)(2,1)S(1)} %copy-done.15), channel_id=1, source_target_pairs={{0,64},{64,0},{128,192},{192,128},{1,65},{65,1},{129,193},{193,129... | collective-permute-start | bytes 393224 | tf_op jit(solution)/shard_map/ppermute | solution.py:241
  113.0 21.9 %all-to-all-start.3 = ((bf16[16,16,128]{2,1,0:T(8,128)(2,1)}), bf16[16,16,128]{2,1,0:T(8,128)(2,1)S(1)}, u32[]{:S(2)}, u32[]{:S(2)}) async-start(bf16[16,16,128]{2,1,0:T(8,128)(2,1)} %reduce_sum.21), calls=%async_computation.3 | async-start | bytes 131072 | tf_op jit(solution)/shard_map/all_to_all | solution.py:296
  123.4 11.5 %collective-permute-start.13 = (bf16[2,256,128]{2,1,0:T(8,128)(2,1)S(1)}, bf16[2,256,128]{2,1,0:T(8,128)(2,1)S(1)}, u32[]{:S(2)}, u32[]{:S(2)}) collective-permute-start(bf16[2,256,128]{2,1,0:T(8,128)(2,1)S(1)} %pad_maximum_fusion), channel_id=1, source_target_pairs={{0,128},{64,192},{128,0},{192,64},{1,129},{65,193},{129,1},{193,65... | collective-permute-start | bytes 393224 | tf_op jit(solution)/shard_map/ppermute | solution.py:241
  135.6 13.3 %all-to-all-start.4 = ((f32[16,16,128]{2,1,0:T(8,128)}), f32[16,16,128]{2,1,0:T(8,128)S(1)}, u32[]{:S(2)}, u32[]{:S(2)}) async-start(f32[16,16,128]{2,1,0:T(8,128)} %broadcast_in_dim.8), calls=%async_computation.4 | async-start | bytes 262144 | tf_op jit(solution)/shard_map/all_to_all | solution.py:32
  (14 other events, 75.0 us)

commit v8 on v7

--- a/solution.py
+++ b/solution.py
@@ -183,7 +183,7 @@
             gq_ref[slot, rows, :] = dot32(ds, ks[slot], NN).astype(jnp.bfloat16)
         return carry
 
-    lax.fori_loop(0, NBL, step, 0)
+    lax.fori_loop(0, NBL, step, 0, unroll=True)
 
     acc = None
     for copy in later:

time: 151 us -> 152 us (level)
  no operation moved by 1% of the time
where the time goes in v8:
time: 152 us; the launch traced here: 151 us
  starting transfers between devices  88.5 us (58%)
  waiting for transfers between devices  32.4 us (21%)
  Pallas kernels  20.6 us (14%)
  local copies, waits for them, and re-layouts  7.3 us (5%)
    ppermute x12, starting transfers between devices, shifted(): lax.ppermute(block, axis, [(i, (i + step) % count) for i in range(count)])  44.3 us
    all_to_all x1, starting transfers between devices, per_device(): weight = lax.all_to_all(weight, 'z', 0, 0, tiled=True)  15 us
    pallas_call x1, Pallas kernels, attention(): pl.pallas_call(attention_kernel, out_shape=(jax.ShapeDtypeStruct((2, *gra...  11 us
    all_to_all x1, starting transfers between devices, per_device(): partial = lax.all_to_all(partial, 'z', 0, 0, tiled=True)  10.3 us
    all_to_all x2, starting transfers between devices, spread(): lax.all_to_all(jnp.broadcast_to(block[None], (count, *block.shape)), axes...  9.78 us
    all_to_all x1, waiting for transfers between devices, per_device(): partial = lax.all_to_all(partial, 'z', 0, 0, tiled=True)  8.43 us
    all_to_all x2, waiting for transfers between devices, spread(): lax.all_to_all(jnp.broadcast_to(block[None], (count, *block.shape)), axes...  7.71 us
    all_to_all x1, waiting for transfers between devices, per_device(): partial = lax.all_to_all(partial, ('yh', 'yl', 'core'), 0, 0, tiled=True)  7.38 us
  transfers between devices with their start and end apart: 19, of which 9 were waited for; matrix products, arithmetic and copies ran while one was open for 3% of the time, Pallas kernels for 4%

profile of v8, /device:TPU:1, one launch (start us, length us, event | category | flops | bytes accessed | tf_op | source)
XLA Modules:
  0.0 151.1 jit_solution(8417236897425465205)
XLA Ops:
  0.6 5.2 %collective-permute-start.1 = (bf16[256,2048]{1,0:T(8,128)(2,1)}, bf16[256,2048]{1,0:T(8,128)(2,1)S(1)}, u32[]{:S(2)}, u32[]{:S(2)}) collective-permute-start(bf16[256,2048]{1,0:T(8,128)(2,1)} %bitcast.20), channel_id=1, source_target_pairs={{0,192},{64,0},{128,64},{192,128},{1,193},{65,1},{129,65},{193,129... | collective-permute-start | bytes 3145736 | tf_op jit(solution)/shard_map/ppermute | solution.py:39
  10.3 15.0 %all-to-all-start = ((bf16[16,16,384]{2,1,0:T(8,128)(2,1)}), bf16[16,16,384]{2,1,0:T(8,128)(2,1)S(1)}, u32[]{:S(2)}, u32[]{:S(2)}) async-start(bf16[16,16,384]{2,1,0:T(8,128)(2,1)} %get-tuple-element.25), calls=%async_computation | async-start | bytes 393216 | tf_op jit(solution)/shard_map/all_to_all | solution.py:264
  25.4 3.6 %collective-permute-start.2 = (bf16[256,128]{1,0:T(8,128)(2,1)S(1)}, bf16[256,128]{1,0:T(8,128)(2,1)S(1)}, u32[]{:S(2)}, u32[]{:S(2)}) collective-permute-start(bf16[256,128]{1,0:T(8,128)(2,1)S(1)} %copy-done.18), channel_id=1, source_target_pairs={{0,128},{64,192},{128,0},{192,64},{1,129},{65,193},{129,1},{193,65... | collective-permute-start | bytes 196616 | tf_op jit(solution)/shard_map/ppermute | solution.py:39
  31.1 2.2 %collective-permute-done.2.rest_2_ = bf16[256,128]{1,0:T(8,128)(2,1)S(1)} collective-permute-done((bf16[256,128]{1,0:T(8,128)(2,1)S(1)}, bf16[256,128]{1,0:T(8,128)(2,1)S(1)}, u32[]{:S(2)}, u32[]{:S(2)}) %collective-permute-start.2) | collective-permute-done | bytes 65568 | tf_op jit(solution)/shard_map/ppermute | solution.py:39
  33.3 4.4 %all-to-all-done = bf16[16,16,384]{2,1,0:T(8,128)(2,1)S(1)} async-done(((bf16[16,16,384]{2,1,0:T(8,128)(2,1)}), bf16[16,16,384]{2,1,0:T(8,128)(2,1)S(1)}, u32[]{:S(2)}, u32[]{:S(2)}) %all-to-all-start) | async-done | bytes 196640 | tf_op jit(solution)/shard_map/all_to_all | solution.py:264
  38.7 4.2 %all-to-all-start.1 = ((bf16[4,16,16,384]{3,2,1,0:T(8,128)(2,1)}), bf16[4,16,16,384]{3,2,1,0:T(8,128)(2,1)S(1)}, u32[]{:S(2)}, u32[]{:S(2)}) async-start(bf16[4,16,16,384]{3,2,1,0:T(8,128)(2,1)} %broadcast_in_dim.6), calls=%async_computation.1 | async-start | bytes 1572864 | tf_op jit(solution)/shard_map/all_to_all | solution.py:32
  42.9 2.1 %collective-permute-start.5 = (bf16[128,2048]{1,0:T(8,128)(2,1)}, bf16[128,2048]{1,0:T(8,128)(2,1)S(1)}, u32[]{:S(2)}, u32[]{:S(2)}) collective-permute-start(bf16[128,2048]{1,0:T(8,128)(2,1)} %slice.19), channel_id=1, source_target_pairs={{0,64},{64,128},{128,192},{192,0},{1,65},{65,129},{129,193},{193,1... | collective-permute-start | bytes 1572872 | tf_op jit(solution)/shard_map/ppermute | solution.py:39
  44.9 4.4 %collective-permute-start.6 = (bf16[128,2048]{1,0:T(8,128)(2,1)}, bf16[128,2048]{1,0:T(8,128)(2,1)}, u32[]{:S(2)}, u32[]{:S(2)}) collective-permute-start(bf16[128,2048]{1,0:T(8,128)(2,1)} %slice.20), channel_id=1, source_target_pairs={{0,192},{64,0},{128,64},{192,128},{1,193},{65,1},{129,65},{193,129... | collective-permute-start | bytes 1572872 | tf_op jit(solution)/shard_map/ppermute | solution.py:39
  51.3 8.6 %collective-permute-start.4 = (bf16[2,16,16,384]{3,2,1,0:T(8,128)(2,1)S(1)}, bf16[2,16,16,384]{3,2,1,0:T(8,128)(2,1)S(1)}, u32[]{:S(2)}, u32[]{:S(2)}) collective-permute-start(bf16[2,16,16,384]{3,2,1,0:T(8,128)(2,1)S(1)} %get-tuple-element.46), channel_id=1, source_target_pairs={{0,32},{32,0},{1,33},{33,1},{2,34},{34,2},{3,35},{35,3},{4,36},{36... | collective-permute-start | bytes 1179656 | tf_op jit(solution)/shard_map/ppermute | solution.py:39
  63.5 3.4 %keys_values.1 = bf16[1024,256]{1,0:T(8,128)(2,1)} custom-call(s32[3]{0:T(128)S(1)} %copy-done.5, bf16[2,2,16,16,384]{4,3,2,1,0:T(8,128)(2,1)S(1)} %bitcast.18, bf16[2,16,16,384]{3,2,1,0:T(8,128)(2,1)S(1)} %collective-permute-done.3.theirs_a_ref, bf16[2,16,16,384]{3,2,1,0:T(8,128)(2,1)S(1)} %collective-permute-done.4.theirs_b_ref, ...), custom_call_target="tpu_custom_call" | custom-call | flops 1073741824 | bytes 5242880 | tf_op jit(solution)/shard_map/keys_values/pallas_call | solution.py:88
  66.9 2.7 %collective-permute-start.7 = (bf16[16,64,256]{2,1,0:T(8,128)(2,1)}, bf16[16,64,256]{2,1,0:T(8,128)(2,1)}, u32[]{:S(2)}, u32[]{:S(2)}) collective-permute-start(bf16[16,64,256]{2,1,0:T(8,128)(2,1)} %bitcast.8.rest_5_), channel_id=1, source_target_pairs={{0,256},{256,0},{1,257},{257,1},{2,258},{258,2},{3,259},{259,3},{4... | collective-permute-start | bytes 1572872 | tf_op jit(solution)/shard_map/ppermute | solution.py:39
  71.6 4.6 %collective-permute-start.9 = (bf16[256,128]{1,0:T(8,128)(2,1)S(1)}, bf16[256,128]{1,0:T(8,128)(2,1)S(1)}, u32[]{:S(2)}, u32[]{:S(2)}) collective-permute-start(bf16[256,128]{1,0:T(8,128)(2,1)S(1)} %copy-done.16), channel_id=1, source_target_pairs={{0,192},{64,0},{128,64},{192,128},{1,193},{65,1},{129,65},{193,129... | collective-permute-start | bytes 196616 | tf_op jit(solution)/shard_map/ppermute | solution.py:39
  76.2 4.5 %collective-permute-start.10 = (bf16[16,64,256]{2,1,0:T(8,128)(2,1)}, bf16[16,64,256]{2,1,0:T(8,128)(2,1)}, u32[]{:S(2)}, u32[]{:S(2)}) collective-permute-start(bf16[16,64,256]{2,1,0:T(8,128)(2,1)} %bitcast.8.rest_5_), channel_id=1, source_target_pairs={{0,32},{32,0},{1,33},{33,1},{2,34},{34,2},{3,35},{35,3},{4,36},{36... | collective-permute-start | bytes 1572872 | tf_op jit(solution)/shard_map/ppermute | solution.py:39
  80.7 2.6 %queries.1.rest_4_ = bf16[1024,128]{1,0:T(8,128)(2,1)S(1)} custom-call(s32[3]{0:T(128)S(1)} %copy-done.5, bf16[2,2,16,16,384]{4,3,2,1,0:T(8,128)(2,1)S(1)} %bitcast.19, bf16[2,16,16,384]{3,2,1,0:T(8,128)(2,1)S(1)} %collective-permute-done.3.theirs_a_ref, bf16[2,16,16,384]{3,2,1,0:T(8,128)(2,1)S(1)} %collective-permute-done.4.theirs_b_ref, ...), custom_call_target="tpu_custom_call" | custom-call | flops 536870912 | bytes 4718592 | tf_op jit(solution)/shard_map/queries/pallas_call | solution.py:88
  84.0 2.9 %collective-permute-start.11 = (bf16[16,64,256]{2,1,0:T(8,128)(2,1)}, bf16[16,64,256]{2,1,0:T(8,128)(2,1)S(1)}, u32[]{:S(2)}, u32[]{:S(2)}) collective-permute-start(bf16[16,64,256]{2,1,0:T(8,128)(2,1)} %collective-permute-done.7.rest_7_), channel_id=1, source_target_pairs={{0,32},{32,0},{1,33},{33,1},{2,34},{34,2},{3,35},{35,3},{4,36},{36... | collective-permute-start | bytes 1572872 | tf_op jit(solution)/shard_map/ppermute | solution.py:39
  89.4 11.0 %attention.1 = (bf16[2,256,128]{2,1,0:T(8,128)(2,1)}, bf16[2,256,128]{2,1,0:T(8,128)(2,1)}, bf16[8,16,16,128]{3,2,1,0:T(8,128)(2,1)}) custom-call(s32[3]{0:T(128)} %pad_add_fusion.where_ref, s32[64,3]{1,0:T(8,128)} %bitcast.29, s32[64,3]{1,0:T(8,128)} %bitcast.30, s32[1,2]{1,0:T(1,128)} %global_ref.1, bf16[256,128]{1,0:T(8,128)(2,1)} %get-tuple-element.24.rest_0_, ...), custom_call_target="tpu_custom_call" | custom-call | tf_op jit(solution)/shard_map/attention/pallas_call | solution.py:206
  100.3 3.9 %all-to-all-start.2 = ((bf16[8,16,16,128]{3,2,1,0:T(8,128)(2,1)}), bf16[8,16,16,128]{3,2,1,0:T(8,128)(2,1)S(1)}, u32[]{:S(2)}, u32[]{:S(2)}) async-start(bf16[8,16,16,128]{3,2,1,0:T(8,128)(2,1)} %get-tuple-element.40), calls=%async_computation.2 | async-start | bytes 1048576 | tf_op jit(solution)/shard_map/all_to_all | solution.py:292
  104.2 2.1 %collective-permute-start.12 = (bf16[2,256,128]{2,1,0:T(8,128)(2,1)S(1)}, bf16[2,256,128]{2,1,0:T(8,128)(2,1)S(1)}, u32[]{:S(2)}, u32[]{:S(2)}) collective-permute-start(bf16[2,256,128]{2,1,0:T(8,128)(2,1)S(1)} %copy-done.15), channel_id=1, source_target_pairs={{0,64},{64,0},{128,192},{192,128},{1,65},{65,1},{129,193},{193,129... | collective-permute-start | bytes 393224 | tf_op jit(solution)/shard_map/ppermute | solution.py:241
  106.4 7.4 %all-to-all-done.2 = bf16[8,16,16,128]{3,2,1,0:T(8,128)(2,1)S(1)} async-done(((bf16[8,16,16,128]{3,2,1,0:T(8,128)(2,1)}), bf16[8,16,16,128]{3,2,1,0:T(8,128)(2,1)S(1)}, u32[]{:S(2)}, u32[]{:S(2)}) %all-to-all-start.2) | async-done | bytes 524320 | tf_op jit(solution)/shard_map/all_to_all | solution.py:292
  114.5 10.3 %all-to-all-start.3 = ((bf16[16,16,128]{2,1,0:T(8,128)(2,1)}), bf16[16,16,128]{2,1,0:T(8,128)(2,1)S(1)}, u32[]{:S(2)}, u32[]{:S(2)}) async-start(bf16[16,16,128]{2,1,0:T(8,128)(2,1)} %reduce_sum.21), calls=%async_computation.3 | async-start | bytes 131072 | tf_op jit(solution)/shard_map/all_to_all | solution.py:296
  124.8 3.1 %collective-permute-start.13 = (bf16[2,256,128]{2,1,0:T(8,128)(2,1)S(1)}, bf16[2,256,128]{2,1,0:T(8,128)(2,1)S(1)}, u32[]{:S(2)}, u32[]{:S(2)}) collective-permute-start(bf16[2,256,128]{2,1,0:T(8,128)(2,1)S(1)} %pad_maximum_fusion), channel_id=1, source_target_pairs={{0,128},{64,192},{128,0},{192,64},{1,129},{65,193},{129,1},{193,65... | collective-permute-start | bytes 393224 | tf_op jit(solution)/shard_map/ppermute | solution.py:241
  127.9 8.4 %all-to-all-done.3 = bf16[16,16,128]{2,1,0:T(8,128)(2,1)S(1)} async-done(((bf16[16,16,128]{2,1,0:T(8,128)(2,1)}), bf16[16,16,128]{2,1,0:T(8,128)(2,1)S(1)}, u32[]{:S(2)}, u32[]{:S(2)}) %all-to-all-start.3) | async-done | bytes 65568 | tf_op jit(solution)/shard_map/all_to_all | solution.py:296
  137.1 5.6 %all-to-all-start.4 = ((f32[16,16,128]{2,1,0:T(8,128)}), f32[16,16,128]{2,1,0:T(8,128)S(1)}, u32[]{:S(2)}, u32[]{:S(2)}) async-start(f32[16,16,128]{2,1,0:T(8,128)} %broadcast_in_dim.8), calls=%async_computation.4 | async-start | bytes 262144 | tf_op jit(solution)/shard_map/all_to_all | solution.py:32
  144.5 5.9 %all-to-all-done.4 = f32[16,16,128]{2,1,0:T(8,128)S(1)} async-done(((f32[16,16,128]{2,1,0:T(8,128)}), f32[16,16,128]{2,1,0:T(8,128)S(1)}, u32[]{:S(2)}, u32[]{:S(2)}) %all-to-all-start.4) | async-done | bytes 131104 | tf_op jit(solution)/shard_map/all_to_all | solution.py:32
  (72 shorter events, 22.2 us)
Async XLA Ops:
  0.6 28.4 %collective-permute-start.1 = (bf16[256,2048]{1,0:T(8,128)(2,1)}, bf16[256,2048]{1,0:T(8,128)(2,1)S(1)}, u32[]{:S(2)}, u32[]{:S(2)}) collective-permute-start(bf16[256,2048]{1,0:T(8,128)(2,1)} %bitcast.20), channel_id=1, source_target_pairs={{0,192},{64,0},{128,64},{192,128},{1,193},{65,1},{129,65},{193,129... | collective-permute-start | bytes 3145736 | tf_op jit(solution)/shard_map/ppermute | solution.py:39
  5.9 24.4 %collective-permute-start = (bf16[256,2048]{1,0:T(8,128)(2,1)}, bf16[256,2048]{1,0:T(8,128)(2,1)S(1)}, u32[]{:S(2)}, u32[]{:S(2)}) collective-permute-start(bf16[256,2048]{1,0:T(8,128)(2,1)} %bitcast.21), channel_id=1, source_target_pairs={{0,64},{64,128},{128,192},{192,0},{1,65},{65,129},{129,193},{193,1... | collective-permute-start | bytes 3145736 | tf_op jit(solution)/shard_map/ppermute | solution.py:39
  10.3 15.1 %copy-start.18 = (bf16[256,128]{1,0:T(8,128)(2,1)S(1)}, bf16[256,128]{1,0:T(8,128)(2,1)}, u32[]{:S(2)}) copy-start(bf16[256,128]{1,0:T(8,128)(2,1)} %get-tuple-element.26) | copy-start | bytes 196612
  10.3 27.4 %all-to-all-start = ((bf16[16,16,384]{2,1,0:T(8,128)(2,1)}), bf16[16,16,384]{2,1,0:T(8,128)(2,1)S(1)}, u32[]{:S(2)}, u32[]{:S(2)}) async-start(bf16[16,16,384]{2,1,0:T(8,128)(2,1)} %get-tuple-element.25), calls=%async_computation | async-start | bytes 393216 | tf_op jit(solution)/shard_map/all_to_all | solution.py:264
  25.4 8.0 %collective-permute-start.2 = (bf16[256,128]{1,0:T(8,128)(2,1)S(1)}, bf16[256,128]{1,0:T(8,128)(2,1)S(1)}, u32[]{:S(2)}, u32[]{:S(2)}) collective-permute-start(bf16[256,128]{1,0:T(8,128)(2,1)S(1)} %copy-done.18), channel_id=1, source_target_pairs={{0,128},{64,192},{128,0},{192,64},{1,129},{65,193},{129,1},{193,65... | collective-permute-start | bytes 196616 | tf_op jit(solution)/shard_map/ppermute | solution.py:39
  29.0 51.6 %copy-start = (bf16[256,2048]{1,0:T(8,128)(2,1)}, bf16[256,2048]{1,0:T(8,128)(2,1)S(1)}, u32[]{:S(2)}) copy-start(bf16[256,2048]{1,0:T(8,128)(2,1)S(1)} %collective-permute-done.1.rest_2_.rest_11_) | copy-start | bytes 3145732
  30.2 50.4 %copy-start.1 = (bf16[256,2048]{1,0:T(8,128)(2,1)}, bf16[256,2048]{1,0:T(8,128)(2,1)S(1)}, u32[]{:S(2)}) copy-start(bf16[256,2048]{1,0:T(8,128)(2,1)S(1)} %collective-permute-done.rest_1_.rest_10_) | copy-start | bytes 3145732
  38.7 12.5 %all-to-all-start.1 = ((bf16[4,16,16,384]{3,2,1,0:T(8,128)(2,1)}), bf16[4,16,16,384]{3,2,1,0:T(8,128)(2,1)S(1)}, u32[]{:S(2)}, u32[]{:S(2)}) async-start(bf16[4,16,16,384]{3,2,1,0:T(8,128)(2,1)} %broadcast_in_dim.6), calls=%async_computation.1 | async-start | bytes 1572864 | tf_op jit(solution)/shard_map/all_to_all | solution.py:32
  42.9 18.9 %collective-permute-start.5 = (bf16[128,2048]{1,0:T(8,128)(2,1)}, bf16[128,2048]{1,0:T(8,128)(2,1)S(1)}, u32[]{:S(2)}, u32[]{:S(2)}) collective-permute-start(bf16[128,2048]{1,0:T(8,128)(2,1)} %slice.19), channel_id=1, source_target_pairs={{0,64},{64,128},{128,192},{192,0},{1,65},{65,129},{129,193},{193,1... | collective-permute-start | bytes 1572872 | tf_op jit(solution)/shard_map/ppermute | solution.py:39
  44.9 16.9 %collective-permute-start.6 = (bf16[128,2048]{1,0:T(8,128)(2,1)}, bf16[128,2048]{1,0:T(8,128)(2,1)}, u32[]{:S(2)}, u32[]{:S(2)}) collective-permute-start(bf16[128,2048]{1,0:T(8,128)(2,1)} %slice.20), channel_id=1, source_target_pairs={{0,192},{64,0},{128,64},{192,128},{1,193},{65,1},{129,65},{193,129... | collective-permute-start | bytes 1572872 | tf_op jit(solution)/shard_map/ppermute | solution.py:39
  51.3 10.5 %collective-permute-start.4 = (bf16[2,16,16,384]{3,2,1,0:T(8,128)(2,1)S(1)}, bf16[2,16,16,384]{3,2,1,0:T(8,128)(2,1)S(1)}, u32[]{:S(2)}, u32[]{:S(2)}) collective-permute-start(bf16[2,16,16,384]{3,2,1,0:T(8,128)(2,1)S(1)} %get-tuple-element.46), channel_id=1, source_target_pairs={{0,32},{32,0},{1,33},{33,1},{2,34},{34,2},{3,35},{35,3},{4,36},{36... | collective-permute-start | bytes 1179656 | tf_op jit(solution)/shard_map/ppermute | solution.py:39
  59.9 3.6 %collective-permute-start.3 = (bf16[2,16,16,384]{3,2,1,0:T(8,128)(2,1)S(1)}, bf16[2,16,16,384]{3,2,1,0:T(8,128)(2,1)S(1)}, u32[]{:S(2)}, u32[]{:S(2)}) collective-permute-start(bf16[2,16,16,384]{3,2,1,0:T(8,128)(2,1)S(1)} %get-tuple-element.47), channel_id=1, source_target_pairs={{0,32},{32,0},{1,33},{33,1},{2,34},{34,2},{3,35},{35,3},{4,36},{36... | collective-permute-start | bytes 1179656 | tf_op jit(solution)/shard_map/ppermute | solution.py:39
  61.8 18.9 %copy-start.3 = (bf16[128,2048]{1,0:T(8,128)(2,1)}, bf16[128,2048]{1,0:T(8,128)(2,1)S(1)}, u32[]{:S(2)}) copy-start(bf16[128,2048]{1,0:T(8,128)(2,1)S(1)} %collective-permute-done.5.rest_3_.rest_12_) | copy-start | bytes 1572868
  66.9 17.1 %collective-permute-start.7 = (bf16[16,64,256]{2,1,0:T(8,128)(2,1)}, bf16[16,64,256]{2,1,0:T(8,128)(2,1)}, u32[]{:S(2)}, u32[]{:S(2)}) collective-permute-start(bf16[16,64,256]{2,1,0:T(8,128)(2,1)} %bitcast.8.rest_5_), channel_id=1, source_target_pairs={{0,256},{256,0},{1,257},{257,1},{2,258},{258,2},{3,259},{259,3},{4... | collective-permute-start | bytes 1572872 | tf_op jit(solution)/shard_map/ppermute | solution.py:39
  69.6 14.3 %collective-permute-start.8 = (bf16[256,128]{1,0:T(8,128)(2,1)S(1)}, bf16[256,128]{1,0:T(8,128)(2,1)S(1)}, u32[]{:S(2)}, u32[]{:S(2)}) collective-permute-start(bf16[256,128]{1,0:T(8,128)(2,1)S(1)} %copy-done.17), channel_id=1, source_target_pairs={{0,64},{64,128},{128,192},{192,0},{1,65},{65,129},{129,193},{193,1... | collective-permute-start | bytes 196616 | tf_op jit(solution)/shard_map/ppermute | solution.py:39
  71.6 15.3 %copy-start.13 = (s32[1,64,3]{1,0,2:T(1,128)S(1)}, s32[1,64,3]{1,0,2:T(1,128)}, u32[]{:S(2)}) copy-start(s32[1,64,3]{1,0,2:T(1,128)} %param.13) | copy-start | bytes 2308
  71.6 12.4 %collective-permute-start.9 = (bf16[256,128]{1,0:T(8,128)(2,1)S(1)}, bf16[256,128]{1,0:T(8,128)(2,1)S(1)}, u32[]{:S(2)}, u32[]{:S(2)}) collective-permute-start(bf16[256,128]{1,0:T(8,128)(2,1)S(1)} %copy-done.16), channel_id=1, source_target_pairs={{0,192},{64,0},{128,64},{192,128},{1,193},{65,1},{129,65},{193,129... | collective-permute-start | bytes 196616 | tf_op jit(solution)/shard_map/ppermute | solution.py:39
  76.2 12.1 %collective-permute-start.10 = (bf16[16,64,256]{2,1,0:T(8,128)(2,1)}, bf16[16,64,256]{2,1,0:T(8,128)(2,1)}, u32[]{:S(2)}, u32[]{:S(2)}) collective-permute-start(bf16[16,64,256]{2,1,0:T(8,128)(2,1)} %bitcast.8.rest_5_), channel_id=1, source_target_pairs={{0,32},{32,0},{1,33},{33,1},{2,34},{34,2},{3,35},{35,3},{4,36},{36... | collective-permute-start | bytes 1572872 | tf_op jit(solution)/shard_map/ppermute | solution.py:39
  84.0 4.6 %collective-permute-start.11 = (bf16[16,64,256]{2,1,0:T(8,128)(2,1)}, bf16[16,64,256]{2,1,0:T(8,128)(2,1)S(1)}, u32[]{:S(2)}, u32[]{:S(2)}) collective-permute-start(bf16[16,64,256]{2,1,0:T(8,128)(2,1)} %collective-permute-done.7.rest_7_), channel_id=1, source_target_pairs={{0,32},{32,0},{1,33},{33,1},{2,34},{34,2},{3,35},{35,3},{4,36},{36... | collective-permute-start | bytes 1572872 | tf_op jit(solution)/shard_map/ppermute | solution.py:39
  100.3 13.4 %all-to-all-start.2 = ((bf16[8,16,16,128]{3,2,1,0:T(8,128)(2,1)}), bf16[8,16,16,128]{3,2,1,0:T(8,128)(2,1)S(1)}, u32[]{:S(2)}, u32[]{:S(2)}) async-start(bf16[8,16,16,128]{3,2,1,0:T(8,128)(2,1)} %get-tuple-element.40), calls=%async_computation.2 | async-start | bytes 1048576 | tf_op jit(solution)/shard_map/all_to_all | solution.py:292
  104.2 10.2 %collective-permute-start.12 = (bf16[2,256,128]{2,1,0:T(8,128)(2,1)S(1)}, bf16[2,256,128]{2,1,0:T(8,128)(2,1)S(1)}, u32[]{:S(2)}, u32[]{:S(2)}) collective-permute-start(bf16[2,256,128]{2,1,0:T(8,128)(2,1)S(1)} %copy-done.15), channel_id=1, source_target_pairs={{0,64},{64,0},{128,192},{192,128},{1,65},{65,1},{129,193},{193,129... | collective-permute-start | bytes 393224 | tf_op jit(solution)/shard_map/ppermute | solution.py:241
  114.5 21.9 %all-to-all-start.3 = ((bf16[16,16,128]{2,1,0:T(8,128)(2,1)}), bf16[16,16,128]{2,1,0:T(8,128)(2,1)S(1)}, u32[]{:S(2)}, u32[]{:S(2)}) async-start(bf16[16,16,128]{2,1,0:T(8,128)(2,1)} %reduce_sum.21), calls=%async_computation.3 | async-start | bytes 131072 | tf_op jit(solution)/shard_map/all_to_all | solution.py:296
  124.8 11.5 %collective-permute-start.13 = (bf16[2,256,128]{2,1,0:T(8,128)(2,1)S(1)}, bf16[2,256,128]{2,1,0:T(8,128)(2,1)S(1)}, u32[]{:S(2)}, u32[]{:S(2)}) collective-permute-start(bf16[2,256,128]{2,1,0:T(8,128)(2,1)S(1)} %pad_maximum_fusion), channel_id=1, source_target_pairs={{0,128},{64,192},{128,0},{192,64},{1,129},{65,193},{129,1},{193,65... | collective-permute-start | bytes 393224 | tf_op jit(solution)/shard_map/ppermute | solution.py:241
  137.1 13.3 %all-to-all-start.4 = ((f32[16,16,128]{2,1,0:T(8,128)}), f32[16,16,128]{2,1,0:T(8,128)S(1)}, u32[]{:S(2)}, u32[]{:S(2)}) async-start(f32[16,16,128]{2,1,0:T(8,128)} %broadcast_in_dim.8), calls=%async_computation.4 | async-start | bytes 262144 | tf_op jit(solution)/shard_map/all_to_all | solution.py:32
  (14 other events, 75.1 us)
